TPU v7x, 32 devices: a whole 2x2x4 slice. The times are simulated.
32 devices in a mesh: groups: 2 (over y), seq: 8 (over z, x), head: 2 (over core).
Axes of the slice: x: 2, y: 2, z: 4, core: 2. Of those that a mesh axis runs over, the one named last changes fastest.
Arguments:
- queries: bfloat16 [12288, 4096], P(('groups', 'seq'), 'head'), parts along dimension 0, may hold values from -500 to 500
- text_rows: bfloat16 [128, 2048], P(('groups', 'seq')), parts along dimension 0, may hold values from -6 to 6
- null_rows: bfloat16 [16, 2048], replicated, may hold values from -6 to 6
- kv_weight: bfloat16 [2048, 2, 4096], P('seq', None, 'head'), may hold values from -0.125 to 0.125
- prompt_lengths: int32 [16], P('groups'), parts along dimension 0, may hold values from 1 to 16, 64 in all
- block_owner: int32 [16], P(('groups', 'seq')), parts along dimension 0, may hold values from 0 to 7
- uncond_flags: int32 [16], P(('groups', 'seq')), parts along dimension 0, may hold values 0 or 1
Outputs:
- context: bfloat16 [12288, 4096], P(('groups', 'seq'), 'head'), parts along dimension 0
There are 2 independent parts, one for each index of `groups`. A program takes and returns all parts, laid end to end along the dimension named above; an argument that names none is the same for every part. Nothing has to cross between parts.
Inputs may be any that keep to these rules, and one draw needn't show every extreme that they name: `prompt_lengths`: prompt j holds the text rows after those of prompts 0 to j - 1; the lengths sum to 64.
All inputs are finite; a program needn't handle non-finite values. No bound on the sum of `uncond_flags` on one device may be relied on, other than what follows from the above.
Results may differ from a plain program's by a relative error of at most 0.012.
Values may be sent and summed in bfloat16 or wider, within the bound.
No kernel may reach another device: no remote copies, remote signals or barrier semaphores. Data moves between devices by JAX's collectives and lax.ppermute only.
A program may use at most 128 MiB of HBM per device.

v0:
```python
import jax
import jax.numpy as jnp
from jax import lax
from jax.sharding import PartitionSpec as P

HDIM = 128
NULL_LEN = 16


def per_device(queries, text_rows, null_rows, kv_weight, prompt_lengths, block_owner, uncond_flags):
    features_dev = kv_weight.shape[0]
    half_width = kv_weight.shape[2]
    text_dev = text_rows.shape[0]
    flat_weight = kv_weight.reshape(features_dev, 2 * half_width)
    text_cols = lax.all_to_all(text_rows, "seq", split_axis=1, concat_axis=0, tiled=True)
    own_rows = lax.psum_scatter(
        jnp.dot(text_cols, flat_weight, preferred_element_type=jnp.float32),
        "seq",
        scatter_dimension=0,
        tiled=True,
    )
    null_cols = lax.dynamic_slice_in_dim(
        null_rows, lax.axis_index("seq") * features_dev, features_dev, 1
    )
    null_part = jnp.dot(null_cols, flat_weight, preferred_element_type=jnp.float32)
    null_sum = lax.psum(null_part, "seq")
    own_kv = own_rows.astype(jnp.bfloat16).reshape(text_dev, 2, half_width)
    null_kv = null_sum.astype(jnp.bfloat16).reshape(NULL_LEN, 2, half_width)
    all_text = lax.all_gather(own_kv, "seq", axis=0, tiled=True)
    text_total = all_text.shape[0]
    heads_dev = half_width // HDIM
    keys_local = jnp.concatenate([all_text[:, 0], null_kv[:, 0]], axis=0).reshape(
        -1, heads_dev, HDIM
    )
    values_local = jnp.concatenate([all_text[:, 1], null_kv[:, 1]], axis=0).reshape(
        -1, heads_dev, HDIM
    )
    prompt_ends = jnp.cumsum(prompt_lengths)
    text_index = jnp.arange(text_total, dtype=jnp.int32)
    segment = jnp.sum((text_index[:, None] >= prompt_ends[None, :]).astype(jnp.int32), axis=1)
    segment_all = jnp.concatenate([segment, jnp.full((NULL_LEN,), -1, jnp.int32)])
    is_null = jnp.arange(text_total + NULL_LEN, dtype=jnp.int32) >= text_total
    allowed = jnp.where(uncond_flags[0] == 1, is_null, segment_all == block_owner[0])
    score_scale = HDIM ** (-0.5)
    row_count = queries.shape[0]
    query_blocks = queries.reshape(row_count // row_count, row_count, heads_dev, HDIM)

    def attend(query_block):
        scores = (
            jnp.einsum("qhd,khd->hqk", query_block, keys_local, preferred_element_type=jnp.float32)
            * score_scale
        )
        scores = jnp.where(allowed[None, None, :], scores, jnp.float32(-1e30))
        row_max = jnp.max(scores, axis=-1, keepdims=True)
        weights_exp = jnp.exp(scores - row_max)
        row_total = jnp.sum(weights_exp, axis=-1, keepdims=True)
        probs = (weights_exp / row_total).astype(jnp.bfloat16)
        context = jnp.einsum(
            "hqk,khd->qhd", probs, values_local, preferred_element_type=jnp.float32
        )
        return context.reshape(row_count, half_width).astype(jnp.bfloat16)

    context = lax.map(attend, query_blocks)
    return context.reshape(row_count, half_width)


def solution(mesh):
    placed = (
        P(("groups", "seq"), "head"),
        P(("groups", "seq"), None),
        P(),
        P("seq", None, "head"),
        P("groups"),
        P(("groups", "seq")),
        P(("groups", "seq")),
    )
    return jax.shard_map(
        per_device,
        mesh=mesh,
        in_specs=placed,
        out_specs=P(("groups", "seq"), "head"),
        check_vma=False,
    )
```

profile of v0, /device:TPU:0, one launch (start us, length us, event | category | flops | bytes accessed | tf_op | source)
XLA Modules:
  0.0 136.5 jit_solution(17477493198711283409)
XLA Ops:
  6.5 0.0 copy-start
  6.5 7.5 %all-to-all-start = ((bf16[8,8,256]{2,0,1:T(8,128)(2,1)}), bf16[8,8,256]{2,0,1:T(8,128)(2,1)S(1)}, u32[]{:S(2)}, u32[]{:S(2)}) async-start(bf16[8,8,256]{2,0,1:T(8,128)(2,1)} %bitcast.64), calls=%async_computation | async-start | bytes 65536 | tf_op jit(solution)/shard_map/all_to_all | solution.py:15
  14.1 0.0 reduce-scatter.2.cloned.1.call-start
  14.1 0.0 copy-start.1
  14.1 3.8 %copy.31 = bf16[32,8,2,2048]{3,1,2,0:T(8,128)(2,1)} copy(bf16[32,8,2,2048]{3,2,1,0:T(2,128)(2,1)} %bitcast.60) | data formatting | bytes 4194304
  17.9 2.8 %all-to-all-done = bf16[8,8,256]{2,0,1:T(8,128)(2,1)S(1)} async-done(((bf16[8,8,256]{2,0,1:T(8,128)(2,1)}), bf16[8,8,256]{2,0,1:T(8,128)(2,1)S(1)}, u32[]{:S(2)}, u32[]{:S(2)}) %all-to-all-start) | async-done | bytes 32800 | tf_op jit(solution)/shard_map/all_to_all | solution.py:15
  20.7 3.1 %fusion.18 = f32[64,4096]{1,0:T(8,128)} fusion(bf16[256,4096]{1,0:T(8,128)(2,1)} %bitcast.57, bf16[8,8,256]{2,0,1:T(8,128)(2,1)S(1)} %all-to-all-done), kind=kOutput, calls=%fused_computation.27 | convolution fusion | flops 134217728 | bytes 3178496 | tf_op jit(solution)/shard_map/dot_general | solution.py:17
  23.8 0.0 reduce-scatter.2.cloned.1.call-update
  25.1 0.0 copy-done.1
  25.1 0.2 reduce-window.8
  25.3 2.0 %fusion.20 = f32[16,4096]{1,0:T(8,128)S(1)} fusion(bf16[256,4096]{1,0:T(8,128)(2,1)} %bitcast.58, bf16[16,2048]{1,0:T(8,128)(2,1)} %param.9, s32[]{:T(128)S(6)} %select_n.19), kind=kOutput, calls=%fused_computation.29 | convolution fusion | flops 33554432 | bytes 2367492 | tf_op jit(solution)/shard_map/dot_general | solution.py:25
  27.3 38.3 %all-reduce.2 = bf16[16,4096]{1,0:T(8,128)(2,1)S(1)} all-reduce(f32[16,4096]{1,0:T(8,128)S(1)} %fusion.20), channel_id=1, replica_groups=mesh['groups'=2,'seq'=8,'head'=2] {'seq'}, use_global_device_ids=true, to_apply=%region_1.0 | all-reduce | flops 65536 | bytes 393216 | tf_op jit(solution)/shard_map/psum | solution.py:26
  65.6 0.1 reshape.61
  65.7 0.1 convert_reduce_fusion
  65.8 0.5 slice_reduce_fusion.1
  66.3 20.7 %reduce-scatter.2.cloned.1.call-done = f32[8,4096]{1,0:T(8,128)} async-done(((f32[64,4096]{1,0:T(8,128)}), f32[8,4096]{1,0:T(8,128)}) %reduce-scatter.2.cloned.1.call-update) | async-done | bytes 131088 | tf_op jit(solution)/shard_map/reduce_scatter | solution.py:16
  87.0 0.9 convert_element_type.24
  87.9 31.5 %all_gather.3 = bf16[64,2,2048]{2,0,1:T(8,128)(2,1)S(1)} all-gather(bf16[8,2,2048]{2,0,1:T(8,128)(2,1)S(1)} %bitcast.63), channel_id=1, replica_groups=mesh['groups'=2,'seq'=8,'head'=2] {'seq'}, dimensions={0}, use_global_device_ids=true | all-gather | bytes 589824 | tf_op jit(solution)/shard_map/all_gather | solution.py:29
  119.6 0.1 copy.19
  119.7 0.1 copy.22
  119.8 0.0 copy-done
  119.8 1.2 fusion.3
  121.0 1.4 fusion.27
  122.3 2.7 %convolution_convert_fusion = bf16[16,128,768]{2,1,0:T(8,128)(2,1)} fusion(f32[16,768,80]{1,2,0:T(8,128)S(1)} %get-tuple-element.28, f32[16,768]{1,0:T(8,128)S(1)} %get-tuple-element.26, bf16[16,16,128]{2,0,1:T(8,128)(2,1)S(1)} %copy_bitcast_fusion.1, bf16[64,16,128]{2,0,1:T(8,128)(2,1)S(1)} %copy.19), kind=kOutput, calls=%fused_computation.10 | convolution fusion | flops 255852544 | bytes 7454720 | tf_op jit(solution)/shard_map/while/body/eval_jaxpr/hqk,khd->qhd/dot_general | solution.py:58
  125.0 4.6 %copy.25 = bf16[768,2048]{1,0:T(8,128)(2,1)} copy(bf16[768,2048]{0,1:T(8,128)(2,1)} %bitcast.59) | data formatting | bytes 6291456 | tf_op jit(solution)/shard_map/while/body/eval_jaxpr/convert_element_type | solution.py:61
  (6 shorter events, 0.2 us)
Async XLA Ops:
  6.5 113.2 %copy-start = (bf16[768,2048]{1,0:T(8,128)(2,1)S(1)}, bf16[768,2048]{1,0:T(8,128)(2,1)}, u32[]{:S(2)}) copy-start(bf16[768,2048]{1,0:T(8,128)(2,1)} %param.7) | copy-start | bytes 9437188
  6.5 14.2 %all-to-all-start = ((bf16[8,8,256]{2,0,1:T(8,128)(2,1)}), bf16[8,8,256]{2,0,1:T(8,128)(2,1)S(1)}, u32[]{:S(2)}, u32[]{:S(2)}) async-start(bf16[8,8,256]{2,0,1:T(8,128)(2,1)} %bitcast.64), calls=%async_computation | async-start | bytes 65536 | tf_op jit(solution)/shard_map/all_to_all | solution.py:15
  14.1 73.0 %reduce-scatter.2.cloned.1.call-start = ((), (), s32[]{:S(2)}) async-start(), calls=%async_computation.2 | async-start | bytes 1179648 | tf_op jit(solution)/shard_map/reduce_scatter | solution.py:16
  14.1 11.0 %copy-start.1 = (s32[8]{0:T(128)S(1)}, s32[8]{0:T(128)}, u32[]{:S(2)}) copy-start(s32[8]{0:T(128)} %param.11) | copy-start | bytes 100
Sparse Core Ops, SparseCore 0:
  23.9 63.0 reduce-scatter.1
where the time goes:
time: 137 us
  blocking collectives  69.8 us (51%)
  waiting for transfers between devices  23.5 us (17%)
  between operations  14.8 us (11%)
  local copies, waits for them, and re-layouts  9.34 us (7%)
  matrix products  8.96 us (7%)
  starting transfers between devices  7.55 us (6%)
  other arithmetic  2.54 us (2%)
    psum x1, blocking collectives, per_device(): null_sum = lax.psum(null_part, 'seq')  38.3 us
    all_gather x1, blocking collectives, per_device(): all_text = lax.all_gather(own_kv, 'seq', axis=0, tiled=True)  31.5 us
    reduce_scatter x1, waiting for transfers between devices, per_device(): lax.psum_scatter(jnp.dot(text_cols, flat_weight, preferred_element_type=j...  20.7 us
    all_to_all x1, starting transfers between devices, per_device(): lax.all_to_all(text_rows, 'seq', split_axis=1, concat_axis=0, tiled=True)  7.52 us
    convert_element_type x1, local copies, waits for them, and re-layouts, attend(): return context.reshape(row_count, half_width).astype(jnp.bfloat16)  4.63 us
    unnamed x8, local copies, waits for them, and re-layouts  3.93 us
    dot_general x1, matrix products, per_device(): jnp.dot(text_cols, flat_weight, preferred_element_type=jnp.float32)  3.06 us
    all_to_all x1, waiting for transfers between devices, per_device(): lax.all_to_all(text_rows, 'seq', split_axis=1, concat_axis=0, tiled=True)  2.82 us
  transfers between devices with their start and end apart: 2, of which 2 were waited for; matrix products, arithmetic and copies ran while one was open for 5% of the time, Pallas kernels for 0%

commit v1 on v0

--- a/solution.py
+++ b/solution.py
@@ -1,13 +1,20 @@
+import functools
+
 import jax
 import jax.numpy as jnp
 from jax import lax
+from jax.experimental import pallas as pl
+from jax.experimental.pallas import tpu as pltpu
 from jax.sharding import PartitionSpec as P
 
 HDIM = 128
 NULL_LEN = 16
-
-
-def per_device(queries, text_rows, null_rows, kv_weight, prompt_lengths, block_owner, uncond_flags):
+SCALE = HDIM ** (-0.5)
+VMEM_LIMIT = 48 * 1024 * 1024
+NEG = -1e30
+
+
+def gather_plan(queries, text_rows, null_rows, kv_weight, prompt_lengths, block_owner, uncond_flags):
     features_dev = kv_weight.shape[0]
     half_width = kv_weight.shape[2]
     text_dev = text_rows.shape[0]
@@ -41,30 +48,211 @@
     segment_all = jnp.concatenate([segment, jnp.full((NULL_LEN,), -1, jnp.int32)])
     is_null = jnp.arange(text_total + NULL_LEN, dtype=jnp.int32) >= text_total
     allowed = jnp.where(uncond_flags[0] == 1, is_null, segment_all == block_owner[0])
-    score_scale = HDIM ** (-0.5)
     row_count = queries.shape[0]
-    query_blocks = queries.reshape(row_count // row_count, row_count, heads_dev, HDIM)
-
-    def attend(query_block):
-        scores = (
-            jnp.einsum("qhd,khd->hqk", query_block, keys_local, preferred_element_type=jnp.float32)
-            * score_scale
+    query_heads = queries.reshape(row_count, heads_dev, HDIM)
+    scores = (
+        jnp.einsum("qhd,khd->hqk", query_heads, keys_local, preferred_element_type=jnp.float32)
+        * SCALE
+    )
+    scores = jnp.where(allowed[None, None, :], scores, jnp.float32(NEG))
+    row_max = jnp.max(scores, axis=-1, keepdims=True)
+    weights_exp = jnp.exp(scores - row_max)
+    row_total = jnp.sum(weights_exp, axis=-1, keepdims=True)
+    probs = (weights_exp / row_total).astype(jnp.bfloat16)
+    context = jnp.einsum("hqk,khd->qhd", probs, values_local, preferred_element_type=jnp.float32)
+    return context.reshape(row_count, half_width).astype(jnp.bfloat16)
+
+
+def swap(x, n, mask):
+    return lax.ppermute(x, "seq", [(i, i ^ mask) for i in range(n)])
+
+
+def project_kernel(order, pos_ref, len_ref, null_ref, w_ref, pack_ref, send_k, keep_k, send_v, keep_v):
+    n = len(order)
+    pos = pos_ref[0]
+    text_dev = pack_ref.shape[1] // 2
+    rows = n * NULL_LEN
+    packs = [pack_ref[jnp.bitwise_xor(pos, m)] for m in order]
+    pack = jnp.concatenate(packs, axis=0)
+    code = jnp.concatenate(
+        [p.astype(jnp.float32)[text_dev:, :128] for p in packs for _ in range(2)], axis=0
+    ).astype(jnp.int32)
+    reqs = len_ref.shape[0]
+    uncond = code >= reqs
+    owner = jnp.where(uncond, code - reqs, code)
+    start = jnp.zeros_like(owner)
+    running = jnp.int32(0)
+    for r in range(reqs):
+        start = jnp.where(owner == r, running, start)
+        running = running + len_ref[r]
+    wanted = start + lax.broadcasted_iota(jnp.int32, (rows, 128), 0) % NULL_LEN
+    col = lax.broadcasted_iota(jnp.int32, (rows, 128), 1)
+    held = jnp.full((rows, 128), -1, jnp.int32)
+    for slot, m in enumerate(order):
+        first = slot * 2 * text_dev
+        base = jnp.bitwise_xor(pos, m) * text_dev - first
+        held = jnp.where((col >= first) & (col < first + text_dev), col + base, held)
+    pick = (held == wanted).astype(jnp.float32).astype(jnp.bfloat16)
+    text_sel = jnp.dot(pick, pack, preferred_element_type=jnp.float32)
+    null_sel = jnp.concatenate([null_ref[...].astype(jnp.float32)] * n, axis=0)
+    wide = jnp.concatenate([uncond] * (null_sel.shape[1] // 128), axis=1)
+    sel = jnp.where(wide, null_sel, text_sel).astype(jnp.bfloat16)
+    half = rows // 2
+    width = send_k.shape[1]
+    for kind, (send, keep) in enumerate(((send_k, keep_k), (send_v, keep_v))):
+        for c in range(0, width, 512):
+            part = jnp.dot(
+                sel,
+                w_ref[:, kind * width + c : kind * width + c + 512],
+                preferred_element_type=jnp.float32,
+            )
+            send[:, c : c + 512] = part[:half].astype(jnp.bfloat16)
+            keep[:, c : c + 512] = part[half:]
+
+
+def spread_heads(kept_ref, got_ref, wide_ref):
+    total = kept_ref[...] + got_ref[...].astype(jnp.float32)
+    keys, width = total.shape
+    heads = width // HDIM
+    total = total.astype(jnp.bfloat16).astype(jnp.float32)
+    head = lax.broadcasted_iota(jnp.int32, (heads, width), 0)
+    col = lax.broadcasted_iota(jnp.int32, (heads, width), 1)
+    mine = (col // HDIM) == head
+    for key in range(keys):
+        block = jnp.where(mine, jnp.broadcast_to(total[key : key + 1], (heads, width)), 0.0)
+        wide_ref[key * heads : (key + 1) * heads] = block.astype(jnp.bfloat16)
+
+
+def probs_kernel(len_ref, own_ref, flag_ref, q_ref, kept_ref, got_ref, out_ref, wide_ref):
+    heads = q_ref.shape[1] // HDIM
+    spread_heads(kept_ref, got_ref, wide_ref)
+    count = jnp.int32(0)
+    for r in range(len_ref.shape[0]):
+        count = jnp.where(own_ref[0] == r, len_ref[r], count)
+    count = jnp.where(flag_ref[0] == 1, NULL_LEN, count)
+    block = 256
+    for first in range(0, q_ref.shape[0], block):
+        scores = lax.dot_general(
+            q_ref[first : first + block],
+            wide_ref[...],
+            (((1,), (1,)), ((), ())),
+            preferred_element_type=jnp.float32,
         )
-        scores = jnp.where(allowed[None, None, :], scores, jnp.float32(-1e30))
-        row_max = jnp.max(scores, axis=-1, keepdims=True)
-        weights_exp = jnp.exp(scores - row_max)
-        row_total = jnp.sum(weights_exp, axis=-1, keepdims=True)
-        probs = (weights_exp / row_total).astype(jnp.bfloat16)
-        context = jnp.einsum(
-            "hqk,khd->qhd", probs, values_local, preferred_element_type=jnp.float32
-        )
-        return context.reshape(row_count, half_width).astype(jnp.bfloat16)
-
-    context = lax.map(attend, query_blocks)
-    return context.reshape(row_count, half_width)
+        scores = scores * SCALE
+        key = lax.broadcasted_iota(jnp.int32, scores.shape, 1) // heads
+        scores = jnp.where(key < count, scores, NEG)
+        parts = [scores[:, c : c + 128] for c in range(0, scores.shape[1], 128)]
+        top = functools.reduce(jnp.maximum, parts)
+        step = heads
+        while step < 128:
+            top = jnp.maximum(top, pltpu.roll(top, step, 1))
+            step *= 2
+        parts = [jnp.exp(p - top) for p in parts]
+        total = functools.reduce(jnp.add, parts)
+        step = heads
+        while step < 128:
+            total = total + pltpu.roll(total, step, 1)
+            step *= 2
+        out_ref[first : first + block] = jnp.concatenate(
+            [p / total for p in parts], axis=1
+        ).astype(jnp.bfloat16)
+
+
+def context_kernel(p_ref, kept_ref, got_ref, out_ref, wide_ref):
+    @pl.when(pl.program_id(0) == 0)
+    def _():
+        spread_heads(kept_ref, got_ref, wide_ref)
+
+    block = out_ref.shape[0]
+    first = pl.multiple_of(pl.program_id(0) * block, block)
+    out_ref[...] = jnp.dot(
+        p_ref[pl.ds(first, block)], wide_ref[...], preferred_element_type=jnp.float32
+    ).astype(jnp.bfloat16)
+
+
+def select_plan(n, queries, text_rows, null_rows, kv_weight, prompt_lengths, block_owner, uncond_flags):
+    features = kv_weight.shape[0]
+    width = kv_weight.shape[2]
+    rows = queries.shape[0]
+    reqs = prompt_lengths.shape[0]
+    heads = width // HDIM
+    pos = lax.axis_index("seq").astype(jnp.int32)
+    code = (block_owner[0] + reqs * uncond_flags[0]).astype(jnp.bfloat16)
+    packed = jnp.concatenate([text_rows, jnp.full(text_rows.shape, code, jnp.bfloat16)], axis=0)
+    packed = packed.reshape(-1, n, features).transpose(1, 0, 2)
+    packs = lax.all_to_all(packed, "seq", split_axis=0, concat_axis=0, tiled=True)
+    null_cols = lax.dynamic_slice_in_dim(null_rows, pos * features, features, 1)
+    flat_weight = kv_weight.reshape(features, 2 * width)
+    order = [7, 3, 5, 1, 6, 2, 4, 0]
+    half = n * NULL_LEN // 2
+    sent = jax.ShapeDtypeStruct((half, width), jnp.bfloat16)
+    kept = jax.ShapeDtypeStruct((half, width), jnp.float32)
+    smem = pl.BlockSpec(memory_space=pltpu.SMEM)
+    vmem = pl.BlockSpec(memory_space=pltpu.VMEM)
+    params = pltpu.CompilerParams(vmem_limit_bytes=VMEM_LIMIT)
+    send_k, keep_k, send_v, keep_v = pl.pallas_call(
+        functools.partial(project_kernel, order),
+        out_shape=[sent, kept] * 2,
+        in_specs=[smem, smem, vmem, vmem, vmem],
+        out_specs=[vmem] * 4,
+        compiler_params=params,
+        cost_estimate=pl.CostEstimate(
+            flops=2 * 2 * half * features * 2 * width,
+            bytes_accessed=8 * features * width,
+            transcendentals=0,
+        ),
+        name="project",
+    )(pos.reshape(1), prompt_lengths, null_cols, flat_weight, packs)
+
+    def reduce_parts(send, keep):
+        for mask in (1, 2):
+            total = keep + swap(send, n, mask).astype(jnp.float32)
+            cut = total.shape[0] // 2
+            send, keep = total[:cut].astype(jnp.bfloat16), total[cut:]
+        return keep, swap(send, n, 4)
+
+    k_parts = reduce_parts(send_k, keep_k)
+    v_parts = reduce_parts(send_v, keep_v)
+
+    lanes = heads * NULL_LEN
+    probs = pl.pallas_call(
+        probs_kernel,
+        out_shape=jax.ShapeDtypeStruct((rows, lanes), jnp.bfloat16),
+        in_specs=[smem] * 3 + [vmem] * 3,
+        out_specs=vmem,
+        scratch_shapes=[pltpu.VMEM((lanes, width), jnp.bfloat16)],
+        compiler_params=params,
+        cost_estimate=pl.CostEstimate(
+            flops=2 * rows * width * lanes, bytes_accessed=2 * rows * width, transcendentals=rows * lanes
+        ),
+        name="probs",
+    )(prompt_lengths, block_owner, uncond_flags, queries, *k_parts)
+    block = 256
+    return pl.pallas_call(
+        context_kernel,
+        out_shape=jax.ShapeDtypeStruct((rows, width), jnp.bfloat16),
+        grid=(rows // block,),
+        in_specs=[vmem] * 3,
+        out_specs=pl.BlockSpec((block, width), lambda i: (i, 0)),
+        scratch_shapes=[pltpu.VMEM((lanes, width), jnp.bfloat16)],
+        compiler_params=params,
+        cost_estimate=pl.CostEstimate(
+            flops=2 * rows * width * lanes, bytes_accessed=2 * rows * width, transcendentals=0
+        ),
+        name="context",
+    )(probs, *v_parts)
 
 
 def solution(mesh):
+    n = mesh.shape["seq"]
+
+    def per_device(queries, text_rows, null_rows, kv_weight, *rest):
+        longest = n * text_rows.shape[0] // 4
+        few = n == 8 and longest == NULL_LEN and text_rows.shape[0] == 8
+        if few:
+            return select_plan(n, queries, text_rows, null_rows, kv_weight, *rest)
+        return gather_plan(queries, text_rows, null_rows, kv_weight, *rest)
+
     placed = (
         P(("groups", "seq"), "head"),
         P(("groups", "seq"), None),

time: 137 us -> 44.9 us (0.33)
  blocking collectives: 69.8 us -> 0 us
  between operations: 14.8 us -> 1.45 us
  matrix products: 8.96 us -> 0 us
  Pallas kernels: 0 us -> 6.11 us
  local copies, waits for them, and re-layouts: 9.34 us -> 3.98 us
  starting transfers between devices: 7.55 us -> 11.9 us
  waiting for transfers between devices: 23.5 us -> 20.9 us
  other arithmetic: 2.54 us -> 0.17 us
    psum x1 -> x0, blocking collectives: 38.3 us -> none  [per_device(): null_sum = lax.psum(null_part, 'seq')]
    all_gather x1 -> x0, blocking collectives: 31.5 us -> none  [per_device(): all_text = lax.all_gather(own_kv, 'seq', axis=0, tiled=True)]
    reduce_scatter x1 -> x0, waiting for transfers between devices: 20.7 us -> none  [per_device(): lax.psum_scatter(jnp.dot(text_cols, flat_weight, preferred_element_type=j...]
    ppermute x0 -> x6, waiting for transfers between devices: none -> 16.5 us  [swap(): return lax.ppermute(x, 'seq', [(i, i ^ mask) for i in range(n)])]
    dot_general x4 -> x0, matrix products: 8.96 us -> none  [the longest x1 3.06 us: per_device(): jnp.dot(text_cols, flat_weight, preferred_element_type=jnp.float32)]
    pallas_call x0 -> x3, Pallas kernels: none -> 6.11 us  [the longest x1 2.99 us: select_plan(): pl.pallas_call(context_kernel, out_shape=jax.ShapeDtypeStruct((rows, widt...]
    ppermute x0 -> x6, starting transfers between devices: none -> 4.63 us  [swap(): return lax.ppermute(x, 'seq', [(i, i ^ mask) for i in range(n)])]
    convert_element_type x1 -> x0, local copies, waits for them, and re-layouts: 4.63 us -> none  [attend(): return context.reshape(row_count, half_width).astype(jnp.bfloat16)]
  transfers between devices with their start and end apart: 2 -> 7, of which waited for: 2 -> 6; matrix products, arithmetic and copies ran while one was open for 5% -> 6% of each run, Pallas kernels for 0% -> 5%
where the time goes in v1:
time: 44.9 us; the launch traced here: 44.5 us
  waiting for transfers between devices  20.9 us (47%)
  starting transfers between devices  11.9 us (27%)
  Pallas kernels  6.11 us (14%)
  local copies, waits for them, and re-layouts  3.98 us (9%)
  between operations  1.45 us (3%)
    ppermute x6, waiting for transfers between devices, swap(): return lax.ppermute(x, 'seq', [(i, i ^ mask) for i in range(n)])  16.5 us
    all_to_all x1, starting transfers between devices, select_plan(): lax.all_to_all(packed, 'seq', split_axis=0, concat_axis=0, tiled=True)  7.25 us
    ppermute x6, starting transfers between devices, swap(): return lax.ppermute(x, 'seq', [(i, i ^ mask) for i in range(n)])  4.63 us
    all_to_all x1, waiting for transfers between devices, select_plan(): lax.all_to_all(packed, 'seq', split_axis=0, concat_axis=0, tiled=True)  4.39 us
    pallas_call x1, Pallas kernels, select_plan(): pl.pallas_call(context_kernel, out_shape=jax.ShapeDtypeStruct((rows, widt...  2.99 us
    unnamed x7, local copies, waits for them, and re-layouts  2.5 us
    pallas_call x1, Pallas kernels, select_plan(): pl.pallas_call(probs_kernel, out_shape=jax.ShapeDtypeStruct((rows, lanes)...  2.02 us
    pallas_call x1, Pallas kernels, select_plan(): pl.pallas_call(functools.partial(project_kernel, order), out_shape=[sent,...  1.1 us
  transfers between devices with their start and end apart: 7, of which 6 were waited for; matrix products, arithmetic and copies ran while one was open for 6% of the time, Pallas kernels for 5%

profile of v1, /device:TPU:0, one launch (start us, length us, event | category | flops | bytes accessed | tf_op | source)
XLA Modules:
  0.0 44.5 jit_solution(15117650580536337107)
XLA Ops:
  0.0 0.0 copy-start
  0.0 0.0 copy-start.2
  1.3 0.8 %concatenate.3 = bf16[16,2048]{1,0:T(8,128)(2,1)S(1)} pad(bf16[8,2048]{1,0:T(8,128)(2,1)} %param.8, bf16[]{:T(256)} %bitcast.1), padding=0_8x0_0 | pad | bytes 98306 | tf_op jit(solution)/shard_map/concatenate | solution.py:181
  2.1 0.6 %copy.12 = bf16[2,8,8,256]{3,2,0,1:T(8,128)(2,1)} copy(bf16[2,8,8,256]{3,2,1,0:T(8,128)(2,1)S(1)} %bitcast.13) | data formatting | bytes 131072 | tf_op jit(solution)/shard_map/reshape | solution.py:182
  2.7 7.3 %all-to-all-start = ((bf16[8,16,256]{2,1,0:T(8,128)(2,1)}), bf16[8,16,256]{2,1,0:T(8,128)(2,1)S(1)}, u32[]{:S(2)}, u32[]{:S(2)}) async-start(bf16[8,16,256]{2,1,0:T(8,128)(2,1)} %bitcast.10), calls=%async_computation | async-start | bytes 131072 | tf_op jit(solution)/shard_map/all_to_all | solution.py:183
  10.0 2.5 %copy.10 = bf16[32,8,2,2048]{3,1,2,0:T(8,128)(2,1)S(1)} copy(bf16[32,8,2,2048]{3,2,1,0:T(2,128)(2,1)} %bitcast.12) | data formatting | bytes 4194304
  12.5 0.0 copy-done
  12.5 4.4 %all-to-all-done.pack_ref = bf16[8,16,256]{2,1,0:T(8,128)(2,1)S(1)} async-done(((bf16[8,16,256]{2,1,0:T(8,128)(2,1)}), bf16[8,16,256]{2,1,0:T(8,128)(2,1)S(1)}, u32[]{:S(2)}, u32[]{:S(2)}) %all-to-all-start) | async-done | bytes 65568 | tf_op jit(solution)/shard_map/all_to_all | solution.py:183
  16.9 0.0 copy-done.2
  16.9 1.1 %project.1 = (bf16[64,2048]{1,0:T(8,128)(2,1)S(1)}, f32[64,2048]{1,0:T(8,128)S(1)}, bf16[64,2048]{1,0:T(8,128)(2,1)S(1)}, f32[64,2048]{1,0:T(8,128)S(1)}) custom-call(s32[1]{0:T(128)} %bitcast.pos_ref, s32[8]{0:T(128)S(1)} %copy-done.2, bf16[16,256]{1,0:T(8,128)(2,1)S(1)} %constant_dynamic-slice_fusion.null_ref, bf16[256,4096]{1,0:T(8,128)(2,1)S(1)} %bitcast.11, ...), custom_call_target="tpu_custom_call" | custom-call | flops 268435456 | bytes 4194304 | tf_op jit(solution)/shard_map/project/pallas_call | solution.py:193
  18.0 0.0 copy-start.1
  18.0 0.5 %collective-permute-start = (bf16[64,2048]{1,0:T(8,128)(2,1)S(1)}, bf16[64,2048]{1,0:T(8,128)(2,1)S(1)}, u32[]{:S(2)}, u32[]{:S(2)}) collective-permute-start(bf16[64,2048]{1,0:T(8,128)(2,1)S(1)} %get-tuple-element.10), channel_id=1, source_target_pairs={{0,2},{2,0},{4,6},{6,4},{8,10},{10,8},{12,14},{14,12},{1,3},{3,1},... | collective-permute-start | bytes 786440 | tf_op jit(solution)/shard_map/ppermute | solution.py:67
  18.5 1.6 %collective-permute-start.3 = (bf16[64,2048]{1,0:T(8,128)(2,1)S(1)}, bf16[64,2048]{1,0:T(8,128)(2,1)S(1)}, u32[]{:S(2)}, u32[]{:S(2)}) collective-permute-start(bf16[64,2048]{1,0:T(8,128)(2,1)S(1)} %get-tuple-element.12), channel_id=1, source_target_pairs={{0,2},{2,0},{4,6},{6,4},{8,10},{10,8},{12,14},{14,12},{1,3},{3,1},... | collective-permute-start | bytes 786440 | tf_op jit(solution)/shard_map/ppermute | solution.py:67
  20.1 7.2 %collective-permute-done = bf16[64,2048]{1,0:T(8,128)(2,1)S(1)} collective-permute-done((bf16[64,2048]{1,0:T(8,128)(2,1)S(1)}, bf16[64,2048]{1,0:T(8,128)(2,1)S(1)}, u32[]{:S(2)}, u32[]{:S(2)}) %collective-permute-start) | collective-permute-done | bytes 262176 | tf_op jit(solution)/shard_map/ppermute | solution.py:67
  27.3 0.1 convert_add_fusion.1
  27.4 0.3 collective-permute-start.1
  27.7 2.6 %collective-permute-done.3 = bf16[64,2048]{1,0:T(8,128)(2,1)S(1)} collective-permute-done((bf16[64,2048]{1,0:T(8,128)(2,1)S(1)}, bf16[64,2048]{1,0:T(8,128)(2,1)S(1)}, u32[]{:S(2)}, u32[]{:S(2)}) %collective-permute-start.3) | collective-permute-done | bytes 262176 | tf_op jit(solution)/shard_map/ppermute | solution.py:67
  30.3 0.1 convert_add_fusion
  30.4 0.3 collective-permute-start.4
  30.7 3.3 %collective-permute-done.1 = bf16[32,2048]{1,0:T(8,128)(2,1)S(1)} collective-permute-done((bf16[32,2048]{1,0:T(8,128)(2,1)S(1)}, bf16[32,2048]{1,0:T(8,128)(2,1)S(1)}, u32[]{:S(2)}, u32[]{:S(2)}) %collective-permute-start.1) | collective-permute-done | bytes 131104 | tf_op jit(solution)/shard_map/ppermute | solution.py:67
  34.1 0.2 collective-permute-start.2
  34.3 1.1 %collective-permute-done.4 = bf16[32,2048]{1,0:T(8,128)(2,1)S(1)} collective-permute-done((bf16[32,2048]{1,0:T(8,128)(2,1)S(1)}, bf16[32,2048]{1,0:T(8,128)(2,1)S(1)}, u32[]{:S(2)}, u32[]{:S(2)}) %collective-permute-start.4) | collective-permute-done | bytes 131104 | tf_op jit(solution)/shard_map/ppermute | solution.py:67
  35.5 1.7 %collective-permute-start.5 = (bf16[16,2048]{1,0:T(8,128)(2,1)S(1)}, bf16[16,2048]{1,0:T(8,128)(2,1)S(1)}, u32[]{:S(2)}, u32[]{:S(2)}) collective-permute-start(bf16[16,2048]{1,0:T(8,128)(2,1)S(1)} %slice.52), channel_id=1, source_target_pairs={{0,8},{2,10},{4,12},{6,14},{8,0},{10,2},{12,4},{14,6},{1,9},{3,11}... | collective-permute-start | bytes 196616 | tf_op jit(solution)/shard_map/ppermute | solution.py:67
  37.2 2.2 %collective-permute-done.2.got_ref = bf16[16,2048]{1,0:T(8,128)(2,1)S(1)} collective-permute-done((bf16[16,2048]{1,0:T(8,128)(2,1)S(1)}, bf16[16,2048]{1,0:T(8,128)(2,1)S(1)}, u32[]{:S(2)}, u32[]{:S(2)}) %collective-permute-start.2) | collective-permute-done | bytes 65568 | tf_op jit(solution)/shard_map/ppermute | solution.py:67
  39.5 0.0 copy-done.1
  39.5 2.0 %probs.1.p_ref = bf16[768,256]{1,0:T(8,128)(2,1)S(1)} custom-call(s32[8]{0:T(128)S(1)} %copy-done.2, s32[1]{0:T(128)S(6)} %copy.13.own_ref, s32[1]{0:T(128)S(6)} %copy.14.flag_ref, bf16[768,2048]{1,0:T(8,128)(2,1)S(1)} %copy-done.1, f32[16,2048]{1,0:T(8,128)S(1)} %slice.38.kept_ref, bf16[16,2048]{1,0:T(8,128)(2,1)S(1)} %collective-permute-done.2.got_ref), custom_call_target="tpu_custom_call" | custom-call | flops 805306368 | bytes 3145728 | tf_op jit(solution)/shard_map/probs/pallas_call | solution.py:218
  41.5 0.0 collective-permute-done.5.got_ref
  41.5 3.0 %context.1 = bf16[768,2048]{1,0:T(8,128)(2,1)} custom-call(bf16[768,256]{1,0:T(8,128)(2,1)S(1)} %probs.1.p_ref, f32[16,2048]{1,0:T(8,128)S(1)} %slice.42.kept_ref, bf16[16,2048]{1,0:T(8,128)(2,1)S(1)} %collective-permute-done.5.got_ref), custom_call_target="tpu_custom_call" | custom-call | flops 805306368 | bytes 3145728 | tf_op jit(solution)/shard_map/context/pallas_call | solution.py:231
  (9 shorter events, 0.1 us)
Async XLA Ops:
  0.0 12.5 %copy-start = (bf16[16,2048]{1,0:T(8,128)(2,1)S(1)}, bf16[16,2048]{1,0:T(8,128)(2,1)}, u32[]{:S(2)}) copy-start(bf16[16,2048]{1,0:T(8,128)(2,1)} %param.9) | copy-start | bytes 196612
  0.0 16.9 %copy-start.2 = (s32[8]{0:T(128)S(1)}, s32[8]{0:T(128)}, u32[]{:S(2)}) copy-start(s32[8]{0:T(128)} %len_ref.3) | copy-start | bytes 100
  2.7 14.2 %all-to-all-start = ((bf16[8,16,256]{2,1,0:T(8,128)(2,1)}), bf16[8,16,256]{2,1,0:T(8,128)(2,1)S(1)}, u32[]{:S(2)}, u32[]{:S(2)}) async-start(bf16[8,16,256]{2,1,0:T(8,128)(2,1)} %bitcast.10), calls=%async_computation | async-start | bytes 131072 | tf_op jit(solution)/shard_map/all_to_all | solution.py:183
  18.0 21.5 %copy-start.1 = (bf16[768,2048]{1,0:T(8,128)(2,1)S(1)}, bf16[768,2048]{1,0:T(8,128)(2,1)}, u32[]{:S(2)}) copy-start(bf16[768,2048]{1,0:T(8,128)(2,1)} %q_ref.1) | copy-start | bytes 9437188
  18.0 9.3 %collective-permute-start = (bf16[64,2048]{1,0:T(8,128)(2,1)S(1)}, bf16[64,2048]{1,0:T(8,128)(2,1)S(1)}, u32[]{:S(2)}, u32[]{:S(2)}) collective-permute-start(bf16[64,2048]{1,0:T(8,128)(2,1)S(1)} %get-tuple-element.10), channel_id=1, source_target_pairs={{0,2},{2,0},{4,6},{6,4},{8,10},{10,8},{12,14},{14,12},{1,3},{3,1},... | collective-permute-start | bytes 786440 | tf_op jit(solution)/shard_map/ppermute | solution.py:67
  18.5 11.8 %collective-permute-start.3 = (bf16[64,2048]{1,0:T(8,128)(2,1)S(1)}, bf16[64,2048]{1,0:T(8,128)(2,1)S(1)}, u32[]{:S(2)}, u32[]{:S(2)}) collective-permute-start(bf16[64,2048]{1,0:T(8,128)(2,1)S(1)} %get-tuple-element.12), channel_id=1, source_target_pairs={{0,2},{2,0},{4,6},{6,4},{8,10},{10,8},{12,14},{14,12},{1,3},{3,1},... | collective-permute-start | bytes 786440 | tf_op jit(solution)/shard_map/ppermute | solution.py:67
  27.4 6.6 %collective-permute-start.1 = (bf16[32,2048]{1,0:T(8,128)(2,1)S(1)}, bf16[32,2048]{1,0:T(8,128)(2,1)S(1)}, u32[]{:S(2)}, u32[]{:S(2)}) collective-permute-start(bf16[32,2048]{1,0:T(8,128)(2,1)S(1)} %slice.51), channel_id=1, source_target_pairs={{0,4},{2,6},{4,0},{6,2},{8,12},{10,14},{12,8},{14,10},{1,5},{3,7},... | collective-permute-start | bytes 393224 | tf_op jit(solution)/shard_map/ppermute | solution.py:67
  30.4 5.1 %collective-permute-start.4 = (bf16[32,2048]{1,0:T(8,128)(2,1)S(1)}, bf16[32,2048]{1,0:T(8,128)(2,1)S(1)}, u32[]{:S(2)}, u32[]{:S(2)}) collective-permute-start(bf16[32,2048]{1,0:T(8,128)(2,1)S(1)} %slice.50), channel_id=1, source_target_pairs={{0,4},{2,6},{4,0},{6,2},{8,12},{10,14},{12,8},{14,10},{1,5},{3,7},... | collective-permute-start | bytes 393224 | tf_op jit(solution)/shard_map/ppermute | solution.py:67
  34.1 5.4 %collective-permute-start.2 = (bf16[16,2048]{1,0:T(8,128)(2,1)S(1)}, bf16[16,2048]{1,0:T(8,128)(2,1)S(1)}, u32[]{:S(2)}, u32[]{:S(2)}) collective-permute-start(bf16[16,2048]{1,0:T(8,128)(2,1)S(1)} %slice.53), channel_id=1, source_target_pairs={{0,8},{2,10},{4,12},{6,14},{8,0},{10,2},{12,4},{14,6},{1,9},{3,11}... | collective-permute-start | bytes 196616 | tf_op jit(solution)/shard_map/ppermute | solution.py:67
  35.5 6.0 %collective-permute-start.5 = (bf16[16,2048]{1,0:T(8,128)(2,1)S(1)}, bf16[16,2048]{1,0:T(8,128)(2,1)S(1)}, u32[]{:S(2)}, u32[]{:S(2)}) collective-permute-start(bf16[16,2048]{1,0:T(8,128)(2,1)S(1)} %slice.52), channel_id=1, source_target_pairs={{0,8},{2,10},{4,12},{6,14},{8,0},{10,2},{12,4},{14,6},{1,9},{3,11}... | collective-permute-start | bytes 196616 | tf_op jit(solution)/shard_map/ppermute | solution.py:67

commit v2 on v1

--- a/solution.py
+++ b/solution.py
@@ -67,15 +67,28 @@
     return lax.ppermute(x, "seq", [(i, i ^ mask) for i in range(n)])
 
 
-def project_kernel(order, pos_ref, len_ref, null_ref, w_ref, pack_ref, send_k, keep_k, send_v, keep_v):
-    n = len(order)
+SOURCES = (0, 4, 2, 6, 1, 5, 3, 7)
+TARGETS = (7, 3, 5, 1, 6, 2, 4, 0)
+
+
+def project_kernel(
+    pos_ref, len_ref, null_ref, w_ref, text_ref, code_ref, got_ref, send_k, keep_k, send_v, keep_v
+):
+    features = text_ref.shape[1]
+    text_dev = 2 * text_ref.shape[0] // len(SOURCES)
+    rows = len(TARGETS) * NULL_LEN
     pos = pos_ref[0]
-    text_dev = pack_ref.shape[1] // 2
-    rows = n * NULL_LEN
-    packs = [pack_ref[jnp.bitwise_xor(pos, m)] for m in order]
-    pack = jnp.concatenate(packs, axis=0)
+    got = got_ref[...].astype(jnp.float32)
+    text = jnp.concatenate([text_ref[...].astype(jnp.float32), got[:, :features]], axis=0)
+    codes = jnp.concatenate([code_ref[...].astype(jnp.float32), got[:, features:]], axis=0)
+    repeat = NULL_LEN // text_dev
     code = jnp.concatenate(
-        [p.astype(jnp.float32)[text_dev:, :128] for p in packs for _ in range(2)], axis=0
+        [
+            codes[SOURCES.index(m) * text_dev : (SOURCES.index(m) + 1) * text_dev]
+            for m in TARGETS
+            for _ in range(repeat)
+        ],
+        axis=0,
     ).astype(jnp.int32)
     reqs = len_ref.shape[0]
     uncond = code >= reqs
@@ -88,26 +101,34 @@
     wanted = start + lax.broadcasted_iota(jnp.int32, (rows, 128), 0) % NULL_LEN
     col = lax.broadcasted_iota(jnp.int32, (rows, 128), 1)
     held = jnp.full((rows, 128), -1, jnp.int32)
-    for slot, m in enumerate(order):
-        first = slot * 2 * text_dev
+    for slot, m in enumerate(SOURCES):
+        first = slot * text_dev
         base = jnp.bitwise_xor(pos, m) * text_dev - first
         held = jnp.where((col >= first) & (col < first + text_dev), col + base, held)
     pick = (held == wanted).astype(jnp.float32).astype(jnp.bfloat16)
-    text_sel = jnp.dot(pick, pack, preferred_element_type=jnp.float32)
-    null_sel = jnp.concatenate([null_ref[...].astype(jnp.float32)] * n, axis=0)
-    wide = jnp.concatenate([uncond] * (null_sel.shape[1] // 128), axis=1)
+    spare = jnp.zeros((128 - text.shape[0], features), jnp.float32)
+    text = jnp.concatenate([text, spare], axis=0).astype(jnp.bfloat16)
+    text_sel = jnp.dot(pick, text, preferred_element_type=jnp.float32)
+    null_sel = jnp.concatenate([null_ref[...].astype(jnp.float32)] * len(TARGETS), axis=0)
+    wide = jnp.concatenate([uncond] * (features // 128), axis=1)
     sel = jnp.where(wide, null_sel, text_sel).astype(jnp.bfloat16)
     half = rows // 2
+    quarter = rows // 4
     width = send_k.shape[1]
-    for kind, (send, keep) in enumerate(((send_k, keep_k), (send_v, keep_v))):
-        for c in range(0, width, 512):
-            part = jnp.dot(
-                sel,
-                w_ref[:, kind * width + c : kind * width + c + 512],
-                preferred_element_type=jnp.float32,
-            )
-            send[:, c : c + 512] = part[:half].astype(jnp.bfloat16)
-            keep[:, c : c + 512] = part[half:]
+    for c in range(0, width, 512):
+        cols = slice(c, c + 512)
+        part = jnp.dot(sel, w_ref[:, cols], preferred_element_type=jnp.float32)
+        send_k[:, cols] = part[:half].astype(jnp.bfloat16)
+        keep_k[:, cols] = part[half:]
+    for c in range(0, width, 512):
+        cols = slice(c, c + 512)
+        part = jnp.dot(
+            sel, w_ref[:, width + c : width + c + 512], preferred_element_type=jnp.float32
+        )
+        send_v[:quarter, cols] = part[:quarter].astype(jnp.bfloat16)
+        send_v[quarter:, cols] = part[half : half + quarter].astype(jnp.bfloat16)
+        keep_v[:quarter, cols] = part[quarter:half]
+        keep_v[quarter:, cols] = part[half + quarter :]
 
 
 def spread_heads(kept_ref, got_ref, wide_ref):
@@ -177,13 +198,20 @@
     reqs = prompt_lengths.shape[0]
     heads = width // HDIM
     pos = lax.axis_index("seq").astype(jnp.int32)
+    text = text_rows
     code = (block_owner[0] + reqs * uncond_flags[0]).astype(jnp.bfloat16)
-    packed = jnp.concatenate([text_rows, jnp.full(text_rows.shape, code, jnp.bfloat16)], axis=0)
-    packed = packed.reshape(-1, n, features).transpose(1, 0, 2)
-    packs = lax.all_to_all(packed, "seq", split_axis=0, concat_axis=0, tiled=True)
+    code = jnp.full((text_rows.shape[0], 128), code, jnp.bfloat16)
+    for mask in (4, 2, 1):
+        cut = text.shape[1] // 2
+        side = (pos // mask) % 2
+        theirs = lax.dynamic_slice_in_dim(text, (1 - side) * cut, cut, 1)
+        text = lax.dynamic_slice_in_dim(text, side * cut, cut, 1)
+        got = swap(jnp.concatenate([theirs, code], axis=1), n, mask)
+        if mask > 1:
+            text = jnp.concatenate([text, got[:, :cut]], axis=0)
+            code = jnp.concatenate([code, got[:, cut:]], axis=0)
     null_cols = lax.dynamic_slice_in_dim(null_rows, pos * features, features, 1)
     flat_weight = kv_weight.reshape(features, 2 * width)
-    order = [7, 3, 5, 1, 6, 2, 4, 0]
     half = n * NULL_LEN // 2
     sent = jax.ShapeDtypeStruct((half, width), jnp.bfloat16)
     kept = jax.ShapeDtypeStruct((half, width), jnp.float32)
@@ -191,9 +219,9 @@
     vmem = pl.BlockSpec(memory_space=pltpu.VMEM)
     params = pltpu.CompilerParams(vmem_limit_bytes=VMEM_LIMIT)
     send_k, keep_k, send_v, keep_v = pl.pallas_call(
-        functools.partial(project_kernel, order),
+        project_kernel,
         out_shape=[sent, kept] * 2,
-        in_specs=[smem, smem, vmem, vmem, vmem],
+        in_specs=[smem, smem] + [vmem] * 5,
         out_specs=[vmem] * 4,
         compiler_params=params,
         cost_estimate=pl.CostEstimate(
@@ -202,17 +230,17 @@
             transcendentals=0,
         ),
         name="project",
-    )(pos.reshape(1), prompt_lengths, null_cols, flat_weight, packs)
-
-    def reduce_parts(send, keep):
-        for mask in (1, 2):
+    )(pos.reshape(1), prompt_lengths, null_cols, flat_weight, text, code, got)
+
+    def reduce_parts(send, keep, masks):
+        for mask in masks:
             total = keep + swap(send, n, mask).astype(jnp.float32)
             cut = total.shape[0] // 2
             send, keep = total[:cut].astype(jnp.bfloat16), total[cut:]
         return keep, swap(send, n, 4)
 
-    k_parts = reduce_parts(send_k, keep_k)
-    v_parts = reduce_parts(send_v, keep_v)
+    k_parts = reduce_parts(send_k, keep_k, (1, 2))
+    v_parts = reduce_parts(send_v, keep_v, (2, 1))
 
     lanes = heads * NULL_LEN
     probs = pl.pallas_call(

time: 44.9 us -> 40.6 us (0.904)
  waiting for transfers between devices: 20.9 us -> 10.6 us
  starting transfers between devices: 11.9 us -> 18.6 us
  local copies, waits for them, and re-layouts: 3.98 us -> 3.33 us
    ppermute x6 -> x9, starting transfers between devices: 4.63 us -> 18.6 us  [swap(): return lax.ppermute(x, 'seq', [(i, i ^ mask) for i in range(n)])]
    all_to_all x1 -> x0, starting transfers between devices: 7.25 us -> none  [select_plan(): lax.all_to_all(packed, 'seq', split_axis=0, concat_axis=0, tiled=True)]
    ppermute x6 -> x9, waiting for transfers between devices: 16.5 us -> 10.6 us  [swap(): return lax.ppermute(x, 'seq', [(i, i ^ mask) for i in range(n)])]
    all_to_all x1 -> x0, waiting for transfers between devices: 4.39 us -> none  [select_plan(): lax.all_to_all(packed, 'seq', split_axis=0, concat_axis=0, tiled=True)]
    concatenate x1, local copies, waits for them, and re-layouts: 0.77 us -> 0.01 us  [select_plan(): got = swap(jnp.concatenate([theirs, code], axis=1), n, mask)]
    dynamic_slice x0 -> x1, local copies, waits for them, and re-layouts: none -> 0.74 us  [select_plan(): theirs = lax.dynamic_slice_in_dim(text, (1 - side) * cut, cut, 1)]
    reshape x1 -> x0, local copies, waits for them, and re-layouts: 0.64 us -> none  [select_plan(): packed = packed.reshape(-1, n, features).transpose(1, 0, 2)]
  transfers between devices with their start and end apart: 7 -> 9, of which waited for: 6 -> 6; matrix products, arithmetic and copies ran while one was open for 6% -> 7% of each run, Pallas kernels for 5% -> 5%
where the time goes in v2:
time: 40.6 us; the launch traced here: 40.3 us
  starting transfers between devices  18.6 us (46%)
  waiting for transfers between devices  10.6 us (26%)
  Pallas kernels  6.08 us (15%)
  local copies, waits for them, and re-layouts  3.33 us (8%)
  between operations  1.51 us (4%)
    ppermute x9, starting transfers between devices, swap(): return lax.ppermute(x, 'seq', [(i, i ^ mask) for i in range(n)])  18.6 us
    ppermute x9, waiting for transfers between devices, swap(): return lax.ppermute(x, 'seq', [(i, i ^ mask) for i in range(n)])  10.6 us
    pallas_call x1, Pallas kernels, select_plan(): pl.pallas_call(context_kernel, out_shape=jax.ShapeDtypeStruct((rows, widt...  2.96 us
    unnamed x7, local copies, waits for them, and re-layouts  2.5 us
    pallas_call x1, Pallas kernels, select_plan(): pl.pallas_call(probs_kernel, out_shape=jax.ShapeDtypeStruct((rows, lanes)...  2.03 us
    pallas_call x1, Pallas kernels, select_plan(): pl.pallas_call(project_kernel, out_shape=[sent, kept] * 2, in_specs=[smem...  1.09 us
  transfers between devices with their start and end apart: 9, of which 6 were waited for; matrix products, arithmetic and copies ran while one was open for 7% of the time, Pallas kernels for 5%

profile of v2, /device:TPU:0, one launch (start us, length us, event | category | flops | bytes accessed | tf_op | source)
XLA Modules:
  0.0 40.3 jit_solution(8864384196777467226)
XLA Ops:
  0.0 0.0 copy-start
  0.0 0.0 copy-start.2
  1.3 0.7 %constant_dynamic-slice_fusion = (bf16[8,1024]{1,0:T(8,128)(2,1)S(1)}, bf16[8,1024]{1,0:T(8,128)(2,1)S(1)}) fusion(bf16[8,2048]{1,0:T(8,128)(2,1)} %param.8, s32[]{:T(128)S(6)} %select_n.48, s32[]{:T(128)S(6)} %select_n.47), kind=kLoop, calls=%fused_computation.25 | loop fusion | bytes 65544 | tf_op jit(solution)/shard_map/dynamic_slice | solution.py:207
  2.1 4.0 %collective-permute-start = (bf16[8,1152]{1,0:T(8,128)(2,1)S(1)}, bf16[8,1152]{1,0:T(8,128)(2,1)S(1)}, u32[]{:S(2)}, u32[]{:S(2)}) collective-permute-start(bf16[8,1152]{1,0:T(8,128)(2,1)S(1)} %concatenate.22), channel_id=1, source_target_pairs={{0,8},{2,10},{4,12},{6,14},{8,0},{10,2},{12,4},{14,6},{1,9},{3,11}... | collective-permute-start | bytes 55304 | tf_op jit(solution)/shard_map/ppermute | solution.py:67
  6.1 1.7 %collective-permute-done = bf16[8,1152]{1,0:T(8,128)(2,1)S(1)} collective-permute-done((bf16[8,1152]{1,0:T(8,128)(2,1)S(1)}, bf16[8,1152]{1,0:T(8,128)(2,1)S(1)}, u32[]{:S(2)}, u32[]{:S(2)}) %collective-permute-start) | collective-permute-done | bytes 18464 | tf_op jit(solution)/shard_map/ppermute | solution.py:67
  7.9 2.0 %collective-permute-start.1 = (bf16[16,640]{1,0:T(8,128)(2,1)S(1)}, bf16[16,640]{1,0:T(8,128)(2,1)S(1)}, u32[]{:S(2)}, u32[]{:S(2)}) collective-permute-start(bf16[16,640]{1,0:T(8,128)(2,1)S(1)} %fusion.1), channel_id=1, source_target_pairs={{0,4},{2,6},{4,0},{6,2},{8,12},{10,14},{12,8},{14,10},{1,5},{3,7},... | collective-permute-start | bytes 61448 | tf_op jit(solution)/shard_map/ppermute | solution.py:67
  9.9 0.0 copy-done
  9.9 2.5 %copy.8 = bf16[32,8,2,2048]{3,1,2,0:T(8,128)(2,1)S(1)} copy(bf16[32,8,2,2048]{3,2,1,0:T(2,128)(2,1)} %bitcast.5) | data formatting | bytes 4194304
  12.4 0.0 collective-permute-done.1
  12.4 1.6 %collective-permute-start.2 = (bf16[32,384]{1,0:T(8,128)(2,1)S(1)}, bf16[32,384]{1,0:T(8,128)(2,1)S(1)}, u32[]{:S(2)}, u32[]{:S(2)}) collective-permute-start(bf16[32,384]{1,0:T(8,128)(2,1)S(1)} %maximum_maximum_fusion), channel_id=1, source_target_pairs={{0,2},{2,0},{4,6},{6,4},{8,10},{10,8},{12,14},{14,12},{1,3},{3,1},... | collective-permute-start | bytes 73736 | tf_op jit(solution)/shard_map/ppermute | solution.py:67
  14.0 2.3 %collective-permute-done.2.got_ref = bf16[32,384]{1,0:T(8,128)(2,1)S(1)} collective-permute-done((bf16[32,384]{1,0:T(8,128)(2,1)S(1)}, bf16[32,384]{1,0:T(8,128)(2,1)S(1)}, u32[]{:S(2)}, u32[]{:S(2)}) %collective-permute-start.2) | collective-permute-done | bytes 24608 | tf_op jit(solution)/shard_map/ppermute | solution.py:67
  16.3 0.0 copy-done.2
  16.3 1.1 %project.1 = (bf16[64,2048]{1,0:T(8,128)(2,1)S(1)}, f32[64,2048]{1,0:T(8,128)S(1)}, bf16[64,2048]{1,0:T(8,128)(2,1)S(1)}, f32[64,2048]{1,0:T(8,128)S(1)}) custom-call(s32[1]{0:T(128)} %bitcast.pos_ref, s32[8]{0:T(128)S(1)} %copy-done.2, bf16[16,256]{1,0:T(8,128)(2,1)S(1)} %constant_dynamic-slice_fusion.2.null_ref, bf16[256,4096]{1,0:T(8,128)(2,1)S(1)} %bitcast.4, ...), custom_call_target="tpu_custom_call" | custom-call | flops 268435456 | bytes 4194304 | tf_op jit(solution)/shard_map/project/pallas_call | solution.py:221
  17.4 0.0 copy-start.1
  17.4 1.6 %collective-permute-start.3 = (bf16[64,2048]{1,0:T(8,128)(2,1)S(1)}, bf16[64,2048]{1,0:T(8,128)(2,1)S(1)}, u32[]{:S(2)}, u32[]{:S(2)}) collective-permute-start(bf16[64,2048]{1,0:T(8,128)(2,1)S(1)} %get-tuple-element.10), channel_id=1, source_target_pairs={{0,2},{2,0},{4,6},{6,4},{8,10},{10,8},{12,14},{14,12},{1,3},{3,1},... | collective-permute-start | bytes 786440 | tf_op jit(solution)/shard_map/ppermute | solution.py:67
  19.0 1.2 %collective-permute-start.6 = (bf16[64,2048]{1,0:T(8,128)(2,1)S(1)}, bf16[64,2048]{1,0:T(8,128)(2,1)S(1)}, u32[]{:S(2)}, u32[]{:S(2)}) collective-permute-start(bf16[64,2048]{1,0:T(8,128)(2,1)S(1)} %get-tuple-element.12), channel_id=1, source_target_pairs={{0,4},{2,6},{4,0},{6,2},{8,12},{10,14},{12,8},{14,10},{1,5},{3,7},... | collective-permute-start | bytes 786440 | tf_op jit(solution)/shard_map/ppermute | solution.py:67
  20.2 3.6 %collective-permute-done.3 = bf16[64,2048]{1,0:T(8,128)(2,1)S(1)} collective-permute-done((bf16[64,2048]{1,0:T(8,128)(2,1)S(1)}, bf16[64,2048]{1,0:T(8,128)(2,1)S(1)}, u32[]{:S(2)}, u32[]{:S(2)}) %collective-permute-start.3) | collective-permute-done | bytes 262176 | tf_op jit(solution)/shard_map/ppermute | solution.py:67
  23.9 0.1 convert_add_fusion.1
  24.0 1.7 %collective-permute-start.4 = (bf16[32,2048]{1,0:T(8,128)(2,1)S(1)}, bf16[32,2048]{1,0:T(8,128)(2,1)S(1)}, u32[]{:S(2)}, u32[]{:S(2)}) collective-permute-start(bf16[32,2048]{1,0:T(8,128)(2,1)S(1)} %slice.71), channel_id=1, source_target_pairs={{0,4},{2,6},{4,0},{6,2},{8,12},{10,14},{12,8},{14,10},{1,5},{3,7},... | collective-permute-start | bytes 393224 | tf_op jit(solution)/shard_map/ppermute | solution.py:67
  25.7 1.1 %collective-permute-done.6 = bf16[64,2048]{1,0:T(8,128)(2,1)S(1)} collective-permute-done((bf16[64,2048]{1,0:T(8,128)(2,1)S(1)}, bf16[64,2048]{1,0:T(8,128)(2,1)S(1)}, u32[]{:S(2)}, u32[]{:S(2)}) %collective-permute-start.6) | collective-permute-done | bytes 262176 | tf_op jit(solution)/shard_map/ppermute | solution.py:67
  26.8 0.1 convert_add_fusion
  26.9 0.6 %collective-permute-start.7 = (bf16[32,2048]{1,0:T(8,128)(2,1)S(1)}, bf16[32,2048]{1,0:T(8,128)(2,1)S(1)}, u32[]{:S(2)}, u32[]{:S(2)}) collective-permute-start(bf16[32,2048]{1,0:T(8,128)(2,1)S(1)} %slice.70), channel_id=1, source_target_pairs={{0,2},{2,0},{4,6},{6,4},{8,10},{10,8},{12,14},{14,12},{1,3},{3,1},... | collective-permute-start | bytes 393224 | tf_op jit(solution)/shard_map/ppermute | solution.py:67
  27.5 1.5 %collective-permute-done.4 = bf16[32,2048]{1,0:T(8,128)(2,1)S(1)} collective-permute-done((bf16[32,2048]{1,0:T(8,128)(2,1)S(1)}, bf16[32,2048]{1,0:T(8,128)(2,1)S(1)}, u32[]{:S(2)}, u32[]{:S(2)}) %collective-permute-start.4) | collective-permute-done | bytes 131104 | tf_op jit(solution)/shard_map/ppermute | solution.py:67
  29.1 2.9 %collective-permute-start.5 = (bf16[16,2048]{1,0:T(8,128)(2,1)S(1)}, bf16[16,2048]{1,0:T(8,128)(2,1)S(1)}, u32[]{:S(2)}, u32[]{:S(2)}) collective-permute-start(bf16[16,2048]{1,0:T(8,128)(2,1)S(1)} %slice.73), channel_id=1, source_target_pairs={{0,8},{2,10},{4,12},{6,14},{8,0},{10,2},{12,4},{14,6},{1,9},{3,11}... | collective-permute-start | bytes 196616 | tf_op jit(solution)/shard_map/ppermute | solution.py:67
  31.9 0.0 collective-permute-done.7
  32.0 3.0 %collective-permute-start.8 = (bf16[16,2048]{1,0:T(8,128)(2,1)S(1)}, bf16[16,2048]{1,0:T(8,128)(2,1)S(1)}, u32[]{:S(2)}, u32[]{:S(2)}) collective-permute-start(bf16[16,2048]{1,0:T(8,128)(2,1)S(1)} %slice.72), channel_id=1, source_target_pairs={{0,8},{2,10},{4,12},{6,14},{8,0},{10,2},{12,4},{14,6},{1,9},{3,11}... | collective-permute-start | bytes 196616 | tf_op jit(solution)/shard_map/ppermute | solution.py:67
  35.1 0.0 collective-permute-done.5.got_ref
  35.1 0.0 copy-done.1
  35.1 2.0 %probs.1.p_ref = bf16[768,256]{1,0:T(8,128)(2,1)S(1)} custom-call(s32[8]{0:T(128)S(1)} %copy-done.2, s32[1]{0:T(128)S(6)} %copy.9.own_ref, s32[1]{0:T(128)S(6)} %copy.10.flag_ref, bf16[768,2048]{1,0:T(8,128)(2,1)S(1)} %copy-done.1, f32[16,2048]{1,0:T(8,128)S(1)} %slice.58.kept_ref, bf16[16,2048]{1,0:T(8,128)(2,1)S(1)} %collective-permute-done.5.got_ref), custom_call_target="tpu_custom_call" | custom-call | flops 805306368 | bytes 3145728 | tf_op jit(solution)/shard_map/probs/pallas_call | solution.py:246
  37.1 0.2 collective-permute-done.8.got_ref
  37.3 3.0 %context.1 = bf16[768,2048]{1,0:T(8,128)(2,1)} custom-call(bf16[768,256]{1,0:T(8,128)(2,1)S(1)} %probs.1.p_ref, f32[16,2048]{1,0:T(8,128)S(1)} %slice.62.kept_ref, bf16[16,2048]{1,0:T(8,128)(2,1)S(1)} %collective-permute-done.8.got_ref), custom_call_target="tpu_custom_call" | custom-call | flops 805306368 | bytes 3145728 | tf_op jit(solution)/shard_map/context/pallas_call | solution.py:259
  (20 shorter events, 0.2 us)
Async XLA Ops:
  0.0 9.9 %copy-start = (bf16[16,2048]{1,0:T(8,128)(2,1)S(1)}, bf16[16,2048]{1,0:T(8,128)(2,1)}, u32[]{:S(2)}) copy-start(bf16[16,2048]{1,0:T(8,128)(2,1)} %param.9) | copy-start | bytes 196612
  0.0 16.3 %copy-start.2 = (s32[8]{0:T(128)S(1)}, s32[8]{0:T(128)}, u32[]{:S(2)}) copy-start(s32[8]{0:T(128)} %len_ref.3) | copy-start | bytes 100
  2.1 5.8 %collective-permute-start = (bf16[8,1152]{1,0:T(8,128)(2,1)S(1)}, bf16[8,1152]{1,0:T(8,128)(2,1)S(1)}, u32[]{:S(2)}, u32[]{:S(2)}) collective-permute-start(bf16[8,1152]{1,0:T(8,128)(2,1)S(1)} %concatenate.22), channel_id=1, source_target_pairs={{0,8},{2,10},{4,12},{6,14},{8,0},{10,2},{12,4},{14,6},{1,9},{3,11}... | collective-permute-start | bytes 55304 | tf_op jit(solution)/shard_map/ppermute | solution.py:67
  7.9 4.5 %collective-permute-start.1 = (bf16[16,640]{1,0:T(8,128)(2,1)S(1)}, bf16[16,640]{1,0:T(8,128)(2,1)S(1)}, u32[]{:S(2)}, u32[]{:S(2)}) collective-permute-start(bf16[16,640]{1,0:T(8,128)(2,1)S(1)} %fusion.1), channel_id=1, source_target_pairs={{0,4},{2,6},{4,0},{6,2},{8,12},{10,14},{12,8},{14,10},{1,5},{3,7},... | collective-permute-start | bytes 61448 | tf_op jit(solution)/shard_map/ppermute | solution.py:67
  12.4 3.9 %collective-permute-start.2 = (bf16[32,384]{1,0:T(8,128)(2,1)S(1)}, bf16[32,384]{1,0:T(8,128)(2,1)S(1)}, u32[]{:S(2)}, u32[]{:S(2)}) collective-permute-start(bf16[32,384]{1,0:T(8,128)(2,1)S(1)} %maximum_maximum_fusion), channel_id=1, source_target_pairs={{0,2},{2,0},{4,6},{6,4},{8,10},{10,8},{12,14},{14,12},{1,3},{3,1},... | collective-permute-start | bytes 73736 | tf_op jit(solution)/shard_map/ppermute | solution.py:67
  17.4 17.6 %copy-start.1 = (bf16[768,2048]{1,0:T(8,128)(2,1)S(1)}, bf16[768,2048]{1,0:T(8,128)(2,1)}, u32[]{:S(2)}) copy-start(bf16[768,2048]{1,0:T(8,128)(2,1)} %q_ref.1) | copy-start | bytes 9437188
  17.4 6.4 %collective-permute-start.3 = (bf16[64,2048]{1,0:T(8,128)(2,1)S(1)}, bf16[64,2048]{1,0:T(8,128)(2,1)S(1)}, u32[]{:S(2)}, u32[]{:S(2)}) collective-permute-start(bf16[64,2048]{1,0:T(8,128)(2,1)S(1)} %get-tuple-element.10), channel_id=1, source_target_pairs={{0,2},{2,0},{4,6},{6,4},{8,10},{10,8},{12,14},{14,12},{1,3},{3,1},... | collective-permute-start | bytes 786440 | tf_op jit(solution)/shard_map/ppermute | solution.py:67
  19.0 7.8 %collective-permute-start.6 = (bf16[64,2048]{1,0:T(8,128)(2,1)S(1)}, bf16[64,2048]{1,0:T(8,128)(2,1)S(1)}, u32[]{:S(2)}, u32[]{:S(2)}) collective-permute-start(bf16[64,2048]{1,0:T(8,128)(2,1)S(1)} %get-tuple-element.12), channel_id=1, source_target_pairs={{0,4},{2,6},{4,0},{6,2},{8,12},{10,14},{12,8},{14,10},{1,5},{3,7},... | collective-permute-start | bytes 786440 | tf_op jit(solution)/shard_map/ppermute | solution.py:67
  24.0 5.0 %collective-permute-start.4 = (bf16[32,2048]{1,0:T(8,128)(2,1)S(1)}, bf16[32,2048]{1,0:T(8,128)(2,1)S(1)}, u32[]{:S(2)}, u32[]{:S(2)}) collective-permute-start(bf16[32,2048]{1,0:T(8,128)(2,1)S(1)} %slice.71), channel_id=1, source_target_pairs={{0,4},{2,6},{4,0},{6,2},{8,12},{10,14},{12,8},{14,10},{1,5},{3,7},... | collective-permute-start | bytes 393224 | tf_op jit(solution)/shard_map/ppermute | solution.py:67
  26.9 5.1 %collective-permute-start.7 = (bf16[32,2048]{1,0:T(8,128)(2,1)S(1)}, bf16[32,2048]{1,0:T(8,128)(2,1)S(1)}, u32[]{:S(2)}, u32[]{:S(2)}) collective-permute-start(bf16[32,2048]{1,0:T(8,128)(2,1)S(1)} %slice.70), channel_id=1, source_target_pairs={{0,2},{2,0},{4,6},{6,4},{8,10},{10,8},{12,14},{14,12},{1,3},{3,1},... | collective-permute-start | bytes 393224 | tf_op jit(solution)/shard_map/ppermute | solution.py:67
  29.1 6.0 %collective-permute-start.5 = (bf16[16,2048]{1,0:T(8,128)(2,1)S(1)}, bf16[16,2048]{1,0:T(8,128)(2,1)S(1)}, u32[]{:S(2)}, u32[]{:S(2)}) collective-permute-start(bf16[16,2048]{1,0:T(8,128)(2,1)S(1)} %slice.73), channel_id=1, source_target_pairs={{0,8},{2,10},{4,12},{6,14},{8,0},{10,2},{12,4},{14,6},{1,9},{3,11}... | collective-permute-start | bytes 196616 | tf_op jit(solution)/shard_map/ppermute | solution.py:67
  32.0 5.3 %collective-permute-start.8 = (bf16[16,2048]{1,0:T(8,128)(2,1)S(1)}, bf16[16,2048]{1,0:T(8,128)(2,1)S(1)}, u32[]{:S(2)}, u32[]{:S(2)}) collective-permute-start(bf16[16,2048]{1,0:T(8,128)(2,1)S(1)} %slice.72), channel_id=1, source_target_pairs={{0,8},{2,10},{4,12},{6,14},{8,0},{10,2},{12,4},{14,6},{1,9},{3,11}... | collective-permute-start | bytes 196616 | tf_op jit(solution)/shard_map/ppermute | solution.py:67

commit v3 on v2

--- a/solution.py
+++ b/solution.py
@@ -71,22 +71,28 @@
 TARGETS = (7, 3, 5, 1, 6, 2, 4, 0)
 
 
+def weight_kernel(w_ref, after_ref, out_ref):
+    del after_ref
+    rows, width = out_ref.shape
+    flat = w_ref.reshape(rows, width)
+    for c in range(0, width, 512):
+        out_ref[:, c : c + 512] = flat[:, c : c + 512]
+
+
 def project_kernel(
-    pos_ref, len_ref, null_ref, w_ref, text_ref, code_ref, got_ref, send_k, keep_k, send_v, keep_v
+    pos_ref, len_ref, null_ref, w0_ref, w1_ref, held_ref, send_k, keep_k, send_v, keep_v, count_ref
 ):
-    features = text_ref.shape[1]
-    text_dev = 2 * text_ref.shape[0] // len(SOURCES)
+    features = null_ref.shape[1]
+    text_dev = held_ref.shape[0] // len(SOURCES)
     rows = len(TARGETS) * NULL_LEN
     pos = pos_ref[0]
-    got = got_ref[...].astype(jnp.float32)
-    text = jnp.concatenate([text_ref[...].astype(jnp.float32), got[:, :features]], axis=0)
-    codes = jnp.concatenate([code_ref[...].astype(jnp.float32), got[:, features:]], axis=0)
-    repeat = NULL_LEN // text_dev
+    text = held_ref[:, :features]
+    codes = held_ref[:, features:].astype(jnp.float32)
     code = jnp.concatenate(
         [
             codes[SOURCES.index(m) * text_dev : (SOURCES.index(m) + 1) * text_dev]
             for m in TARGETS
-            for _ in range(repeat)
+            for _ in range(NULL_LEN // text_dev)
         ],
         axis=0,
     ).astype(jnp.int32)
@@ -106,29 +112,40 @@
         base = jnp.bitwise_xor(pos, m) * text_dev - first
         held = jnp.where((col >= first) & (col < first + text_dev), col + base, held)
     pick = (held == wanted).astype(jnp.float32).astype(jnp.bfloat16)
-    spare = jnp.zeros((128 - text.shape[0], features), jnp.float32)
-    text = jnp.concatenate([text, spare], axis=0).astype(jnp.bfloat16)
+    text = jnp.concatenate([text, jnp.zeros((128 - text.shape[0], features), jnp.bfloat16)], axis=0)
     text_sel = jnp.dot(pick, text, preferred_element_type=jnp.float32)
     null_sel = jnp.concatenate([null_ref[...].astype(jnp.float32)] * len(TARGETS), axis=0)
     wide = jnp.concatenate([uncond] * (features // 128), axis=1)
     sel = jnp.where(wide, null_sel, text_sel).astype(jnp.bfloat16)
+    own = TARGETS.index(0) * NULL_LEN
+    count = jnp.zeros_like(owner[own : own + 8])
+    for r in range(reqs):
+        count = jnp.where(owner[own : own + 8] == r, len_ref[r], count)
+    count_ref[...] = jnp.where(uncond[own : own + 8], NULL_LEN, count)
+    feature = lax.broadcasted_iota(jnp.int32, (features, 2 * features), 0)
+    place = lax.broadcasted_iota(jnp.int32, (features, 2 * features), 1)
+    spread = [
+        jnp.dot(
+            sel,
+            (place == 2 * feature + kind).astype(jnp.float32).astype(jnp.bfloat16),
+            preferred_element_type=jnp.float32,
+        )
+        for kind in range(2)
+    ]
+    spread = jnp.concatenate(spread, axis=0).astype(jnp.bfloat16)
     half = rows // 2
     quarter = rows // 4
     width = send_k.shape[1]
     for c in range(0, width, 512):
         cols = slice(c, c + 512)
-        part = jnp.dot(sel, w_ref[:, cols], preferred_element_type=jnp.float32)
+        w_ref, at = (w0_ref, c) if c < w0_ref.shape[1] else (w1_ref, c - w0_ref.shape[1])
+        part = jnp.dot(spread, w_ref[:, at : at + 512], preferred_element_type=jnp.float32)
         send_k[:, cols] = part[:half].astype(jnp.bfloat16)
-        keep_k[:, cols] = part[half:]
-    for c in range(0, width, 512):
-        cols = slice(c, c + 512)
-        part = jnp.dot(
-            sel, w_ref[:, width + c : width + c + 512], preferred_element_type=jnp.float32
-        )
-        send_v[:quarter, cols] = part[:quarter].astype(jnp.bfloat16)
-        send_v[quarter:, cols] = part[half : half + quarter].astype(jnp.bfloat16)
-        keep_v[:quarter, cols] = part[quarter:half]
-        keep_v[quarter:, cols] = part[half + quarter :]
+        keep_k[:, cols] = part[half:rows]
+        send_v[:quarter, cols] = part[rows : rows + quarter].astype(jnp.bfloat16)
+        send_v[quarter:, cols] = part[rows + half : rows + half + quarter].astype(jnp.bfloat16)
+        keep_v[:quarter, cols] = part[rows + quarter : rows + half]
+        keep_v[quarter:, cols] = part[rows + half + quarter :]
 
 
 def spread_heads(kept_ref, got_ref, wide_ref):
@@ -144,13 +161,10 @@
         wide_ref[key * heads : (key + 1) * heads] = block.astype(jnp.bfloat16)
 
 
-def probs_kernel(len_ref, own_ref, flag_ref, q_ref, kept_ref, got_ref, out_ref, wide_ref):
+def probs_kernel(count_ref, q_ref, kept_ref, got_ref, out_ref, wide_ref):
     heads = q_ref.shape[1] // HDIM
     spread_heads(kept_ref, got_ref, wide_ref)
-    count = jnp.int32(0)
-    for r in range(len_ref.shape[0]):
-        count = jnp.where(own_ref[0] == r, len_ref[r], count)
-    count = jnp.where(flag_ref[0] == 1, NULL_LEN, count)
+    count = jnp.broadcast_to(jnp.concatenate([count_ref[:1]] * (out_ref.shape[1] // 128), axis=1), (256, out_ref.shape[1]))
     block = 256
     for first in range(0, q_ref.shape[0], block):
         scores = lax.dot_general(
@@ -179,16 +193,19 @@
         ).astype(jnp.bfloat16)
 
 
-def context_kernel(p_ref, kept_ref, got_ref, out_ref, wide_ref):
-    @pl.when(pl.program_id(0) == 0)
-    def _():
-        spread_heads(kept_ref, got_ref, wide_ref)
-
-    block = out_ref.shape[0]
-    first = pl.multiple_of(pl.program_id(0) * block, block)
-    out_ref[...] = jnp.dot(
-        p_ref[pl.ds(first, block)], wide_ref[...], preferred_element_type=jnp.float32
-    ).astype(jnp.bfloat16)
+def context_kernel(p_ref, kept_ref, got_ref, out_hbm, wide_ref, out_ref, sems):
+    spread_heads(kept_ref, got_ref, wide_ref)
+    block = out_ref.shape[0] // sems.shape[0]
+    copies = []
+    for i in range(sems.shape[0]):
+        rows = pl.ds(i * block, block)
+        out_ref[rows] = jnp.dot(
+            p_ref[rows], wide_ref[...], preferred_element_type=jnp.float32
+        ).astype(jnp.bfloat16)
+        copies.append(pltpu.make_async_copy(out_ref.at[rows], out_hbm.at[rows], sems.at[i]))
+        copies[-1].start()
+    for copy in copies:
+        copy.wait()
 
 
 def select_plan(n, queries, text_rows, null_rows, kv_weight, prompt_lengths, block_owner, uncond_flags):
@@ -198,31 +215,61 @@
     reqs = prompt_lengths.shape[0]
     heads = width // HDIM
     pos = lax.axis_index("seq").astype(jnp.int32)
+    smem = pl.BlockSpec(memory_space=pltpu.SMEM)
+    vmem = pl.BlockSpec(memory_space=pltpu.VMEM)
+    anywhere = pl.BlockSpec(memory_space=pl.ANY)
+    params = pltpu.CompilerParams(vmem_limit_bytes=VMEM_LIMIT)
+
+    def lay_out(first, after):
+        return pl.pallas_call(
+            weight_kernel,
+            out_shape=jax.ShapeDtypeStruct((2 * features, width // 2), jnp.bfloat16),
+            grid=(1,),
+            in_specs=[
+                pl.BlockSpec((features, 2, width // 2), lambda i: (0, 0, first)),
+                anywhere,
+            ],
+            out_specs=pl.BlockSpec((2 * features, width // 2), lambda i: (0, 0)),
+            compiler_params=params,
+            cost_estimate=pl.CostEstimate(
+                flops=0, bytes_accessed=4 * features * width, transcendentals=0
+            ),
+            name="weight",
+        )(kv_weight, after)
+
+    def swap_last(x, mask):
+        pairs = [(2 * i + 1, 2 * (i ^ mask) + 1) for i in range(n)]
+        return lax.ppermute(x, ("seq", "head"), pairs)
+
     text = text_rows
     code = (block_owner[0] + reqs * uncond_flags[0]).astype(jnp.bfloat16)
     code = jnp.full((text_rows.shape[0], 128), code, jnp.bfloat16)
-    for mask in (4, 2, 1):
+    weights = []
+    for stage, mask in enumerate((4, 2, 1)):
         cut = text.shape[1] // 2
         side = (pos // mask) % 2
         theirs = lax.dynamic_slice_in_dim(text, (1 - side) * cut, cut, 1)
         text = lax.dynamic_slice_in_dim(text, side * cut, cut, 1)
-        got = swap(jnp.concatenate([theirs, code], axis=1), n, mask)
-        if mask > 1:
-            text = jnp.concatenate([text, got[:, :cut]], axis=0)
-            code = jnp.concatenate([code, got[:, cut:]], axis=0)
+        send = jnp.concatenate([theirs, code], axis=1)
+        if stage:
+            send, weights[-1] = lax.optimization_barrier((send, weights[-1]))
+        got = swap_last(send, mask)
+        if stage < 2:
+            weights.append(lay_out(stage, send))
+        text = jnp.concatenate([text, got[:, :cut]], axis=0)
+        code = jnp.concatenate([code, got[:, cut:]], axis=0)
+    held = jnp.concatenate([text, code], axis=1)
+    handed = lax.ppermute(held, ("seq", "head"), [(2 * i + 1, 2 * i) for i in range(n)])
+    held = jnp.where(lax.axis_index("head") == 1, held, handed)
     null_cols = lax.dynamic_slice_in_dim(null_rows, pos * features, features, 1)
-    flat_weight = kv_weight.reshape(features, 2 * width)
     half = n * NULL_LEN // 2
     sent = jax.ShapeDtypeStruct((half, width), jnp.bfloat16)
     kept = jax.ShapeDtypeStruct((half, width), jnp.float32)
-    smem = pl.BlockSpec(memory_space=pltpu.SMEM)
-    vmem = pl.BlockSpec(memory_space=pltpu.VMEM)
-    params = pltpu.CompilerParams(vmem_limit_bytes=VMEM_LIMIT)
-    send_k, keep_k, send_v, keep_v = pl.pallas_call(
+    send_k, keep_k, send_v, keep_v, count = pl.pallas_call(
         project_kernel,
-        out_shape=[sent, kept] * 2,
-        in_specs=[smem, smem] + [vmem] * 5,
-        out_specs=[vmem] * 4,
+        out_shape=[sent, kept] * 2 + [jax.ShapeDtypeStruct((8, 128), jnp.int32)],
+        in_specs=[smem, smem] + [vmem] * 4,
+        out_specs=[vmem] * 5,
         compiler_params=params,
         cost_estimate=pl.CostEstimate(
             flops=2 * 2 * half * features * 2 * width,
@@ -230,7 +277,7 @@
             transcendentals=0,
         ),
         name="project",
-    )(pos.reshape(1), prompt_lengths, null_cols, flat_weight, text, code, got)
+    )(pos.reshape(1), prompt_lengths, null_cols, *weights, held)
 
     def reduce_parts(send, keep, masks):
         for mask in masks:
@@ -246,7 +293,7 @@
     probs = pl.pallas_call(
         probs_kernel,
         out_shape=jax.ShapeDtypeStruct((rows, lanes), jnp.bfloat16),
-        in_specs=[smem] * 3 + [vmem] * 3,
+        in_specs=[vmem] * 4,
         out_specs=vmem,
         scratch_shapes=[pltpu.VMEM((lanes, width), jnp.bfloat16)],
         compiler_params=params,
@@ -254,15 +301,17 @@
             flops=2 * rows * width * lanes, bytes_accessed=2 * rows * width, transcendentals=rows * lanes
         ),
         name="probs",
-    )(prompt_lengths, block_owner, uncond_flags, queries, *k_parts)
-    block = 256
+    )(count, queries, *k_parts)
     return pl.pallas_call(
         context_kernel,
         out_shape=jax.ShapeDtypeStruct((rows, width), jnp.bfloat16),
-        grid=(rows // block,),
         in_specs=[vmem] * 3,
-        out_specs=pl.BlockSpec((block, width), lambda i: (i, 0)),
-        scratch_shapes=[pltpu.VMEM((lanes, width), jnp.bfloat16)],
+        out_specs=anywhere,
+        scratch_shapes=[
+            pltpu.VMEM((lanes, width), jnp.bfloat16),
+            pltpu.VMEM((rows, width), jnp.bfloat16),
+            pltpu.SemaphoreType.DMA((6,)),
+        ],
         compiler_params=params,
         cost_estimate=pl.CostEstimate(
             flops=2 * rows * width * lanes, bytes_accessed=2 * rows * width, transcendentals=0
@@ -276,7 +325,7 @@
 
     def per_device(queries, text_rows, null_rows, kv_weight, *rest):
         longest = n * text_rows.shape[0] // 4
-        few = n == 8 and longest == NULL_LEN and text_rows.shape[0] == 8
+        few = n == 8 and mesh.shape["head"] == 2 and longest == NULL_LEN and text_rows.shape[0] == 8
         if few:
             return select_plan(n, queries, text_rows, null_rows, kv_weight, *rest)
         return gather_plan(queries, text_rows, null_rows, kv_weight, *rest)

time: 40.6 us -> 48.1 us (1.18)
  waiting for transfers between devices: 10.6 us -> 23.7 us
  starting transfers between devices: 18.6 us -> 12 us
  local copies, waits for them, and re-layouts: 3.33 us -> 4.7 us
  Pallas kernels: 6.08 us -> 5.42 us
    ppermute x0 -> x4, waiting for transfers between devices: none -> 12.9 us  [the longest x1 12.9 us: select_plan(): lax.ppermute(held, ('seq', 'head'), [(2 * i + 1, 2 * i) for i in range(n)])]
    ppermute x9 -> x6, starting transfers between devices: 18.6 us -> 8.73 us  [swap(): return lax.ppermute(x, 'seq', [(i, i ^ mask) for i in range(n)])]
    ppermute x0 -> x4, starting transfers between devices: none -> 3.27 us  [the longest x3 1.98 us: swap_last(): return lax.ppermute(x, ('seq', 'head'), pairs)]
    unnamed x7 -> x14, local copies, waits for them, and re-layouts: 2.5 us -> 3.85 us
    pallas_call x1, Pallas kernels: 2.96 us -> 2.03 us  [select_plan(): pl.pallas_call(context_kernel, out_shape=jax.ShapeDtypeStruct((rows, widt...]
    pallas_call x1 -> x3, Pallas kernels: 1.09 us -> 1.9 us  [the longest x1 1.5 us: select_plan(): pl.pallas_call(project_kernel, out_shape=[sent, kept] * 2 + [jax.ShapeDty...]
    pallas_call x1, Pallas kernels: 2.03 us -> 1.48 us  [select_plan(): pl.pallas_call(probs_kernel, out_shape=jax.ShapeDtypeStruct((rows, lanes)...]
    ppermute x9 -> x6, waiting for transfers between devices: 10.6 us -> 10.8 us  [swap(): return lax.ppermute(x, 'seq', [(i, i ^ mask) for i in range(n)])]
  transfers between devices with their start and end apart: 9 -> 10, of which waited for: 6 -> 6; matrix products, arithmetic and copies ran while one was open for 7% -> 0% of each run, Pallas kernels for 5% -> 4%
where the time goes in v3:
time: 48.1 us; the launch traced here: 47.7 us
  waiting for transfers between devices  23.7 us (49%)
  starting transfers between devices  12 us (25%)
  Pallas kernels  5.42 us (11%)
  local copies, waits for them, and re-layouts  4.7 us (10%)
  between operations  1.68 us (3%)
    ppermute x1, waiting for transfers between devices, select_plan(): lax.ppermute(held, ('seq', 'head'), [(2 * i + 1, 2 * i) for i in range(n)])  12.9 us
    ppermute x6, waiting for transfers between devices, swap(): return lax.ppermute(x, 'seq', [(i, i ^ mask) for i in range(n)])  10.8 us
    ppermute x6, starting transfers between devices, swap(): return lax.ppermute(x, 'seq', [(i, i ^ mask) for i in range(n)])  8.73 us
    unnamed x14, local copies, waits for them, and re-layouts  3.85 us
    pallas_call x1, Pallas kernels, select_plan(): pl.pallas_call(context_kernel, out_shape=jax.ShapeDtypeStruct((rows, widt...  2.03 us
    ppermute x3, starting transfers between devices, swap_last(): return lax.ppermute(x, ('seq', 'head'), pairs)  1.98 us
    pallas_call x1, Pallas kernels, select_plan(): pl.pallas_call(project_kernel, out_shape=[sent, kept] * 2 + [jax.ShapeDty...  1.5 us
    pallas_call x1, Pallas kernels, select_plan(): pl.pallas_call(probs_kernel, out_shape=jax.ShapeDtypeStruct((rows, lanes)...  1.48 us
  transfers between devices with their start and end apart: 10, of which 6 were waited for; matrix products, arithmetic and copies ran while one was open for 0% of the time, Pallas kernels for 4%

profile of v3, /device:TPU:0, one launch (start us, length us, event | category | flops | bytes accessed | tf_op | source)
XLA Modules:
  0.0 47.7 jit_solution(12334743997785951364)
XLA Ops:
  0.0 0.0 copy-start
  1.3 0.7 %constant_dynamic-slice_fusion.1 = (bf16[8,1024]{1,0:T(8,128)(2,1)S(1)}, bf16[8,1024]{1,0:T(8,128)(2,1)S(1)}) fusion(bf16[8,2048]{1,0:T(8,128)(2,1)} %param.8, s32[]{:T(128)S(6)} %select_n.55, s32[]{:T(128)S(6)} %select_n.56), kind=kLoop, calls=%fused_computation.27 | loop fusion | bytes 65544 | tf_op jit(solution)/shard_map/dynamic_slice | solution.py:252
  2.1 0.7 %collective-permute-start = (bf16[8,1152]{1,0:T(8,128)(2,1)S(1)}, bf16[8,1152]{1,0:T(8,128)(2,1)S(1)}, u32[]{:S(2)}, u32[]{:S(2)}) collective-permute-start(bf16[8,1152]{1,0:T(8,128)(2,1)S(1)} %concatenate.32.after_ref), channel_id=1, source_target_pairs={{1,9},{3,11},{5,13},{7,15},{9,1},{11,3},{13,5},{15,7},{17,25},{19,... | collective-permute-start | bytes 55304 | tf_op jit(solution)/shard_map/ppermute | solution.py:242
  2.8 0.0 copy-start.1
  2.8 1.6 %copy-done.1 = bf16[256,2,2048]{2,1,0:T(2,128)(2,1)S(1)} copy-done((bf16[256,2,2048]{2,1,0:T(2,128)(2,1)S(1)}, bf16[256,2,2048]{2,1,0:T(2,128)(2,1)}, u32[]{:S(2)}) %copy-start.1) | copy-done | bytes 2097176
  4.4 0.0 copy-start.2
  4.4 0.0 copy-start.6
  4.4 0.2 weight.2.w0_ref
  4.6 0.0 copy-start.3
  4.6 1.0 %copy-done.3 = bf16[512,1024]{1,0:T(8,128)(2,1)} copy-done((bf16[512,1024]{1,0:T(8,128)(2,1)}, bf16[512,1024]{1,0:T(8,128)(2,1)S(1)}, u32[]{:S(2)}) %copy-start.3) | copy-done | bytes 1048600
  5.6 0.0 collective-permute-done
  5.6 0.7 %collective-permute-start.1 = (bf16[16,640]{1,0:T(8,128)(2,1)S(1)}, bf16[16,640]{1,0:T(8,128)(2,1)S(1)}, u32[]{:S(2)}, u32[]{:S(2)}) collective-permute-start(bf16[16,640]{1,0:T(8,128)(2,1)S(1)} %fusion.1.after_ref), channel_id=1, source_target_pairs={{1,5},{3,7},{5,1},{7,3},{9,13},{11,15},{13,9},{15,11},{17,21},{19,... | collective-permute-start | bytes 61448 | tf_op jit(solution)/shard_map/ppermute | solution.py:242
  6.3 0.1 copy-done.2
  6.3 0.2 weight.3.w1_ref
  6.6 0.0 collective-permute-done.1
  6.6 0.7 %collective-permute-start.2 = (bf16[32,384]{1,0:T(8,128)(2,1)S(1)}, bf16[32,384]{1,0:T(8,128)(2,1)S(1)}, u32[]{:S(2)}, u32[]{:S(2)}) collective-permute-start(bf16[32,384]{1,0:T(8,128)(2,1)S(1)} %maximum_maximum_fusion.1), channel_id=1, source_target_pairs={{1,3},{3,1},{5,7},{7,5},{9,11},{11,9},{13,15},{15,13},{17,19},{19,... | collective-permute-start | bytes 73736 | tf_op jit(solution)/shard_map/ppermute | solution.py:242
  7.3 0.0 collective-permute-done.2
  7.3 1.3 %collective-permute-start.3 = (bf16[64,384]{1,0:T(8,128)(2,1)S(1)}, bf16[64,384]{1,0:T(8,128)(2,1)S(1)}, u32[]{:S(2)}, u32[]{:S(2)}) collective-permute-start(bf16[64,384]{1,0:T(8,128)(2,1)S(1)} %maximum_maximum_fusion), channel_id=1, source_target_pairs={{1,0},{3,2},{5,4},{7,6},{9,8},{11,10},{13,12},{15,14},{17,16},{19,... | collective-permute-start | bytes 147464 | tf_op jit(solution)/shard_map/ppermute | solution.py:262
  8.6 0.0 copy-done
  8.7 12.9 %collective-permute-done.3 = bf16[64,384]{1,0:T(8,128)(2,1)S(1)} collective-permute-done((bf16[64,384]{1,0:T(8,128)(2,1)S(1)}, bf16[64,384]{1,0:T(8,128)(2,1)S(1)}, u32[]{:S(2)}, u32[]{:S(2)}) %collective-permute-start.3) | collective-permute-done | bytes 49184 | tf_op jit(solution)/shard_map/ppermute | solution.py:262
  21.6 0.0 copy-done.6
  21.6 0.0 copy-start.4
  21.6 1.2 %copy-done.4 = bf16[512,1024]{1,0:T(8,128)(2,1)S(1)} copy-done((bf16[512,1024]{1,0:T(8,128)(2,1)S(1)}, bf16[512,1024]{1,0:T(8,128)(2,1)}, u32[]{:S(2)}) %copy-start.4) | copy-done | bytes 1048600
  22.8 1.5 %project.1 = (bf16[64,2048]{1,0:T(8,128)(2,1)S(1)}, f32[64,2048]{1,0:T(8,128)S(1)}, bf16[64,2048]{1,0:T(8,128)(2,1)S(1)}, f32[64,2048]{1,0:T(8,128)S(1)}, s32[8,128]{1,0:T(8,128)S(1)}) custom-call(s32[1]{0:T(128)} %bitcast.pos_ref, s32[8]{0:T(128)S(1)} %copy-done.6, bf16[16,256]{1,0:T(8,128)(2,1)S(1)} %constant_dynamic-slice_fusion.2.null_ref, ...), custom_call_target="tpu_custom_call" | custom-call | flops 268435456 | bytes 4194304 | tf_op jit(solution)/shard_map/project/pallas_call | solution.py:268
  24.4 0.0 copy-start.5
  24.4 1.6 %collective-permute-start.4 = (bf16[64,2048]{1,0:T(8,128)(2,1)S(1)}, bf16[64,2048]{1,0:T(8,128)(2,1)S(1)}, u32[]{:S(2)}, u32[]{:S(2)}) collective-permute-start(bf16[64,2048]{1,0:T(8,128)(2,1)S(1)} %get-tuple-element.20), channel_id=1, source_target_pairs={{0,2},{2,0},{4,6},{6,4},{8,10},{10,8},{12,14},{14,12},{1,3},{3,1},... | collective-permute-start | bytes 786440 | tf_op jit(solution)/shard_map/ppermute | solution.py:67
  25.9 1.6 %collective-permute-start.7 = (bf16[64,2048]{1,0:T(8,128)(2,1)S(1)}, bf16[64,2048]{1,0:T(8,128)(2,1)S(1)}, u32[]{:S(2)}, u32[]{:S(2)}) collective-permute-start(bf16[64,2048]{1,0:T(8,128)(2,1)S(1)} %get-tuple-element.22), channel_id=1, source_target_pairs={{0,4},{2,6},{4,0},{6,2},{8,12},{10,14},{12,8},{14,10},{1,5},{3,7},... | collective-permute-start | bytes 786440 | tf_op jit(solution)/shard_map/ppermute | solution.py:67
  27.5 5.3 %collective-permute-done.4 = bf16[64,2048]{1,0:T(8,128)(2,1)S(1)} collective-permute-done((bf16[64,2048]{1,0:T(8,128)(2,1)S(1)}, bf16[64,2048]{1,0:T(8,128)(2,1)S(1)}, u32[]{:S(2)}, u32[]{:S(2)}) %collective-permute-start.4) | collective-permute-done | bytes 262176 | tf_op jit(solution)/shard_map/ppermute | solution.py:67
  32.9 1.6 %collective-permute-start.5 = (bf16[32,2048]{1,0:T(8,128)(2,1)S(1)}, bf16[32,2048]{1,0:T(8,128)(2,1)S(1)}, u32[]{:S(2)}, u32[]{:S(2)}) collective-permute-start(bf16[32,2048]{1,0:T(8,128)(2,1)S(1)} %slice.81), channel_id=1, source_target_pairs={{0,4},{2,6},{4,0},{6,2},{8,12},{10,14},{12,8},{14,10},{1,5},{3,7},... | collective-permute-start | bytes 393224 | tf_op jit(solution)/shard_map/ppermute | solution.py:67
  34.5 0.0 collective-permute-done.7
  34.6 1.6 %collective-permute-start.8 = (bf16[32,2048]{1,0:T(8,128)(2,1)S(1)}, bf16[32,2048]{1,0:T(8,128)(2,1)S(1)}, u32[]{:S(2)}, u32[]{:S(2)}) collective-permute-start(bf16[32,2048]{1,0:T(8,128)(2,1)S(1)} %slice.80), channel_id=1, source_target_pairs={{0,2},{2,0},{4,6},{6,4},{8,10},{10,8},{12,14},{14,12},{1,3},{3,1},... | collective-permute-start | bytes 393224 | tf_op jit(solution)/shard_map/ppermute | solution.py:67
  36.2 1.8 %collective-permute-done.5 = bf16[32,2048]{1,0:T(8,128)(2,1)S(1)} collective-permute-done((bf16[32,2048]{1,0:T(8,128)(2,1)S(1)}, bf16[32,2048]{1,0:T(8,128)(2,1)S(1)}, u32[]{:S(2)}, u32[]{:S(2)}) %collective-permute-start.5) | collective-permute-done | bytes 131104 | tf_op jit(solution)/shard_map/ppermute | solution.py:67
  38.0 1.0 %collective-permute-start.6 = (bf16[16,2048]{1,0:T(8,128)(2,1)S(1)}, bf16[16,2048]{1,0:T(8,128)(2,1)S(1)}, u32[]{:S(2)}, u32[]{:S(2)}) collective-permute-start(bf16[16,2048]{1,0:T(8,128)(2,1)S(1)} %slice.83), channel_id=1, source_target_pairs={{0,8},{2,10},{4,12},{6,14},{8,0},{10,2},{12,4},{14,6},{1,9},{3,11}... | collective-permute-start | bytes 196616 | tf_op jit(solution)/shard_map/ppermute | solution.py:67
  39.0 0.7 %collective-permute-done.8 = bf16[32,2048]{1,0:T(8,128)(2,1)S(1)} collective-permute-done((bf16[32,2048]{1,0:T(8,128)(2,1)S(1)}, bf16[32,2048]{1,0:T(8,128)(2,1)S(1)}, u32[]{:S(2)}, u32[]{:S(2)}) %collective-permute-start.8) | collective-permute-done | bytes 131104 | tf_op jit(solution)/shard_map/ppermute | solution.py:67
  39.7 1.4 %collective-permute-start.9 = (bf16[16,2048]{1,0:T(8,128)(2,1)S(1)}, bf16[16,2048]{1,0:T(8,128)(2,1)S(1)}, u32[]{:S(2)}, u32[]{:S(2)}) collective-permute-start(bf16[16,2048]{1,0:T(8,128)(2,1)S(1)} %slice.82), channel_id=1, source_target_pairs={{0,8},{2,10},{4,12},{6,14},{8,0},{10,2},{12,4},{14,6},{1,9},{3,11}... | collective-permute-start | bytes 196616 | tf_op jit(solution)/shard_map/ppermute | solution.py:67
  41.1 2.5 %collective-permute-done.6.got_ref = bf16[16,2048]{1,0:T(8,128)(2,1)S(1)} collective-permute-done((bf16[16,2048]{1,0:T(8,128)(2,1)S(1)}, bf16[16,2048]{1,0:T(8,128)(2,1)S(1)}, u32[]{:S(2)}, u32[]{:S(2)}) %collective-permute-start.6) | collective-permute-done | bytes 65568 | tf_op jit(solution)/shard_map/ppermute | solution.py:67
  43.6 0.0 copy-done.5
  43.6 1.5 %probs.1.p_ref = bf16[768,256]{1,0:T(8,128)(2,1)S(1)} custom-call(s32[8,128]{1,0:T(8,128)S(1)} %get-tuple-element.18.count_ref, bf16[768,2048]{1,0:T(8,128)(2,1)S(1)} %copy-done.5, f32[16,2048]{1,0:T(8,128)S(1)} %slice.68.kept_ref, bf16[16,2048]{1,0:T(8,128)(2,1)S(1)} %collective-permute-done.6.got_ref), custom_call_target="tpu_custom_call" | custom-call | flops 805306368 | bytes 3145728 | tf_op jit(solution)/shard_map/probs/pallas_call | solution.py:293
  45.1 0.6 %collective-permute-done.9.got_ref = bf16[16,2048]{1,0:T(8,128)(2,1)S(1)} collective-permute-done((bf16[16,2048]{1,0:T(8,128)(2,1)S(1)}, bf16[16,2048]{1,0:T(8,128)(2,1)S(1)}, u32[]{:S(2)}, u32[]{:S(2)}) %collective-permute-start.9) | collective-permute-done | bytes 65568 | tf_op jit(solution)/shard_map/ppermute | solution.py:67
  45.7 2.0 %context.1 = bf16[768,2048]{1,0:T(8,128)(2,1)} custom-call(bf16[768,256]{1,0:T(8,128)(2,1)S(1)} %probs.1.p_ref, f32[16,2048]{1,0:T(8,128)S(1)} %slice.72.kept_ref, bf16[16,2048]{1,0:T(8,128)(2,1)S(1)} %collective-permute-done.9.got_ref), custom_call_target="tpu_custom_call" | custom-call | flops 805306368 | bytes 3145728 | tf_op jit(solution)/shard_map/context/pallas_call | solution.py:305
  (25 shorter events, 0.3 us)
Async XLA Ops:
  0.0 8.7 %copy-start = (bf16[16,2048]{1,0:T(8,128)(2,1)S(1)}, bf16[16,2048]{1,0:T(8,128)(2,1)}, u32[]{:S(2)}) copy-start(bf16[16,2048]{1,0:T(8,128)(2,1)} %param.9) | copy-start | bytes 196612
  2.1 3.5 %collective-permute-start = (bf16[8,1152]{1,0:T(8,128)(2,1)S(1)}, bf16[8,1152]{1,0:T(8,128)(2,1)S(1)}, u32[]{:S(2)}, u32[]{:S(2)}) collective-permute-start(bf16[8,1152]{1,0:T(8,128)(2,1)S(1)} %concatenate.32.after_ref), channel_id=1, source_target_pairs={{1,9},{3,11},{5,13},{7,15},{9,1},{11,3},{13,5},{15,7},{17,25},{19,... | collective-permute-start | bytes 55304 | tf_op jit(solution)/shard_map/ppermute | solution.py:242
  2.8 1.6 %copy-start.1 = (bf16[256,2,2048]{2,1,0:T(2,128)(2,1)S(1)}, bf16[256,2,2048]{2,1,0:T(2,128)(2,1)}, u32[]{:S(2)}) copy-start(bf16[256,2,2048]{2,1,0:T(2,128)(2,1)} %w_ref.3) | copy-start | bytes 6291460
  4.4 2.0 %copy-start.2 = (bf16[256,2,2048]{2,1,0:T(2,128)(2,1)S(1)}, bf16[256,2,2048]{2,1,0:T(2,128)(2,1)}, u32[]{:S(2)}) copy-start(bf16[256,2,2048]{2,1,0:T(2,128)(2,1)} %w_ref.3) | copy-start | bytes 6291460
  4.4 17.2 %copy-start.6 = (s32[8]{0:T(128)S(1)}, s32[8]{0:T(128)}, u32[]{:S(2)}) copy-start(s32[8]{0:T(128)} %len_ref.1) | copy-start | bytes 100
  4.6 1.0 %copy-start.3 = (bf16[512,1024]{1,0:T(8,128)(2,1)}, bf16[512,1024]{1,0:T(8,128)(2,1)S(1)}, u32[]{:S(2)}) copy-start(bf16[512,1024]{1,0:T(8,128)(2,1)S(1)} %weight.2.w0_ref) | copy-start | bytes 3145732
  5.6 1.0 %collective-permute-start.1 = (bf16[16,640]{1,0:T(8,128)(2,1)S(1)}, bf16[16,640]{1,0:T(8,128)(2,1)S(1)}, u32[]{:S(2)}, u32[]{:S(2)}) collective-permute-start(bf16[16,640]{1,0:T(8,128)(2,1)S(1)} %fusion.1.after_ref), channel_id=1, source_target_pairs={{1,5},{3,7},{5,1},{7,3},{9,13},{11,15},{13,9},{15,11},{17,21},{19,... | collective-permute-start | bytes 61448 | tf_op jit(solution)/shard_map/ppermute | solution.py:242
  6.6 0.7 %collective-permute-start.2 = (bf16[32,384]{1,0:T(8,128)(2,1)S(1)}, bf16[32,384]{1,0:T(8,128)(2,1)S(1)}, u32[]{:S(2)}, u32[]{:S(2)}) collective-permute-start(bf16[32,384]{1,0:T(8,128)(2,1)S(1)} %maximum_maximum_fusion.1), channel_id=1, source_target_pairs={{1,3},{3,1},{5,7},{7,5},{9,11},{11,9},{13,15},{15,13},{17,19},{19,... | collective-permute-start | bytes 73736 | tf_op jit(solution)/shard_map/ppermute | solution.py:242
  7.3 14.2 %collective-permute-start.3 = (bf16[64,384]{1,0:T(8,128)(2,1)S(1)}, bf16[64,384]{1,0:T(8,128)(2,1)S(1)}, u32[]{:S(2)}, u32[]{:S(2)}) collective-permute-start(bf16[64,384]{1,0:T(8,128)(2,1)S(1)} %maximum_maximum_fusion), channel_id=1, source_target_pairs={{1,0},{3,2},{5,4},{7,6},{9,8},{11,10},{13,12},{15,14},{17,16},{19,... | collective-permute-start | bytes 147464 | tf_op jit(solution)/shard_map/ppermute | solution.py:262
  21.6 1.2 %copy-start.4 = (bf16[512,1024]{1,0:T(8,128)(2,1)S(1)}, bf16[512,1024]{1,0:T(8,128)(2,1)}, u32[]{:S(2)}) copy-start(bf16[512,1024]{1,0:T(8,128)(2,1)} %copy-done.3) | copy-start | bytes 3145732
  24.4 19.2 %copy-start.5 = (bf16[768,2048]{1,0:T(8,128)(2,1)S(1)}, bf16[768,2048]{1,0:T(8,128)(2,1)}, u32[]{:S(2)}) copy-start(bf16[768,2048]{1,0:T(8,128)(2,1)} %q_ref.1) | copy-start | bytes 9437188
  24.4 8.4 %collective-permute-start.4 = (bf16[64,2048]{1,0:T(8,128)(2,1)S(1)}, bf16[64,2048]{1,0:T(8,128)(2,1)S(1)}, u32[]{:S(2)}, u32[]{:S(2)}) collective-permute-start(bf16[64,2048]{1,0:T(8,128)(2,1)S(1)} %get-tuple-element.20), channel_id=1, source_target_pairs={{0,2},{2,0},{4,6},{6,4},{8,10},{10,8},{12,14},{14,12},{1,3},{3,1},... | collective-permute-start | bytes 786440 | tf_op jit(solution)/shard_map/ppermute | solution.py:67
  25.9 8.6 %collective-permute-start.7 = (bf16[64,2048]{1,0:T(8,128)(2,1)S(1)}, bf16[64,2048]{1,0:T(8,128)(2,1)S(1)}, u32[]{:S(2)}, u32[]{:S(2)}) collective-permute-start(bf16[64,2048]{1,0:T(8,128)(2,1)S(1)} %get-tuple-element.22), channel_id=1, source_target_pairs={{0,4},{2,6},{4,0},{6,2},{8,12},{10,14},{12,8},{14,10},{1,5},{3,7},... | collective-permute-start | bytes 786440 | tf_op jit(solution)/shard_map/ppermute | solution.py:67
  32.9 5.0 %collective-permute-start.5 = (bf16[32,2048]{1,0:T(8,128)(2,1)S(1)}, bf16[32,2048]{1,0:T(8,128)(2,1)S(1)}, u32[]{:S(2)}, u32[]{:S(2)}) collective-permute-start(bf16[32,2048]{1,0:T(8,128)(2,1)S(1)} %slice.81), channel_id=1, source_target_pairs={{0,4},{2,6},{4,0},{6,2},{8,12},{10,14},{12,8},{14,10},{1,5},{3,7},... | collective-permute-start | bytes 393224 | tf_op jit(solution)/shard_map/ppermute | solution.py:67
  34.6 5.0 %collective-permute-start.8 = (bf16[32,2048]{1,0:T(8,128)(2,1)S(1)}, bf16[32,2048]{1,0:T(8,128)(2,1)S(1)}, u32[]{:S(2)}, u32[]{:S(2)}) collective-permute-start(bf16[32,2048]{1,0:T(8,128)(2,1)S(1)} %slice.80), channel_id=1, source_target_pairs={{0,2},{2,0},{4,6},{6,4},{8,10},{10,8},{12,14},{14,12},{1,3},{3,1},... | collective-permute-start | bytes 393224 | tf_op jit(solution)/shard_map/ppermute | solution.py:67
  38.0 5.6 %collective-permute-start.6 = (bf16[16,2048]{1,0:T(8,128)(2,1)S(1)}, bf16[16,2048]{1,0:T(8,128)(2,1)S(1)}, u32[]{:S(2)}, u32[]{:S(2)}) collective-permute-start(bf16[16,2048]{1,0:T(8,128)(2,1)S(1)} %slice.83), channel_id=1, source_target_pairs={{0,8},{2,10},{4,12},{6,14},{8,0},{10,2},{12,4},{14,6},{1,9},{3,11}... | collective-permute-start | bytes 196616 | tf_op jit(solution)/shard_map/ppermute | solution.py:67
  39.7 6.0 %collective-permute-start.9 = (bf16[16,2048]{1,0:T(8,128)(2,1)S(1)}, bf16[16,2048]{1,0:T(8,128)(2,1)S(1)}, u32[]{:S(2)}, u32[]{:S(2)}) collective-permute-start(bf16[16,2048]{1,0:T(8,128)(2,1)S(1)} %slice.82), channel_id=1, source_target_pairs={{0,8},{2,10},{4,12},{6,14},{8,0},{10,2},{12,4},{14,6},{1,9},{3,11}... | collective-permute-start | bytes 196616 | tf_op jit(solution)/shard_map/ppermute | solution.py:67

commit v4 on v1

--- a/solution.py
+++ b/solution.py
@@ -10,7 +10,7 @@
 HDIM = 128
 NULL_LEN = 16
 SCALE = HDIM ** (-0.5)
-VMEM_LIMIT = 48 * 1024 * 1024
+VMEM_LIMIT = 16 * 1024 * 1024
 NEG = -1e30
 
 
@@ -67,69 +67,88 @@
     return lax.ppermute(x, "seq", [(i, i ^ mask) for i in range(n)])
 
 
-def project_kernel(order, pos_ref, len_ref, null_ref, w_ref, pack_ref, send_k, keep_k, send_v, keep_v):
-    n = len(order)
-    pos = pos_ref[0]
-    text_dev = pack_ref.shape[1] // 2
-    rows = n * NULL_LEN
-    packs = [pack_ref[jnp.bitwise_xor(pos, m)] for m in order]
-    pack = jnp.concatenate(packs, axis=0)
-    code = jnp.concatenate(
-        [p.astype(jnp.float32)[text_dev:, :128] for p in packs for _ in range(2)], axis=0
-    ).astype(jnp.int32)
+def keys_kernel(pos_ref, len_ref, null_ref, w_ref, rows_ref, send_ref, keep_ref, sel_ref, count_ref):
+    features = null_ref.shape[1]
+    rows = sel_ref.shape[0]
+    total = rows_ref.shape[0]
+    text_dev = total * NULL_LEN // rows
     reqs = len_ref.shape[0]
+    held = rows_ref[...]
+    held = jnp.concatenate([held, jnp.zeros((rows - total, held.shape[1]), held.dtype)], axis=0)
+    row = lax.broadcasted_iota(jnp.int32, (rows, rows), 0)
+    col = lax.broadcasted_iota(jnp.int32, (rows, rows), 1)
+    slot = row // NULL_LEN
+    flip = 7 - ((slot % 2) * 4 + (slot // 2 % 2) * 2 + slot // 4)
+    first = jnp.bitwise_xor(flip, pos_ref[0]) * text_dev
+
+    def take(which, columns):
+        which = which.astype(jnp.float32).astype(jnp.bfloat16)
+        return jnp.dot(which, columns, preferred_element_type=jnp.float32)
+
+    code = take(col == first, held[:, features:]).astype(jnp.int32)
     uncond = code >= reqs
     owner = jnp.where(uncond, code - reqs, code)
     start = jnp.zeros_like(owner)
+    length = jnp.zeros_like(owner)
     running = jnp.int32(0)
     for r in range(reqs):
         start = jnp.where(owner == r, running, start)
+        length = jnp.where(owner == r, len_ref[r], length)
         running = running + len_ref[r]
-    wanted = start + lax.broadcasted_iota(jnp.int32, (rows, 128), 0) % NULL_LEN
-    col = lax.broadcasted_iota(jnp.int32, (rows, 128), 1)
-    held = jnp.full((rows, 128), -1, jnp.int32)
-    for slot, m in enumerate(order):
-        first = slot * 2 * text_dev
-        base = jnp.bitwise_xor(pos, m) * text_dev - first
-        held = jnp.where((col >= first) & (col < first + text_dev), col + base, held)
-    pick = (held == wanted).astype(jnp.float32).astype(jnp.bfloat16)
-    text_sel = jnp.dot(pick, pack, preferred_element_type=jnp.float32)
-    null_sel = jnp.concatenate([null_ref[...].astype(jnp.float32)] * n, axis=0)
-    wide = jnp.concatenate([uncond] * (null_sel.shape[1] // 128), axis=1)
+    own = rows - NULL_LEN
+    count_ref[...] = jnp.where(uncond, NULL_LEN, length)[own : own + 8]
+    text_sel = take(col == start + row % NULL_LEN, held[:, :features])
+    null_sel = jnp.concatenate([null_ref[...].astype(jnp.float32)] * (rows // NULL_LEN), axis=0)
+    wide = jnp.concatenate([uncond] * (features // rows), axis=1)
     sel = jnp.where(wide, null_sel, text_sel).astype(jnp.bfloat16)
+    sel_ref[...] = sel
     half = rows // 2
-    width = send_k.shape[1]
-    for kind, (send, keep) in enumerate(((send_k, keep_k), (send_v, keep_v))):
-        for c in range(0, width, 512):
-            part = jnp.dot(
-                sel,
-                w_ref[:, kind * width + c : kind * width + c + 512],
-                preferred_element_type=jnp.float32,
-            )
-            send[:, c : c + 512] = part[:half].astype(jnp.bfloat16)
-            keep[:, c : c + 512] = part[half:]
-
-
-def spread_heads(kept_ref, got_ref, wide_ref):
-    total = kept_ref[...] + got_ref[...].astype(jnp.float32)
+    width = send_ref.shape[1]
+    for c in range(0, width, 512):
+        cols = slice(c, c + 512)
+        part = jnp.dot(sel, w_ref[:, cols], preferred_element_type=jnp.float32)
+        send_ref[:, cols] = part[:half].astype(jnp.bfloat16)
+        keep_ref[:, cols] = part[half:]
+
+
+def values_kernel(sel_ref, w_ref, send_ref, keep_ref):
+    quarter = sel_ref.shape[0] // 4
+    width = send_ref.shape[1]
+    for c in range(0, width, 512):
+        cols = slice(c, c + 512)
+        part = jnp.dot(
+            sel_ref[...], w_ref[:, width + c : width + c + 512], preferred_element_type=jnp.float32
+        )
+        send_ref[:quarter, cols] = part[:quarter].astype(jnp.bfloat16)
+        send_ref[quarter:, cols] = part[2 * quarter : 3 * quarter].astype(jnp.bfloat16)
+        keep_ref[:quarter, cols] = part[quarter : 2 * quarter]
+        keep_ref[quarter:, cols] = part[3 * quarter :]
+
+
+def spread_heads(kept_ref, got_ref, cols):
+    heads = kept_ref.shape[1] // HDIM
+    total = kept_ref[:, cols] + got_ref[:, cols].astype(jnp.float32)
     keys, width = total.shape
-    heads = width // HDIM
     total = total.astype(jnp.bfloat16).astype(jnp.float32)
     head = lax.broadcasted_iota(jnp.int32, (heads, width), 0)
-    col = lax.broadcasted_iota(jnp.int32, (heads, width), 1)
+    col = lax.broadcasted_iota(jnp.int32, (heads, width), 1) + cols.start
     mine = (col // HDIM) == head
-    for key in range(keys):
-        block = jnp.where(mine, jnp.broadcast_to(total[key : key + 1], (heads, width)), 0.0)
-        wide_ref[key * heads : (key + 1) * heads] = block.astype(jnp.bfloat16)
-
-
-def probs_kernel(len_ref, own_ref, flag_ref, q_ref, kept_ref, got_ref, out_ref, wide_ref):
+    blocks = [
+        jnp.where(mine, jnp.broadcast_to(total[key : key + 1], (heads, width)), 0.0).astype(
+            jnp.bfloat16
+        )
+        for key in range(keys)
+    ]
+    return jnp.concatenate(blocks, axis=0)
+
+
+def probs_kernel(count_ref, q_ref, kept_ref, got_ref, out_ref, wide_ref):
     heads = q_ref.shape[1] // HDIM
-    spread_heads(kept_ref, got_ref, wide_ref)
-    count = jnp.int32(0)
-    for r in range(len_ref.shape[0]):
-        count = jnp.where(own_ref[0] == r, len_ref[r], count)
-    count = jnp.where(flag_ref[0] == 1, NULL_LEN, count)
+    width = q_ref.shape[1]
+    for c in range(0, width, 512):
+        cols = slice(c, c + 512)
+        wide_ref[:, cols] = spread_heads(kept_ref, got_ref, cols)
+    count = jnp.broadcast_to(jnp.concatenate([count_ref[:1]] * (out_ref.shape[1] // 128), axis=1), (256, out_ref.shape[1]))
     block = 256
     for first in range(0, q_ref.shape[0], block):
         scores = lax.dot_general(
@@ -158,16 +177,18 @@
         ).astype(jnp.bfloat16)
 
 
-def context_kernel(p_ref, kept_ref, got_ref, out_ref, wide_ref):
-    @pl.when(pl.program_id(0) == 0)
-    def _():
-        spread_heads(kept_ref, got_ref, wide_ref)
-
-    block = out_ref.shape[0]
-    first = pl.multiple_of(pl.program_id(0) * block, block)
-    out_ref[...] = jnp.dot(
-        p_ref[pl.ds(first, block)], wide_ref[...], preferred_element_type=jnp.float32
-    ).astype(jnp.bfloat16)
+def context_kernel(p_ref, kept_ref, got_ref, out_hbm, out_ref, sems):
+    chunk = out_ref.shape[1] // sems.shape[0]
+    copies = []
+    for i in range(sems.shape[0]):
+        cols = slice(i * chunk, (i + 1) * chunk)
+        out_ref[:, cols] = jnp.dot(
+            p_ref[...], spread_heads(kept_ref, got_ref, cols), preferred_element_type=jnp.float32
+        ).astype(jnp.bfloat16)
+        copies.append(pltpu.make_async_copy(out_ref.at[:, cols], out_hbm.at[:, cols], sems.at[i]))
+        copies[-1].start()
+    for copy in copies:
+        copy.wait()
 
 
 def select_plan(n, queries, text_rows, null_rows, kv_weight, prompt_lengths, block_owner, uncond_flags):
@@ -177,48 +198,65 @@
     reqs = prompt_lengths.shape[0]
     heads = width // HDIM
     pos = lax.axis_index("seq").astype(jnp.int32)
+    smem = pl.BlockSpec(memory_space=pltpu.SMEM)
+    vmem = pl.BlockSpec(memory_space=pltpu.VMEM)
+    anywhere = pl.BlockSpec(memory_space=pl.ANY)
+    params = pltpu.CompilerParams(vmem_limit_bytes=VMEM_LIMIT)
+    text_dev = text_rows.shape[0]
     code = (block_owner[0] + reqs * uncond_flags[0]).astype(jnp.bfloat16)
-    packed = jnp.concatenate([text_rows, jnp.full(text_rows.shape, code, jnp.bfloat16)], axis=0)
-    packed = packed.reshape(-1, n, features).transpose(1, 0, 2)
-    packs = lax.all_to_all(packed, "seq", split_axis=0, concat_axis=0, tiled=True)
+    text = text_rows.reshape(text_dev, n, features).transpose(1, 0, 2)
+    packed = jnp.concatenate([text, jnp.full((n, text_dev, 128), code, jnp.bfloat16)], axis=2)
+    held = lax.all_to_all(packed, "seq", split_axis=0, concat_axis=0, tiled=True)
+    held = held.reshape(n * text_dev, features + 128)
     null_cols = lax.dynamic_slice_in_dim(null_rows, pos * features, features, 1)
-    flat_weight = kv_weight.reshape(features, 2 * width)
-    order = [7, 3, 5, 1, 6, 2, 4, 0]
+    weight = kv_weight.reshape(features, 2 * width)
     half = n * NULL_LEN // 2
     sent = jax.ShapeDtypeStruct((half, width), jnp.bfloat16)
     kept = jax.ShapeDtypeStruct((half, width), jnp.float32)
-    smem = pl.BlockSpec(memory_space=pltpu.SMEM)
-    vmem = pl.BlockSpec(memory_space=pltpu.VMEM)
-    params = pltpu.CompilerParams(vmem_limit_bytes=VMEM_LIMIT)
-    send_k, keep_k, send_v, keep_v = pl.pallas_call(
-        functools.partial(project_kernel, order),
-        out_shape=[sent, kept] * 2,
-        in_specs=[smem, smem, vmem, vmem, vmem],
+    estimate = pl.CostEstimate(
+        flops=2 * 2 * half * features * width,
+        bytes_accessed=2 * features * width,
+        transcendentals=0,
+    )
+    send_k, keep_k, sel, count = pl.pallas_call(
+        keys_kernel,
+        out_shape=[
+            sent,
+            kept,
+            jax.ShapeDtypeStruct((2 * half, features), jnp.bfloat16),
+            jax.ShapeDtypeStruct((8, 128), jnp.int32),
+        ],
+        in_specs=[smem, smem] + [vmem] * 3,
         out_specs=[vmem] * 4,
         compiler_params=params,
-        cost_estimate=pl.CostEstimate(
-            flops=2 * 2 * half * features * 2 * width,
-            bytes_accessed=8 * features * width,
-            transcendentals=0,
-        ),
-        name="project",
-    )(pos.reshape(1), prompt_lengths, null_cols, flat_weight, packs)
-
-    def reduce_parts(send, keep):
-        for mask in (1, 2):
+        cost_estimate=estimate,
+        name="keys",
+    )(pos.reshape(1), prompt_lengths, null_cols, weight, held)
+    send_v, keep_v = pl.pallas_call(
+        values_kernel,
+        out_shape=[sent, kept],
+        in_specs=[vmem] * 2,
+        out_specs=[vmem] * 2,
+        compiler_params=params,
+        cost_estimate=estimate,
+        name="values",
+    )(sel, weight)
+
+    def reduce_parts(send, keep, masks):
+        for mask in masks:
             total = keep + swap(send, n, mask).astype(jnp.float32)
             cut = total.shape[0] // 2
             send, keep = total[:cut].astype(jnp.bfloat16), total[cut:]
         return keep, swap(send, n, 4)
 
-    k_parts = reduce_parts(send_k, keep_k)
-    v_parts = reduce_parts(send_v, keep_v)
+    k_parts = reduce_parts(send_k, keep_k, (1, 2))
+    v_parts = reduce_parts(send_v, keep_v, (2, 1))
 
     lanes = heads * NULL_LEN
     probs = pl.pallas_call(
         probs_kernel,
         out_shape=jax.ShapeDtypeStruct((rows, lanes), jnp.bfloat16),
-        in_specs=[smem] * 3 + [vmem] * 3,
+        in_specs=[vmem] * 4,
         out_specs=vmem,
         scratch_shapes=[pltpu.VMEM((lanes, width), jnp.bfloat16)],
         compiler_params=params,
@@ -226,15 +264,16 @@
             flops=2 * rows * width * lanes, bytes_accessed=2 * rows * width, transcendentals=rows * lanes
         ),
         name="probs",
-    )(prompt_lengths, block_owner, uncond_flags, queries, *k_parts)
-    block = 256
+    )(count, queries, *k_parts)
     return pl.pallas_call(
         context_kernel,
         out_shape=jax.ShapeDtypeStruct((rows, width), jnp.bfloat16),
-        grid=(rows // block,),
         in_specs=[vmem] * 3,
-        out_specs=pl.BlockSpec((block, width), lambda i: (i, 0)),
-        scratch_shapes=[pltpu.VMEM((lanes, width), jnp.bfloat16)],
+        out_specs=anywhere,
+        scratch_shapes=[
+            pltpu.VMEM((rows, width), jnp.bfloat16),
+            pltpu.SemaphoreType.DMA((4,)),
+        ],
         compiler_params=params,
         cost_estimate=pl.CostEstimate(
             flops=2 * rows * width * lanes, bytes_accessed=2 * rows * width, transcendentals=0

time: 44.9 us -> 39.7 us (0.88)
  waiting for transfers between devices: 20.9 us -> 14.7 us
  starting transfers between devices: 11.9 us -> 14.1 us
  Pallas kernels: 6.11 us -> 4.96 us
    ppermute x6, waiting for transfers between devices: 16.5 us -> 10.4 us  [swap(): return lax.ppermute(x, 'seq', [(i, i ^ mask) for i in range(n)])]
    ppermute x6, starting transfers between devices: 4.63 us -> 6.84 us  [swap(): return lax.ppermute(x, 'seq', [(i, i ^ mask) for i in range(n)])]
    pallas_call x1, Pallas kernels: 2.99 us -> 2.07 us  [select_plan(): pl.pallas_call(context_kernel, out_shape=jax.ShapeDtypeStruct((rows, widt...]
    reshape x1 -> x0, local copies, waits for them, and re-layouts: 0.64 us -> none  [select_plan(): packed = packed.reshape(-1, n, features).transpose(1, 0, 2)]
    concatenate x1, local copies, waits for them, and re-layouts: 0.77 us -> 1.38 us  [select_plan(): jnp.concatenate([text, jnp.full((n, text_dev, 128), code, jnp.bfloat16)],...]
    pallas_call x1, Pallas kernels: 2.02 us -> 1.49 us  [select_plan(): pl.pallas_call(probs_kernel, out_shape=jax.ShapeDtypeStruct((rows, lanes)...]
    pallas_call x1 -> x2, Pallas kernels: 1.1 us -> 1.41 us  [the longest x1 1.1 us: select_plan(): pl.pallas_call(keys_kernel, out_shape=[sent, kept, jax.ShapeDtypeStruct((...]
  transfers between devices with their start and end apart: 7 -> 7, of which waited for: 6 -> 7; matrix products, arithmetic and copies ran while one was open for 6% -> 7% of each run, Pallas kernels for 5% -> 5%
where the time goes in v4:
time: 39.7 us; the launch traced here: 39.3 us
  waiting for transfers between devices  14.7 us (37%)
  starting transfers between devices  14.1 us (36%)
  Pallas kernels  4.96 us (12%)
  local copies, waits for them, and re-layouts  3.96 us (10%)
  between operations  1.45 us (4%)
    ppermute x6, waiting for transfers between devices, swap(): return lax.ppermute(x, 'seq', [(i, i ^ mask) for i in range(n)])  10.4 us
    all_to_all x1, starting transfers between devices, select_plan(): lax.all_to_all(packed, 'seq', split_axis=0, concat_axis=0, tiled=True)  7.25 us
    ppermute x6, starting transfers between devices, swap(): return lax.ppermute(x, 'seq', [(i, i ^ mask) for i in range(n)])  6.84 us
    all_to_all x1, waiting for transfers between devices, select_plan(): lax.all_to_all(packed, 'seq', split_axis=0, concat_axis=0, tiled=True)  4.28 us
    unnamed x7, local copies, waits for them, and re-layouts  2.5 us
    pallas_call x1, Pallas kernels, select_plan(): pl.pallas_call(context_kernel, out_shape=jax.ShapeDtypeStruct((rows, widt...  2.07 us
    pallas_call x1, Pallas kernels, select_plan(): pl.pallas_call(probs_kernel, out_shape=jax.ShapeDtypeStruct((rows, lanes)...  1.49 us
    concatenate x1, local copies, waits for them, and re-layouts, select_plan(): jnp.concatenate([text, jnp.full((n, text_dev, 128), code, jnp.bfloat16)],...  1.38 us
  transfers between devices with their start and end apart: 7, of which 7 were waited for; matrix products, arithmetic and copies ran while one was open for 7% of the time, Pallas kernels for 5%

profile of v4, /device:TPU:0, one launch (start us, length us, event | category | flops | bytes accessed | tf_op | source)
XLA Modules:
  0.0 39.3 jit_solution(16992401742168767954)
XLA Ops:
  0.0 0.0 copy-start
  0.0 0.0 copy-start.2
  1.3 1.4 %concatenate.3 = bf16[8,8,384]{2,1,0:T(8,128)(2,1)} pad(bf16[8,8,256]{2,1,0:T(8,128)(2,1)} %bitcast.12, bf16[]{:T(256)} %bitcast.3), padding=0_0x0_0x0_128 | pad | bytes 81922 | tf_op jit(solution)/shard_map/concatenate | solution.py:208
  2.7 7.3 %all-to-all-start = ((bf16[8,8,384]{2,1,0:T(8,128)(2,1)}), bf16[8,8,384]{2,1,0:T(8,128)(2,1)S(1)}, u32[]{:S(2)}, u32[]{:S(2)}) async-start(bf16[8,8,384]{2,1,0:T(8,128)(2,1)} %concatenate.3), calls=%async_computation | async-start | bytes 98304 | tf_op jit(solution)/shard_map/all_to_all | solution.py:209
  10.0 2.5 %copy.8 = bf16[32,8,2,2048]{3,1,2,0:T(8,128)(2,1)S(1)} copy(bf16[32,8,2,2048]{3,2,1,0:T(2,128)(2,1)} %bitcast.11) | data formatting | bytes 4194304
  12.5 0.0 copy-done
  12.5 4.3 %all-to-all-done = bf16[8,8,384]{2,1,0:T(8,128)(2,1)S(1)} async-done(((bf16[8,8,384]{2,1,0:T(8,128)(2,1)}), bf16[8,8,384]{2,1,0:T(8,128)(2,1)S(1)}, u32[]{:S(2)}, u32[]{:S(2)}) %all-to-all-start) | async-done | bytes 49184 | tf_op jit(solution)/shard_map/all_to_all | solution.py:209
  16.8 0.0 copy-done.2
  16.8 1.1 %keys.1 = (bf16[64,2048]{1,0:T(8,128)(2,1)S(1)}, f32[64,2048]{1,0:T(8,128)S(1)}, bf16[128,256]{1,0:T(8,128)(2,1)S(1)}, s32[8,128]{1,0:T(8,128)S(1)}) custom-call(s32[1]{0:T(128)} %bitcast.pos_ref, s32[8]{0:T(128)S(1)} %copy-done.2, bf16[16,256]{1,0:T(8,128)(2,1)S(1)} %constant_dynamic-slice_fusion.null_ref, bf16[256,4096]{1,0:T(8,128)(2,1)S(1)} %bitcast.8, ...), custom_call_target="tpu_custom_call" | custom-call | flops 134217728 | bytes 1048576 | tf_op jit(solution)/shard_map/keys/pallas_call | solution.py:221
  17.9 0.5 %collective-permute-start = (bf16[64,2048]{1,0:T(8,128)(2,1)S(1)}, bf16[64,2048]{1,0:T(8,128)(2,1)S(1)}, u32[]{:S(2)}, u32[]{:S(2)}) collective-permute-start(bf16[64,2048]{1,0:T(8,128)(2,1)S(1)} %get-tuple-element.13), channel_id=1, source_target_pairs={{0,2},{2,0},{4,6},{6,4},{8,10},{10,8},{12,14},{14,12},{1,3},{3,1},... | collective-permute-start | bytes 786440 | tf_op jit(solution)/shard_map/ppermute | solution.py:67
  18.4 0.3 values.1
  18.7 0.0 copy-start.1
  18.7 0.8 %collective-permute-start.3 = (bf16[64,2048]{1,0:T(8,128)(2,1)S(1)}, bf16[64,2048]{1,0:T(8,128)(2,1)S(1)}, u32[]{:S(2)}, u32[]{:S(2)}) collective-permute-start(bf16[64,2048]{1,0:T(8,128)(2,1)S(1)} %get-tuple-element.16), channel_id=1, source_target_pairs={{0,4},{2,6},{4,0},{6,2},{8,12},{10,14},{12,8},{14,10},{1,5},{3,7},... | collective-permute-start | bytes 786440 | tf_op jit(solution)/shard_map/ppermute | solution.py:67
  19.5 5.0 %collective-permute-done = bf16[64,2048]{1,0:T(8,128)(2,1)S(1)} collective-permute-done((bf16[64,2048]{1,0:T(8,128)(2,1)S(1)}, bf16[64,2048]{1,0:T(8,128)(2,1)S(1)}, u32[]{:S(2)}, u32[]{:S(2)}) %collective-permute-start) | collective-permute-done | bytes 262176 | tf_op jit(solution)/shard_map/ppermute | solution.py:67
  24.6 0.4 collective-permute-start.1
  25.0 0.4 %collective-permute-done.3 = bf16[64,2048]{1,0:T(8,128)(2,1)S(1)} collective-permute-done((bf16[64,2048]{1,0:T(8,128)(2,1)S(1)}, bf16[64,2048]{1,0:T(8,128)(2,1)S(1)}, u32[]{:S(2)}, u32[]{:S(2)}) %collective-permute-start.3) | collective-permute-done | bytes 262176 | tf_op jit(solution)/shard_map/ppermute | solution.py:67
  25.5 2.8 %collective-permute-start.4 = (bf16[32,2048]{1,0:T(8,128)(2,1)S(1)}, bf16[32,2048]{1,0:T(8,128)(2,1)S(1)}, u32[]{:S(2)}, u32[]{:S(2)}) collective-permute-start(bf16[32,2048]{1,0:T(8,128)(2,1)S(1)} %slice.50), channel_id=1, source_target_pairs={{0,2},{2,0},{4,6},{6,4},{8,10},{10,8},{12,14},{14,12},{1,3},{3,1},... | collective-permute-start | bytes 393224 | tf_op jit(solution)/shard_map/ppermute | solution.py:67
  28.3 1.4 %collective-permute-done.1 = bf16[32,2048]{1,0:T(8,128)(2,1)S(1)} collective-permute-done((bf16[32,2048]{1,0:T(8,128)(2,1)S(1)}, bf16[32,2048]{1,0:T(8,128)(2,1)S(1)}, u32[]{:S(2)}, u32[]{:S(2)}) %collective-permute-start.1) | collective-permute-done | bytes 131104 | tf_op jit(solution)/shard_map/ppermute | solution.py:67
  29.7 0.8 %collective-permute-start.2 = (bf16[16,2048]{1,0:T(8,128)(2,1)S(1)}, bf16[16,2048]{1,0:T(8,128)(2,1)S(1)}, u32[]{:S(2)}, u32[]{:S(2)}) collective-permute-start(bf16[16,2048]{1,0:T(8,128)(2,1)S(1)} %slice.53), channel_id=1, source_target_pairs={{0,8},{2,10},{4,12},{6,14},{8,0},{10,2},{12,4},{14,6},{1,9},{3,11}... | collective-permute-start | bytes 196616 | tf_op jit(solution)/shard_map/ppermute | solution.py:67
  30.6 0.7 %collective-permute-done.4 = bf16[32,2048]{1,0:T(8,128)(2,1)S(1)} collective-permute-done((bf16[32,2048]{1,0:T(8,128)(2,1)S(1)}, bf16[32,2048]{1,0:T(8,128)(2,1)S(1)}, u32[]{:S(2)}, u32[]{:S(2)}) %collective-permute-start.4) | collective-permute-done | bytes 131104 | tf_op jit(solution)/shard_map/ppermute | solution.py:67
  31.3 1.5 %collective-permute-start.5 = (bf16[16,2048]{1,0:T(8,128)(2,1)S(1)}, bf16[16,2048]{1,0:T(8,128)(2,1)S(1)}, u32[]{:S(2)}, u32[]{:S(2)}) collective-permute-start(bf16[16,2048]{1,0:T(8,128)(2,1)S(1)} %slice.52), channel_id=1, source_target_pairs={{0,8},{2,10},{4,12},{6,14},{8,0},{10,2},{12,4},{14,6},{1,9},{3,11}... | collective-permute-start | bytes 196616 | tf_op jit(solution)/shard_map/ppermute | solution.py:67
  32.9 2.6 %collective-permute-done.2.got_ref = bf16[16,2048]{1,0:T(8,128)(2,1)S(1)} collective-permute-done((bf16[16,2048]{1,0:T(8,128)(2,1)S(1)}, bf16[16,2048]{1,0:T(8,128)(2,1)S(1)}, u32[]{:S(2)}, u32[]{:S(2)}) %collective-permute-start.2) | collective-permute-done | bytes 65568 | tf_op jit(solution)/shard_map/ppermute | solution.py:67
  35.5 0.0 copy-done.1
  35.5 1.5 %probs.1.p_ref = bf16[768,256]{1,0:T(8,128)(2,1)S(1)} custom-call(s32[8,128]{1,0:T(8,128)S(1)} %get-tuple-element.11.count_ref, bf16[768,2048]{1,0:T(8,128)(2,1)S(1)} %copy-done.1, f32[16,2048]{1,0:T(8,128)S(1)} %slice.38.kept_ref, bf16[16,2048]{1,0:T(8,128)(2,1)S(1)} %collective-permute-done.2.got_ref), custom_call_target="tpu_custom_call" | custom-call | flops 805306368 | bytes 3145728 | tf_op jit(solution)/shard_map/probs/pallas_call | solution.py:256
  37.0 0.3 collective-permute-done.5.got_ref
  37.3 2.1 %context.1 = bf16[768,2048]{1,0:T(8,128)(2,1)} custom-call(bf16[768,256]{1,0:T(8,128)(2,1)S(1)} %probs.1.p_ref, f32[16,2048]{1,0:T(8,128)S(1)} %slice.42.kept_ref, bf16[16,2048]{1,0:T(8,128)(2,1)S(1)} %collective-permute-done.5.got_ref), custom_call_target="tpu_custom_call" | custom-call | flops 805306368 | bytes 3145728 | tf_op jit(solution)/shard_map/context/pallas_call | solution.py:268
  (11 shorter events, 0.2 us)
Async XLA Ops:
  0.0 12.5 %copy-start = (bf16[16,2048]{1,0:T(8,128)(2,1)S(1)}, bf16[16,2048]{1,0:T(8,128)(2,1)}, u32[]{:S(2)}) copy-start(bf16[16,2048]{1,0:T(8,128)(2,1)} %param.9) | copy-start | bytes 196612
  0.0 16.8 %copy-start.2 = (s32[8]{0:T(128)S(1)}, s32[8]{0:T(128)}, u32[]{:S(2)}) copy-start(s32[8]{0:T(128)} %len_ref.1) | copy-start | bytes 100
  2.7 14.0 %all-to-all-start = ((bf16[8,8,384]{2,1,0:T(8,128)(2,1)}), bf16[8,8,384]{2,1,0:T(8,128)(2,1)S(1)}, u32[]{:S(2)}, u32[]{:S(2)}) async-start(bf16[8,8,384]{2,1,0:T(8,128)(2,1)} %concatenate.3), calls=%async_computation | async-start | bytes 98304 | tf_op jit(solution)/shard_map/all_to_all | solution.py:209
  17.9 6.7 %collective-permute-start = (bf16[64,2048]{1,0:T(8,128)(2,1)S(1)}, bf16[64,2048]{1,0:T(8,128)(2,1)S(1)}, u32[]{:S(2)}, u32[]{:S(2)}) collective-permute-start(bf16[64,2048]{1,0:T(8,128)(2,1)S(1)} %get-tuple-element.13), channel_id=1, source_target_pairs={{0,2},{2,0},{4,6},{6,4},{8,10},{10,8},{12,14},{14,12},{1,3},{3,1},... | collective-permute-start | bytes 786440 | tf_op jit(solution)/shard_map/ppermute | solution.py:67
  18.7 16.8 %copy-start.1 = (bf16[768,2048]{1,0:T(8,128)(2,1)S(1)}, bf16[768,2048]{1,0:T(8,128)(2,1)}, u32[]{:S(2)}) copy-start(bf16[768,2048]{1,0:T(8,128)(2,1)} %q_ref.1) | copy-start | bytes 9437188
  18.7 6.7 %collective-permute-start.3 = (bf16[64,2048]{1,0:T(8,128)(2,1)S(1)}, bf16[64,2048]{1,0:T(8,128)(2,1)S(1)}, u32[]{:S(2)}, u32[]{:S(2)}) collective-permute-start(bf16[64,2048]{1,0:T(8,128)(2,1)S(1)} %get-tuple-element.16), channel_id=1, source_target_pairs={{0,4},{2,6},{4,0},{6,2},{8,12},{10,14},{12,8},{14,10},{1,5},{3,7},... | collective-permute-start | bytes 786440 | tf_op jit(solution)/shard_map/ppermute | solution.py:67
  24.6 5.0 %collective-permute-start.1 = (bf16[32,2048]{1,0:T(8,128)(2,1)S(1)}, bf16[32,2048]{1,0:T(8,128)(2,1)S(1)}, u32[]{:S(2)}, u32[]{:S(2)}) collective-permute-start(bf16[32,2048]{1,0:T(8,128)(2,1)S(1)} %slice.51), channel_id=1, source_target_pairs={{0,4},{2,6},{4,0},{6,2},{8,12},{10,14},{12,8},{14,10},{1,5},{3,7},... | collective-permute-start | bytes 393224 | tf_op jit(solution)/shard_map/ppermute | solution.py:67
  25.5 5.7 %collective-permute-start.4 = (bf16[32,2048]{1,0:T(8,128)(2,1)S(1)}, bf16[32,2048]{1,0:T(8,128)(2,1)S(1)}, u32[]{:S(2)}, u32[]{:S(2)}) collective-permute-start(bf16[32,2048]{1,0:T(8,128)(2,1)S(1)} %slice.50), channel_id=1, source_target_pairs={{0,2},{2,0},{4,6},{6,4},{8,10},{10,8},{12,14},{14,12},{1,3},{3,1},... | collective-permute-start | bytes 393224 | tf_op jit(solution)/shard_map/ppermute | solution.py:67
  29.7 5.7 %collective-permute-start.2 = (bf16[16,2048]{1,0:T(8,128)(2,1)S(1)}, bf16[16,2048]{1,0:T(8,128)(2,1)S(1)}, u32[]{:S(2)}, u32[]{:S(2)}) collective-permute-start(bf16[16,2048]{1,0:T(8,128)(2,1)S(1)} %slice.53), channel_id=1, source_target_pairs={{0,8},{2,10},{4,12},{6,14},{8,0},{10,2},{12,4},{14,6},{1,9},{3,11}... | collective-permute-start | bytes 196616 | tf_op jit(solution)/shard_map/ppermute | solution.py:67
  31.3 5.9 %collective-permute-start.5 = (bf16[16,2048]{1,0:T(8,128)(2,1)S(1)}, bf16[16,2048]{1,0:T(8,128)(2,1)S(1)}, u32[]{:S(2)}, u32[]{:S(2)}) collective-permute-start(bf16[16,2048]{1,0:T(8,128)(2,1)S(1)} %slice.52), channel_id=1, source_target_pairs={{0,8},{2,10},{4,12},{6,14},{8,0},{10,2},{12,4},{14,6},{1,9},{3,11}... | collective-permute-start | bytes 196616 | tf_op jit(solution)/shard_map/ppermute | solution.py:67

commit v5 on v4

--- a/solution.py
+++ b/solution.py
@@ -63,43 +63,46 @@
     return context.reshape(row_count, half_width).astype(jnp.bfloat16)
 
 
-def swap(x, n, mask):
-    return lax.ppermute(x, "seq", [(i, i ^ mask) for i in range(n)])
-
-
-def keys_kernel(pos_ref, len_ref, null_ref, w_ref, rows_ref, send_ref, keep_ref, sel_ref, count_ref):
+def swap(x, n, masks):
+    pairs = [(2 * i + head, 2 * (i ^ masks[head]) + head) for i in range(n) for head in range(2)]
+    return lax.ppermute(x, ("seq", "head"), pairs)
+
+
+TARGETS = ((7, 3, 5, 1, 6, 2, 4, 0), (7, 3, 6, 2, 5, 1, 4, 0))
+
+
+def keys_kernel(
+    pos_ref, head_ref, len_ref, null_ref, w_ref, code_ref, rows_ref, send_ref, keep_ref, sel_ref, count_ref
+):
     features = null_ref.shape[1]
     rows = sel_ref.shape[0]
     total = rows_ref.shape[0]
-    text_dev = total * NULL_LEN // rows
-    reqs = len_ref.shape[0]
-    held = rows_ref[...]
-    held = jnp.concatenate([held, jnp.zeros((rows - total, held.shape[1]), held.dtype)], axis=0)
-    row = lax.broadcasted_iota(jnp.int32, (rows, rows), 0)
-    col = lax.broadcasted_iota(jnp.int32, (rows, rows), 1)
-    slot = row // NULL_LEN
-    flip = 7 - ((slot % 2) * 4 + (slot // 2 % 2) * 2 + slot // 4)
-    first = jnp.bitwise_xor(flip, pos_ref[0]) * text_dev
-
-    def take(which, columns):
-        which = which.astype(jnp.float32).astype(jnp.bfloat16)
-        return jnp.dot(which, columns, preferred_element_type=jnp.float32)
-
-    code = take(col == first, held[:, features:]).astype(jnp.int32)
+    text_dev = code_ref.shape[1]
+    text = rows_ref[:, :features]
+    text = jnp.concatenate([text, jnp.zeros((rows - total, features), text.dtype)], axis=0)
+    codes = []
+    for m, m_last in zip(*TARGETS):
+        peer = jnp.bitwise_xor(pos_ref[0], jnp.where(head_ref[0] == 0, m, m_last))
+        code = code_ref[peer][:, features:].astype(jnp.float32)
+        codes += [code] * (NULL_LEN // text_dev)
+    code = jnp.concatenate(codes, axis=0)
+    reqs = len_ref.shape[1]
     uncond = code >= reqs
-    owner = jnp.where(uncond, code - reqs, code)
-    start = jnp.zeros_like(owner)
-    length = jnp.zeros_like(owner)
-    running = jnp.int32(0)
-    for r in range(reqs):
-        start = jnp.where(owner == r, running, start)
-        length = jnp.where(owner == r, len_ref[r], length)
-        running = running + len_ref[r]
+    owner = jnp.where(uncond, code - reqs, code)[:, :reqs]
+    request = lax.broadcasted_iota(jnp.int32, owner.shape, 1).astype(jnp.float32)
+    lengths = jnp.broadcast_to(len_ref[...].astype(jnp.float32), owner.shape)
+    start = jnp.sum(jnp.where(request < owner, lengths, 0.0), axis=1, keepdims=True)
+    length = jnp.sum(jnp.where(request == owner, lengths, 0.0), axis=1, keepdims=True)
+    length = jnp.where(uncond, NULL_LEN, jnp.broadcast_to(length, uncond.shape))
     own = rows - NULL_LEN
-    count_ref[...] = jnp.where(uncond, NULL_LEN, length)[own : own + 8]
-    text_sel = take(col == start + row % NULL_LEN, held[:, :features])
+    count_ref[...] = length[own : own + 8].astype(jnp.int32)
+    row = lax.broadcasted_iota(jnp.int32, code.shape, 0) % NULL_LEN
+    col = lax.broadcasted_iota(jnp.int32, code.shape, 1)
+    pick = col.astype(jnp.float32) == start + row.astype(jnp.float32)
+    pick = pick.astype(jnp.float32).astype(jnp.bfloat16)
+    text_sel = jnp.dot(pick, text, preferred_element_type=jnp.float32)
     null_sel = jnp.concatenate([null_ref[...].astype(jnp.float32)] * (rows // NULL_LEN), axis=0)
-    wide = jnp.concatenate([uncond] * (features // rows), axis=1)
+    wide = jnp.concatenate([uncond] * (features // 128), axis=1)
     sel = jnp.where(wide, null_sel, text_sel).astype(jnp.bfloat16)
     sel_ref[...] = sel
     half = rows // 2
@@ -207,7 +210,6 @@
     text = text_rows.reshape(text_dev, n, features).transpose(1, 0, 2)
     packed = jnp.concatenate([text, jnp.full((n, text_dev, 128), code, jnp.bfloat16)], axis=2)
     held = lax.all_to_all(packed, "seq", split_axis=0, concat_axis=0, tiled=True)
-    held = held.reshape(n * text_dev, features + 128)
     null_cols = lax.dynamic_slice_in_dim(null_rows, pos * features, features, 1)
     weight = kv_weight.reshape(features, 2 * width)
     half = n * NULL_LEN // 2
@@ -226,12 +228,20 @@
             jax.ShapeDtypeStruct((2 * half, features), jnp.bfloat16),
             jax.ShapeDtypeStruct((8, 128), jnp.int32),
         ],
-        in_specs=[smem, smem] + [vmem] * 3,
+        in_specs=[smem] * 2 + [vmem] * 5,
         out_specs=[vmem] * 4,
         compiler_params=params,
         cost_estimate=estimate,
         name="keys",
-    )(pos.reshape(1), prompt_lengths, null_cols, weight, held)
+    )(
+        pos.reshape(1),
+        lax.axis_index("head").astype(jnp.int32).reshape(1),
+        prompt_lengths.reshape(1, reqs),
+        null_cols,
+        weight,
+        held,
+        held.reshape(n * text_dev, features + 128),
+    )
     send_v, keep_v = pl.pallas_call(
         values_kernel,
         out_shape=[sent, kept],
@@ -247,10 +257,10 @@
             total = keep + swap(send, n, mask).astype(jnp.float32)
             cut = total.shape[0] // 2
             send, keep = total[:cut].astype(jnp.bfloat16), total[cut:]
-        return keep, swap(send, n, 4)
-
-    k_parts = reduce_parts(send_k, keep_k, (1, 2))
-    v_parts = reduce_parts(send_v, keep_v, (2, 1))
+        return keep, swap(send, n, (4, 4))
+
+    k_parts = reduce_parts(send_k, keep_k, ((1, 2), (2, 1)))
+    v_parts = reduce_parts(send_v, keep_v, ((2, 1), (1, 2)))
 
     lanes = heads * NULL_LEN
     probs = pl.pallas_call(
@@ -287,7 +297,7 @@
 
     def per_device(queries, text_rows, null_rows, kv_weight, *rest):
         longest = n * text_rows.shape[0] // 4
-        few = n == 8 and longest == NULL_LEN and text_rows.shape[0] == 8
+        few = n == 8 and mesh.shape["head"] == 2 and longest == NULL_LEN and text_rows.shape[0] == 8
         if few:
             return select_plan(n, queries, text_rows, null_rows, kv_weight, *rest)
         return gather_plan(queries, text_rows, null_rows, kv_weight, *rest)

time: 39.7 us -> 41.1 us (1.035)
  waiting for transfers between devices: 14.7 us -> 17 us
  Pallas kernels: 4.96 us -> 4.34 us
    ppermute x6, waiting for transfers between devices: 10.4 us -> 12.7 us  [swap(): return lax.ppermute(x, ('seq', 'head'), pairs)]
    pallas_call x1, Pallas kernels: 1.1 us -> 0.48 us  [select_plan(): pl.pallas_call(keys_kernel, out_shape=[sent, kept, jax.ShapeDtypeStruct((...]
  transfers between devices with their start and end apart: 7 -> 7, of which waited for: 7 -> 6; matrix products, arithmetic and copies ran while one was open for 7% -> 7% of each run, Pallas kernels for 5% -> 4%
where the time goes in v5:
time: 41.1 us; the launch traced here: 40.7 us
  waiting for transfers between devices  17 us (41%)
  starting transfers between devices  13.9 us (34%)
  Pallas kernels  4.34 us (11%)
  local copies, waits for them, and re-layouts  3.96 us (10%)
  between operations  1.46 us (4%)
    ppermute x6, waiting for transfers between devices, swap(): return lax.ppermute(x, ('seq', 'head'), pairs)  12.7 us
    all_to_all x1, starting transfers between devices, select_plan(): lax.all_to_all(packed, 'seq', split_axis=0, concat_axis=0, tiled=True)  7.25 us
    ppermute x6, starting transfers between devices, swap(): return lax.ppermute(x, ('seq', 'head'), pairs)  6.62 us
    all_to_all x1, waiting for transfers between devices, select_plan(): lax.all_to_all(packed, 'seq', split_axis=0, concat_axis=0, tiled=True)  4.28 us
    unnamed x7, local copies, waits for them, and re-layouts  2.5 us
    pallas_call x1, Pallas kernels, select_plan(): pl.pallas_call(context_kernel, out_shape=jax.ShapeDtypeStruct((rows, widt...  2.07 us
    pallas_call x1, Pallas kernels, select_plan(): pl.pallas_call(probs_kernel, out_shape=jax.ShapeDtypeStruct((rows, lanes)...  1.49 us
    concatenate x1, local copies, waits for them, and re-layouts, select_plan(): jnp.concatenate([text, jnp.full((n, text_dev, 128), code, jnp.bfloat16)],...  1.38 us
  transfers between devices with their start and end apart: 7, of which 6 were waited for; matrix products, arithmetic and copies ran while one was open for 7% of the time, Pallas kernels for 4%

profile of v5, /device:TPU:0, one launch (start us, length us, event | category | flops | bytes accessed | tf_op | source)
XLA Modules:
  0.0 40.7 jit_solution(8317458712930959334)
XLA Ops:
  0.0 0.0 copy-start
  0.0 0.0 copy-start.2
  1.3 1.4 %concatenate.3 = bf16[8,8,384]{2,1,0:T(8,128)(2,1)} pad(bf16[8,8,256]{2,1,0:T(8,128)(2,1)} %bitcast.15, bf16[]{:T(256)} %bitcast.5), padding=0_0x0_0x0_128 | pad | bytes 81922 | tf_op jit(solution)/shard_map/concatenate | solution.py:211
  2.7 7.3 %all-to-all-start = ((bf16[8,8,384]{2,1,0:T(8,128)(2,1)}), bf16[8,8,384]{2,1,0:T(8,128)(2,1)S(1)}, u32[]{:S(2)}, u32[]{:S(2)}) async-start(bf16[8,8,384]{2,1,0:T(8,128)(2,1)} %concatenate.3), calls=%async_computation | async-start | bytes 98304 | tf_op jit(solution)/shard_map/all_to_all | solution.py:212
  10.0 2.5 %copy.8 = bf16[32,8,2,2048]{3,1,2,0:T(8,128)(2,1)S(1)} copy(bf16[32,8,2,2048]{3,2,1,0:T(2,128)(2,1)} %bitcast.14) | data formatting | bytes 4194304
  12.5 0.0 copy-done
  12.5 4.3 %all-to-all-done.code_ref = bf16[8,8,384]{2,1,0:T(8,128)(2,1)S(1)} async-done(((bf16[8,8,384]{2,1,0:T(8,128)(2,1)}), bf16[8,8,384]{2,1,0:T(8,128)(2,1)S(1)}, u32[]{:S(2)}, u32[]{:S(2)}) %all-to-all-start) | async-done | bytes 49184 | tf_op jit(solution)/shard_map/all_to_all | solution.py:212
  16.8 0.0 copy-done.2
  16.8 0.5 %keys.1 = (bf16[64,2048]{1,0:T(8,128)(2,1)S(1)}, f32[64,2048]{1,0:T(8,128)S(1)}, bf16[128,256]{1,0:T(8,128)(2,1)S(1)}, s32[8,128]{1,0:T(8,128)S(1)}) custom-call(s32[1]{0:T(128)} %bitcast.pos_ref, s32[1]{0:T(128)} %bitcast.1.head_ref, s32[1,8]{1,0:T(1,128)S(1)} %bitcast.13, bf16[16,256]{1,0:T(8,128)(2,1)S(1)} %constant_dynamic-slice_fusion.null_ref, ...), custom_call_target="tpu_custom_call" | custom-call | flops 134217728 | bytes 1048576 | tf_op jit(solution)/shard_map/keys/pallas_call | solution.py:223
  17.3 0.5 %collective-permute-start = (bf16[64,2048]{1,0:T(8,128)(2,1)S(1)}, bf16[64,2048]{1,0:T(8,128)(2,1)S(1)}, u32[]{:S(2)}, u32[]{:S(2)}) collective-permute-start(bf16[64,2048]{1,0:T(8,128)(2,1)S(1)} %get-tuple-element.13), channel_id=1, source_target_pairs={{0,2},{1,5},{2,0},{3,7},{4,6},{5,1},{6,4},{7,3},{8,10},{9,13},{10,... | collective-permute-start | bytes 786440 | tf_op jit(solution)/shard_map/ppermute | solution.py:68
  17.8 0.3 values.1
  18.1 0.0 copy-start.1
  18.1 0.8 %collective-permute-start.3 = (bf16[64,2048]{1,0:T(8,128)(2,1)S(1)}, bf16[64,2048]{1,0:T(8,128)(2,1)S(1)}, u32[]{:S(2)}, u32[]{:S(2)}) collective-permute-start(bf16[64,2048]{1,0:T(8,128)(2,1)S(1)} %get-tuple-element.16), channel_id=1, source_target_pairs={{0,4},{1,3},{2,6},{3,1},{4,0},{5,7},{6,2},{7,5},{8,12},{9,11},{10,... | collective-permute-start | bytes 786440 | tf_op jit(solution)/shard_map/ppermute | solution.py:68
  18.9 5.8 %collective-permute-done = bf16[64,2048]{1,0:T(8,128)(2,1)S(1)} collective-permute-done((bf16[64,2048]{1,0:T(8,128)(2,1)S(1)}, bf16[64,2048]{1,0:T(8,128)(2,1)S(1)}, u32[]{:S(2)}, u32[]{:S(2)}) %collective-permute-start) | collective-permute-done | bytes 262176 | tf_op jit(solution)/shard_map/ppermute | solution.py:68
  24.7 2.2 %collective-permute-start.1 = (bf16[32,2048]{1,0:T(8,128)(2,1)S(1)}, bf16[32,2048]{1,0:T(8,128)(2,1)S(1)}, u32[]{:S(2)}, u32[]{:S(2)}) collective-permute-start(bf16[32,2048]{1,0:T(8,128)(2,1)S(1)} %slice.51), channel_id=1, source_target_pairs={{0,4},{1,3},{2,6},{3,1},{4,0},{5,7},{6,2},{7,5},{8,12},{9,11},{10,... | collective-permute-start | bytes 393224 | tf_op jit(solution)/shard_map/ppermute | solution.py:68
  26.9 0.0 collective-permute-done.3
  27.0 1.0 %collective-permute-start.4 = (bf16[32,2048]{1,0:T(8,128)(2,1)S(1)}, bf16[32,2048]{1,0:T(8,128)(2,1)S(1)}, u32[]{:S(2)}, u32[]{:S(2)}) collective-permute-start(bf16[32,2048]{1,0:T(8,128)(2,1)S(1)} %slice.50), channel_id=1, source_target_pairs={{0,2},{1,5},{2,0},{3,7},{4,6},{5,1},{6,4},{7,3},{8,10},{9,13},{10,... | collective-permute-start | bytes 393224 | tf_op jit(solution)/shard_map/ppermute | solution.py:68
  28.0 2.6 %collective-permute-done.1 = bf16[32,2048]{1,0:T(8,128)(2,1)S(1)} collective-permute-done((bf16[32,2048]{1,0:T(8,128)(2,1)S(1)}, bf16[32,2048]{1,0:T(8,128)(2,1)S(1)}, u32[]{:S(2)}, u32[]{:S(2)}) %collective-permute-start.1) | collective-permute-done | bytes 131104 | tf_op jit(solution)/shard_map/ppermute | solution.py:68
  30.6 0.5 %collective-permute-start.2 = (bf16[16,2048]{1,0:T(8,128)(2,1)S(1)}, bf16[16,2048]{1,0:T(8,128)(2,1)S(1)}, u32[]{:S(2)}, u32[]{:S(2)}) collective-permute-start(bf16[16,2048]{1,0:T(8,128)(2,1)S(1)} %slice.53), channel_id=1, source_target_pairs={{0,8},{1,9},{2,10},{3,11},{4,12},{5,13},{6,14},{7,15},{8,0},{9,1},... | collective-permute-start | bytes 196616 | tf_op jit(solution)/shard_map/ppermute | solution.py:68
  31.1 1.0 %collective-permute-done.4 = bf16[32,2048]{1,0:T(8,128)(2,1)S(1)} collective-permute-done((bf16[32,2048]{1,0:T(8,128)(2,1)S(1)}, bf16[32,2048]{1,0:T(8,128)(2,1)S(1)}, u32[]{:S(2)}, u32[]{:S(2)}) %collective-permute-start.4) | collective-permute-done | bytes 131104 | tf_op jit(solution)/shard_map/ppermute | solution.py:68
  32.1 1.6 %collective-permute-start.5 = (bf16[16,2048]{1,0:T(8,128)(2,1)S(1)}, bf16[16,2048]{1,0:T(8,128)(2,1)S(1)}, u32[]{:S(2)}, u32[]{:S(2)}) collective-permute-start(bf16[16,2048]{1,0:T(8,128)(2,1)S(1)} %slice.52), channel_id=1, source_target_pairs={{0,8},{1,9},{2,10},{3,11},{4,12},{5,13},{6,14},{7,15},{8,0},{9,1},... | collective-permute-start | bytes 196616 | tf_op jit(solution)/shard_map/ppermute | solution.py:68
  33.7 2.1 %collective-permute-done.2.got_ref = bf16[16,2048]{1,0:T(8,128)(2,1)S(1)} collective-permute-done((bf16[16,2048]{1,0:T(8,128)(2,1)S(1)}, bf16[16,2048]{1,0:T(8,128)(2,1)S(1)}, u32[]{:S(2)}, u32[]{:S(2)}) %collective-permute-start.2) | collective-permute-done | bytes 65568 | tf_op jit(solution)/shard_map/ppermute | solution.py:68
  35.8 0.0 copy-done.1
  35.8 1.5 %probs.1.p_ref = bf16[768,256]{1,0:T(8,128)(2,1)S(1)} custom-call(s32[8,128]{1,0:T(8,128)S(1)} %get-tuple-element.11.count_ref, bf16[768,2048]{1,0:T(8,128)(2,1)S(1)} %copy-done.1, f32[16,2048]{1,0:T(8,128)S(1)} %slice.38.kept_ref, bf16[16,2048]{1,0:T(8,128)(2,1)S(1)} %collective-permute-done.2.got_ref), custom_call_target="tpu_custom_call" | custom-call | flops 805306368 | bytes 3145728 | tf_op jit(solution)/shard_map/probs/pallas_call | solution.py:266
  37.3 1.3 %collective-permute-done.5.got_ref = bf16[16,2048]{1,0:T(8,128)(2,1)S(1)} collective-permute-done((bf16[16,2048]{1,0:T(8,128)(2,1)S(1)}, bf16[16,2048]{1,0:T(8,128)(2,1)S(1)}, u32[]{:S(2)}, u32[]{:S(2)}) %collective-permute-start.5) | collective-permute-done | bytes 65568 | tf_op jit(solution)/shard_map/ppermute | solution.py:68
  38.7 2.1 %context.1 = bf16[768,2048]{1,0:T(8,128)(2,1)} custom-call(bf16[768,256]{1,0:T(8,128)(2,1)S(1)} %probs.1.p_ref, f32[16,2048]{1,0:T(8,128)S(1)} %slice.42.kept_ref, bf16[16,2048]{1,0:T(8,128)(2,1)S(1)} %collective-permute-done.5.got_ref), custom_call_target="tpu_custom_call" | custom-call | flops 805306368 | bytes 3145728 | tf_op jit(solution)/shard_map/context/pallas_call | solution.py:278
  (11 shorter events, 0.2 us)
Async XLA Ops:
  0.0 12.5 %copy-start = (bf16[16,2048]{1,0:T(8,128)(2,1)S(1)}, bf16[16,2048]{1,0:T(8,128)(2,1)}, u32[]{:S(2)}) copy-start(bf16[16,2048]{1,0:T(8,128)(2,1)} %param.9) | copy-start | bytes 196612
  0.0 16.8 %copy-start.2 = (s32[8]{0:T(128)S(1)}, s32[8]{0:T(128)}, u32[]{:S(2)}) copy-start(s32[8]{0:T(128)} %param.11) | copy-start | bytes 100
  2.7 14.0 %all-to-all-start = ((bf16[8,8,384]{2,1,0:T(8,128)(2,1)}), bf16[8,8,384]{2,1,0:T(8,128)(2,1)S(1)}, u32[]{:S(2)}, u32[]{:S(2)}) async-start(bf16[8,8,384]{2,1,0:T(8,128)(2,1)} %concatenate.3), calls=%async_computation | async-start | bytes 98304 | tf_op jit(solution)/shard_map/all_to_all | solution.py:212
  17.3 7.4 %collective-permute-start = (bf16[64,2048]{1,0:T(8,128)(2,1)S(1)}, bf16[64,2048]{1,0:T(8,128)(2,1)S(1)}, u32[]{:S(2)}, u32[]{:S(2)}) collective-permute-start(bf16[64,2048]{1,0:T(8,128)(2,1)S(1)} %get-tuple-element.13), channel_id=1, source_target_pairs={{0,2},{1,5},{2,0},{3,7},{4,6},{5,1},{6,4},{7,3},{8,10},{9,13},{10,... | collective-permute-start | bytes 786440 | tf_op jit(solution)/shard_map/ppermute | solution.py:68
  18.1 17.8 %copy-start.1 = (bf16[768,2048]{1,0:T(8,128)(2,1)S(1)}, bf16[768,2048]{1,0:T(8,128)(2,1)}, u32[]{:S(2)}) copy-start(bf16[768,2048]{1,0:T(8,128)(2,1)} %q_ref.1) | copy-start | bytes 9437188
  18.1 8.8 %collective-permute-start.3 = (bf16[64,2048]{1,0:T(8,128)(2,1)S(1)}, bf16[64,2048]{1,0:T(8,128)(2,1)S(1)}, u32[]{:S(2)}, u32[]{:S(2)}) collective-permute-start(bf16[64,2048]{1,0:T(8,128)(2,1)S(1)} %get-tuple-element.16), channel_id=1, source_target_pairs={{0,4},{1,3},{2,6},{3,1},{4,0},{5,7},{6,2},{7,5},{8,12},{9,11},{10,... | collective-permute-start | bytes 786440 | tf_op jit(solution)/shard_map/ppermute | solution.py:68
  24.7 5.8 %collective-permute-start.1 = (bf16[32,2048]{1,0:T(8,128)(2,1)S(1)}, bf16[32,2048]{1,0:T(8,128)(2,1)S(1)}, u32[]{:S(2)}, u32[]{:S(2)}) collective-permute-start(bf16[32,2048]{1,0:T(8,128)(2,1)S(1)} %slice.51), channel_id=1, source_target_pairs={{0,4},{1,3},{2,6},{3,1},{4,0},{5,7},{6,2},{7,5},{8,12},{9,11},{10,... | collective-permute-start | bytes 393224 | tf_op jit(solution)/shard_map/ppermute | solution.py:68
  27.0 5.0 %collective-permute-start.4 = (bf16[32,2048]{1,0:T(8,128)(2,1)S(1)}, bf16[32,2048]{1,0:T(8,128)(2,1)S(1)}, u32[]{:S(2)}, u32[]{:S(2)}) collective-permute-start(bf16[32,2048]{1,0:T(8,128)(2,1)S(1)} %slice.50), channel_id=1, source_target_pairs={{0,2},{1,5},{2,0},{3,7},{4,6},{5,1},{6,4},{7,3},{8,10},{9,13},{10,... | collective-permute-start | bytes 393224 | tf_op jit(solution)/shard_map/ppermute | solution.py:68
  30.6 5.2 %collective-permute-start.2 = (bf16[16,2048]{1,0:T(8,128)(2,1)S(1)}, bf16[16,2048]{1,0:T(8,128)(2,1)S(1)}, u32[]{:S(2)}, u32[]{:S(2)}) collective-permute-start(bf16[16,2048]{1,0:T(8,128)(2,1)S(1)} %slice.53), channel_id=1, source_target_pairs={{0,8},{1,9},{2,10},{3,11},{4,12},{5,13},{6,14},{7,15},{8,0},{9,1},... | collective-permute-start | bytes 196616 | tf_op jit(solution)/shard_map/ppermute | solution.py:68
  32.1 6.6 %collective-permute-start.5 = (bf16[16,2048]{1,0:T(8,128)(2,1)S(1)}, bf16[16,2048]{1,0:T(8,128)(2,1)S(1)}, u32[]{:S(2)}, u32[]{:S(2)}) collective-permute-start(bf16[16,2048]{1,0:T(8,128)(2,1)S(1)} %slice.52), channel_id=1, source_target_pairs={{0,8},{1,9},{2,10},{3,11},{4,12},{5,13},{6,14},{7,15},{8,0},{9,1},... | collective-permute-start | bytes 196616 | tf_op jit(solution)/shard_map/ppermute | solution.py:68

commit v6 on v5

--- a/solution.py
+++ b/solution.py
@@ -63,16 +63,38 @@
     return context.reshape(row_count, half_width).astype(jnp.bfloat16)
 
 
-def swap(x, n, masks):
-    pairs = [(2 * i + head, 2 * (i ^ masks[head]) + head) for i in range(n) for head in range(2)]
-    return lax.ppermute(x, ("seq", "head"), pairs)
-
-
-TARGETS = ((7, 3, 5, 1, 6, 2, 4, 0), (7, 3, 6, 2, 5, 1, 4, 0))
+def swap(x, n, mask):
+    return lax.ppermute(x, "seq", [(i, i ^ mask) for i in range(n)])
+
+
+TARGETS = (7, 3, 6, 2, 5, 1, 4, 0)
+MIDDLE = 5
+
+
+def pack_kernel(reqs, owner_ref, flag_ref, text_hbm, out_hbm, code_ref, sems):
+    places, _, width = out_hbm.shape
+    features = width - 128
+    copies = []
+    for place in range(places):
+        cols = pl.ds((place ^ MIDDLE) * features, features)
+        copies.append(
+            pltpu.make_async_copy(
+                text_hbm.at[:, cols], out_hbm.at[place, :, pl.ds(0, features)], sems.at[place]
+            )
+        )
+        copies[-1].start()
+    code = (owner_ref[0] + reqs * flag_ref[0]).astype(jnp.float32)
+    code_ref[...] = jnp.full(code_ref.shape, code, jnp.float32).astype(jnp.bfloat16)
+    copies.append(
+        pltpu.make_async_copy(code_ref, out_hbm.at[:, :, pl.ds(features, 128)], sems.at[places])
+    )
+    copies[-1].start()
+    for copy in copies:
+        copy.wait()
 
 
 def keys_kernel(
-    pos_ref, head_ref, len_ref, null_ref, w_ref, code_ref, rows_ref, send_ref, keep_ref, sel_ref, count_ref
+    pos_ref, len_ref, null_ref, w_ref, code_ref, rows_ref, send_ref, keep_ref, sel_ref, count_ref
 ):
     features = null_ref.shape[1]
     rows = sel_ref.shape[0]
@@ -81,9 +103,8 @@
     text = rows_ref[:, :features]
     text = jnp.concatenate([text, jnp.zeros((rows - total, features), text.dtype)], axis=0)
     codes = []
-    for m, m_last in zip(*TARGETS):
-        peer = jnp.bitwise_xor(pos_ref[0], jnp.where(head_ref[0] == 0, m, m_last))
-        code = code_ref[peer][:, features:].astype(jnp.float32)
+    for m in TARGETS:
+        code = code_ref[jnp.bitwise_xor(pos_ref[0], m ^ MIDDLE)][:, features:].astype(jnp.float32)
         codes += [code] * (NULL_LEN // text_dev)
     code = jnp.concatenate(codes, axis=0)
     reqs = len_ref.shape[1]
@@ -97,7 +118,7 @@
     own = rows - NULL_LEN
     count_ref[...] = length[own : own + 8].astype(jnp.int32)
     row = lax.broadcasted_iota(jnp.int32, code.shape, 0) % NULL_LEN
-    col = lax.broadcasted_iota(jnp.int32, code.shape, 1)
+    col = jnp.bitwise_xor(lax.broadcasted_iota(jnp.int32, code.shape, 1), MIDDLE * text_dev)
     pick = col.astype(jnp.float32) == start + row.astype(jnp.float32)
     pick = pick.astype(jnp.float32).astype(jnp.bfloat16)
     text_sel = jnp.dot(pick, text, preferred_element_type=jnp.float32)
@@ -151,8 +172,8 @@
     for c in range(0, width, 512):
         cols = slice(c, c + 512)
         wide_ref[:, cols] = spread_heads(kept_ref, got_ref, cols)
-    count = jnp.broadcast_to(jnp.concatenate([count_ref[:1]] * (out_ref.shape[1] // 128), axis=1), (256, out_ref.shape[1]))
-    block = 256
+    count = jnp.broadcast_to(jnp.concatenate([count_ref[:1]] * (out_ref.shape[1] // 128), axis=1), out_ref.shape)
+    block = q_ref.shape[0]
     for first in range(0, q_ref.shape[0], block):
         scores = lax.dot_general(
             q_ref[first : first + block],
@@ -206,10 +227,22 @@
     anywhere = pl.BlockSpec(memory_space=pl.ANY)
     params = pltpu.CompilerParams(vmem_limit_bytes=VMEM_LIMIT)
     text_dev = text_rows.shape[0]
-    code = (block_owner[0] + reqs * uncond_flags[0]).astype(jnp.bfloat16)
-    text = text_rows.reshape(text_dev, n, features).transpose(1, 0, 2)
-    packed = jnp.concatenate([text, jnp.full((n, text_dev, 128), code, jnp.bfloat16)], axis=2)
-    held = lax.all_to_all(packed, "seq", split_axis=0, concat_axis=0, tiled=True)
+    packed = pl.pallas_call(
+        functools.partial(pack_kernel, reqs),
+        out_shape=jax.ShapeDtypeStruct((n, text_dev, features + 128), jnp.bfloat16),
+        in_specs=[smem, smem, anywhere],
+        out_specs=anywhere,
+        scratch_shapes=[
+            pltpu.VMEM((n, text_dev, 128), jnp.bfloat16),
+            pltpu.SemaphoreType.DMA((n + 1,)),
+        ],
+        compiler_params=pltpu.CompilerParams(vmem_limit_bytes=56 * 1024 * 1024),
+        name="pack",
+    )(block_owner, uncond_flags, text_rows)
+    group = [place ^ MIDDLE for place in range(n)]
+    held = lax.all_to_all(
+        packed, "seq", split_axis=0, concat_axis=0, axis_index_groups=[group], tiled=True
+    )
     null_cols = lax.dynamic_slice_in_dim(null_rows, pos * features, features, 1)
     weight = kv_weight.reshape(features, 2 * width)
     half = n * NULL_LEN // 2
@@ -228,14 +261,13 @@
             jax.ShapeDtypeStruct((2 * half, features), jnp.bfloat16),
             jax.ShapeDtypeStruct((8, 128), jnp.int32),
         ],
-        in_specs=[smem] * 2 + [vmem] * 5,
+        in_specs=[smem] + [vmem] * 5,
         out_specs=[vmem] * 4,
         compiler_params=params,
         cost_estimate=estimate,
         name="keys",
     )(
         pos.reshape(1),
-        lax.axis_index("head").astype(jnp.int32).reshape(1),
         prompt_lengths.reshape(1, reqs),
         null_cols,
         weight,
@@ -257,10 +289,10 @@
             total = keep + swap(send, n, mask).astype(jnp.float32)
             cut = total.shape[0] // 2
             send, keep = total[:cut].astype(jnp.bfloat16), total[cut:]
-        return keep, swap(send, n, (4, 4))
-
-    k_parts = reduce_parts(send_k, keep_k, ((1, 2), (2, 1)))
-    v_parts = reduce_parts(send_v, keep_v, ((2, 1), (1, 2)))
+        return keep, swap(send, n, 4)
+
+    k_parts = reduce_parts(send_k, keep_k, (2, 1))
+    v_parts = reduce_parts(send_v, keep_v, (1, 2))
 
     lanes = heads * NULL_LEN
     probs = pl.pallas_call(
@@ -297,7 +329,7 @@
 
     def per_device(queries, text_rows, null_rows, kv_weight, *rest):
         longest = n * text_rows.shape[0] // 4
-        few = n == 8 and mesh.shape["head"] == 2 and longest == NULL_LEN and text_rows.shape[0] == 8
+        few = n == 8 and longest == NULL_LEN and text_rows.shape[0] == 8
         if few:
             return select_plan(n, queries, text_rows, null_rows, kv_weight, *rest)
         return gather_plan(queries, text_rows, null_rows, kv_weight, *rest)

time: 41.1 us -> 37.9 us (0.922)
  waiting for transfers between devices: 17 us -> 9.85 us
  starting transfers between devices: 13.9 us -> 17 us
  Pallas kernels: 4.34 us -> 6.6 us
  local copies, waits for them, and re-layouts: 3.96 us -> 2.58 us
    ppermute x6, waiting for transfers between devices: 12.7 us -> 8.97 us  [swap(): return lax.ppermute(x, 'seq', [(i, i ^ mask) for i in range(n)])]
    all_to_all x1, waiting for transfers between devices: 4.28 us -> 0.88 us  [select_plan(): lax.all_to_all(packed, 'seq', split_axis=0, concat_axis=0, axis_index_gro...]
    pallas_call x0 -> x1, Pallas kernels: none -> 2.18 us  [select_plan(): pl.pallas_call(functools.partial(pack_kernel, reqs), out_shape=jax.ShapeD...]
    ppermute x6, starting transfers between devices: 6.62 us -> 8.77 us  [swap(): return lax.ppermute(x, 'seq', [(i, i ^ mask) for i in range(n)])]
    concatenate x1 -> x0, local copies, waits for them, and re-layouts: 1.38 us -> none  [select_plan(): jnp.concatenate([text, jnp.full((n, text_dev, 128), code, jnp.bfloat16)],...]
    all_to_all x1, starting transfers between devices: 7.25 us -> 8.25 us  [select_plan(): lax.all_to_all(packed, 'seq', split_axis=0, concat_axis=0, axis_index_gro...]
  transfers between devices with their start and end apart: 7 -> 7, of which waited for: 6 -> 6; matrix products, arithmetic and copies ran while one was open for 7% -> 7% of each run, Pallas kernels for 4% -> 5%
where the time goes in v6:
time: 37.9 us; the launch traced here: 37.7 us
  starting transfers between devices  17 us (45%)
  waiting for transfers between devices  9.85 us (26%)
  Pallas kernels  6.6 us (17%)
  local copies, waits for them, and re-layouts  2.58 us (7%)
  between operations  1.45 us (4%)
    ppermute x6, waiting for transfers between devices, swap(): return lax.ppermute(x, 'seq', [(i, i ^ mask) for i in range(n)])  8.97 us
    ppermute x6, starting transfers between devices, swap(): return lax.ppermute(x, 'seq', [(i, i ^ mask) for i in range(n)])  8.77 us
    all_to_all x1, starting transfers between devices, select_plan(): lax.all_to_all(packed, 'seq', split_axis=0, concat_axis=0, axis_index_gro...  8.25 us
    unnamed x7, local copies, waits for them, and re-layouts  2.5 us
    pallas_call x1, Pallas kernels, select_plan(): pl.pallas_call(functools.partial(pack_kernel, reqs), out_shape=jax.ShapeD...  2.18 us
    pallas_call x1, Pallas kernels, select_plan(): pl.pallas_call(context_kernel, out_shape=jax.ShapeDtypeStruct((rows, widt...  2.07 us
    pallas_call x1, Pallas kernels, select_plan(): pl.pallas_call(probs_kernel, out_shape=jax.ShapeDtypeStruct((rows, lanes)...  1.57 us
    all_to_all x1, waiting for transfers between devices, select_plan(): lax.all_to_all(packed, 'seq', split_axis=0, concat_axis=0, axis_index_gro...  0.88 us
  transfers between devices with their start and end apart: 7, of which 6 were waited for; matrix products, arithmetic and copies ran while one was open for 7% of the time, Pallas kernels for 5%

profile of v6, /device:TPU:0, one launch (start us, length us, event | category | flops | bytes accessed | tf_op | source)
XLA Modules:
  0.0 37.7 jit_solution(15090600512912587573)
XLA Ops:
  0.0 0.0 copy-start
  0.0 0.0 copy-start.2
  1.3 2.2 %pack.1 = bf16[8,8,384]{2,1,0:T(8,128)(2,1)} custom-call(s32[1]{0:T(128)S(6)} %copy.9.owner_ref, s32[1]{0:T(128)S(6)} %copy.10.flag_ref, bf16[8,2048]{1,0:T(8,128)(2,1)} %text_hbm.1), custom_call_target="tpu_custom_call" | custom-call | tf_op jit(solution)/shard_map/pack/pallas_call | solution.py:230
  3.5 8.3 %all-to-all-start = ((bf16[8,8,384]{2,1,0:T(8,128)(2,1)}), bf16[8,8,384]{2,1,0:T(8,128)(2,1)S(1)}, u32[]{:S(2)}, u32[]{:S(2)}) async-start(bf16[8,8,384]{2,1,0:T(8,128)(2,1)} %pack.1), calls=%async_computation | async-start | bytes 98304 | tf_op jit(solution)/shard_map/all_to_all | solution.py:243
  11.8 2.5 %copy.8 = bf16[32,8,2,2048]{3,1,2,0:T(8,128)(2,1)S(1)} copy(bf16[32,8,2,2048]{3,2,1,0:T(2,128)(2,1)} %bitcast.9) | data formatting | bytes 4194304
  14.3 0.0 copy-done
  14.3 0.9 %all-to-all-done.code_ref = bf16[8,8,384]{2,1,0:T(8,128)(2,1)S(1)} async-done(((bf16[8,8,384]{2,1,0:T(8,128)(2,1)}), bf16[8,8,384]{2,1,0:T(8,128)(2,1)S(1)}, u32[]{:S(2)}, u32[]{:S(2)}) %all-to-all-start) | async-done | bytes 49184 | tf_op jit(solution)/shard_map/all_to_all | solution.py:243
  15.2 0.0 copy-done.2
  15.2 0.5 %keys.1 = (bf16[64,2048]{1,0:T(8,128)(2,1)S(1)}, f32[64,2048]{1,0:T(8,128)S(1)}, bf16[128,256]{1,0:T(8,128)(2,1)S(1)}, s32[8,128]{1,0:T(8,128)S(1)}) custom-call(s32[1]{0:T(128)} %bitcast.pos_ref, s32[1,8]{1,0:T(1,128)S(1)} %bitcast.8, bf16[16,256]{1,0:T(8,128)(2,1)S(1)} %constant_dynamic-slice_fusion.null_ref, bf16[256,4096]{1,0:T(8,128)(2,1)S(1)} %bitcast.5, ...), custom_call_target="tpu_custom_call" | custom-call | flops 134217728 | bytes 1048576 | tf_op jit(solution)/shard_map/keys/pallas_call | solution.py:256
  15.7 0.8 %collective-permute-start = (bf16[64,2048]{1,0:T(8,128)(2,1)S(1)}, bf16[64,2048]{1,0:T(8,128)(2,1)S(1)}, u32[]{:S(2)}, u32[]{:S(2)}) collective-permute-start(bf16[64,2048]{1,0:T(8,128)(2,1)S(1)} %get-tuple-element.13), channel_id=1, source_target_pairs={{0,4},{2,6},{4,0},{6,2},{8,12},{10,14},{12,8},{14,10},{1,5},{3,7},... | collective-permute-start | bytes 786440 | tf_op jit(solution)/shard_map/ppermute | solution.py:67
  16.5 0.3 values.1
  16.8 0.0 copy-start.1
  16.8 1.5 %collective-permute-start.3 = (bf16[64,2048]{1,0:T(8,128)(2,1)S(1)}, bf16[64,2048]{1,0:T(8,128)(2,1)S(1)}, u32[]{:S(2)}, u32[]{:S(2)}) collective-permute-start(bf16[64,2048]{1,0:T(8,128)(2,1)S(1)} %get-tuple-element.16), channel_id=1, source_target_pairs={{0,2},{2,0},{4,6},{6,4},{8,10},{10,8},{12,14},{14,12},{1,3},{3,1},... | collective-permute-start | bytes 786440 | tf_op jit(solution)/shard_map/ppermute | solution.py:67
  18.3 4.3 %collective-permute-done = bf16[64,2048]{1,0:T(8,128)(2,1)S(1)} collective-permute-done((bf16[64,2048]{1,0:T(8,128)(2,1)S(1)}, bf16[64,2048]{1,0:T(8,128)(2,1)S(1)}, u32[]{:S(2)}, u32[]{:S(2)}) %collective-permute-start) | collective-permute-done | bytes 262176 | tf_op jit(solution)/shard_map/ppermute | solution.py:67
  22.7 1.8 %collective-permute-start.1 = (bf16[32,2048]{1,0:T(8,128)(2,1)S(1)}, bf16[32,2048]{1,0:T(8,128)(2,1)S(1)}, u32[]{:S(2)}, u32[]{:S(2)}) collective-permute-start(bf16[32,2048]{1,0:T(8,128)(2,1)S(1)} %slice.51), channel_id=1, source_target_pairs={{0,2},{2,0},{4,6},{6,4},{8,10},{10,8},{12,14},{14,12},{1,3},{3,1},... | collective-permute-start | bytes 393224 | tf_op jit(solution)/shard_map/ppermute | solution.py:67
  24.5 0.0 collective-permute-done.3
  24.5 1.0 %collective-permute-start.4 = (bf16[32,2048]{1,0:T(8,128)(2,1)S(1)}, bf16[32,2048]{1,0:T(8,128)(2,1)S(1)}, u32[]{:S(2)}, u32[]{:S(2)}) collective-permute-start(bf16[32,2048]{1,0:T(8,128)(2,1)S(1)} %slice.50), channel_id=1, source_target_pairs={{0,4},{2,6},{4,0},{6,2},{8,12},{10,14},{12,8},{14,10},{1,5},{3,7},... | collective-permute-start | bytes 393224 | tf_op jit(solution)/shard_map/ppermute | solution.py:67
  25.5 2.2 %collective-permute-done.1 = bf16[32,2048]{1,0:T(8,128)(2,1)S(1)} collective-permute-done((bf16[32,2048]{1,0:T(8,128)(2,1)S(1)}, bf16[32,2048]{1,0:T(8,128)(2,1)S(1)}, u32[]{:S(2)}, u32[]{:S(2)}) %collective-permute-start.1) | collective-permute-done | bytes 131104 | tf_op jit(solution)/shard_map/ppermute | solution.py:67
  27.8 1.9 %collective-permute-start.2 = (bf16[16,2048]{1,0:T(8,128)(2,1)S(1)}, bf16[16,2048]{1,0:T(8,128)(2,1)S(1)}, u32[]{:S(2)}, u32[]{:S(2)}) collective-permute-start(bf16[16,2048]{1,0:T(8,128)(2,1)S(1)} %slice.53), channel_id=1, source_target_pairs={{0,8},{2,10},{4,12},{6,14},{8,0},{10,2},{12,4},{14,6},{1,9},{3,11}... | collective-permute-start | bytes 196616 | tf_op jit(solution)/shard_map/ppermute | solution.py:67
  29.7 0.5 %collective-permute-done.4 = bf16[32,2048]{1,0:T(8,128)(2,1)S(1)} collective-permute-done((bf16[32,2048]{1,0:T(8,128)(2,1)S(1)}, bf16[32,2048]{1,0:T(8,128)(2,1)S(1)}, u32[]{:S(2)}, u32[]{:S(2)}) %collective-permute-start.4) | collective-permute-done | bytes 131104 | tf_op jit(solution)/shard_map/ppermute | solution.py:67
  30.4 1.8 %collective-permute-start.5 = (bf16[16,2048]{1,0:T(8,128)(2,1)S(1)}, bf16[16,2048]{1,0:T(8,128)(2,1)S(1)}, u32[]{:S(2)}, u32[]{:S(2)}) collective-permute-start(bf16[16,2048]{1,0:T(8,128)(2,1)S(1)} %slice.52), channel_id=1, source_target_pairs={{0,8},{2,10},{4,12},{6,14},{8,0},{10,2},{12,4},{14,6},{1,9},{3,11}... | collective-permute-start | bytes 196616 | tf_op jit(solution)/shard_map/ppermute | solution.py:67
  32.1 1.6 %collective-permute-done.2.got_ref = bf16[16,2048]{1,0:T(8,128)(2,1)S(1)} collective-permute-done((bf16[16,2048]{1,0:T(8,128)(2,1)S(1)}, bf16[16,2048]{1,0:T(8,128)(2,1)S(1)}, u32[]{:S(2)}, u32[]{:S(2)}) %collective-permute-start.2) | collective-permute-done | bytes 65568 | tf_op jit(solution)/shard_map/ppermute | solution.py:67
  33.7 0.0 copy-done.1
  33.7 1.6 %probs.1.p_ref = bf16[768,256]{1,0:T(8,128)(2,1)S(1)} custom-call(s32[8,128]{1,0:T(8,128)S(1)} %get-tuple-element.11.count_ref, bf16[768,2048]{1,0:T(8,128)(2,1)S(1)} %copy-done.1, f32[16,2048]{1,0:T(8,128)S(1)} %slice.38.kept_ref, bf16[16,2048]{1,0:T(8,128)(2,1)S(1)} %collective-permute-done.2.got_ref), custom_call_target="tpu_custom_call" | custom-call | flops 805306368 | bytes 3145728 | tf_op jit(solution)/shard_map/probs/pallas_call | solution.py:298
  35.3 0.3 collective-permute-done.5.got_ref
  35.6 2.1 %context.1 = bf16[768,2048]{1,0:T(8,128)(2,1)} custom-call(bf16[768,256]{1,0:T(8,128)(2,1)S(1)} %probs.1.p_ref, f32[16,2048]{1,0:T(8,128)S(1)} %slice.42.kept_ref, bf16[16,2048]{1,0:T(8,128)(2,1)S(1)} %collective-permute-done.5.got_ref), custom_call_target="tpu_custom_call" | custom-call | flops 805306368 | bytes 3145728 | tf_op jit(solution)/shard_map/context/pallas_call | solution.py:310
  (11 shorter events, 0.2 us)
Async XLA Ops:
  0.0 14.3 %copy-start = (bf16[16,2048]{1,0:T(8,128)(2,1)S(1)}, bf16[16,2048]{1,0:T(8,128)(2,1)}, u32[]{:S(2)}) copy-start(bf16[16,2048]{1,0:T(8,128)(2,1)} %param.9) | copy-start | bytes 196612
  0.0 15.2 %copy-start.2 = (s32[8]{0:T(128)S(1)}, s32[8]{0:T(128)}, u32[]{:S(2)}) copy-start(s32[8]{0:T(128)} %param.11) | copy-start | bytes 100
  3.5 11.6 %all-to-all-start = ((bf16[8,8,384]{2,1,0:T(8,128)(2,1)}), bf16[8,8,384]{2,1,0:T(8,128)(2,1)S(1)}, u32[]{:S(2)}, u32[]{:S(2)}) async-start(bf16[8,8,384]{2,1,0:T(8,128)(2,1)} %pack.1), calls=%async_computation | async-start | bytes 98304 | tf_op jit(solution)/shard_map/all_to_all | solution.py:243
  15.7 7.0 %collective-permute-start = (bf16[64,2048]{1,0:T(8,128)(2,1)S(1)}, bf16[64,2048]{1,0:T(8,128)(2,1)S(1)}, u32[]{:S(2)}, u32[]{:S(2)}) collective-permute-start(bf16[64,2048]{1,0:T(8,128)(2,1)S(1)} %get-tuple-element.13), channel_id=1, source_target_pairs={{0,4},{2,6},{4,0},{6,2},{8,12},{10,14},{12,8},{14,10},{1,5},{3,7},... | collective-permute-start | bytes 786440 | tf_op jit(solution)/shard_map/ppermute | solution.py:67
  16.8 16.9 %copy-start.1 = (bf16[768,2048]{1,0:T(8,128)(2,1)S(1)}, bf16[768,2048]{1,0:T(8,128)(2,1)}, u32[]{:S(2)}) copy-start(bf16[768,2048]{1,0:T(8,128)(2,1)} %q_ref.1) | copy-start | bytes 9437188
  16.8 7.7 %collective-permute-start.3 = (bf16[64,2048]{1,0:T(8,128)(2,1)S(1)}, bf16[64,2048]{1,0:T(8,128)(2,1)S(1)}, u32[]{:S(2)}, u32[]{:S(2)}) collective-permute-start(bf16[64,2048]{1,0:T(8,128)(2,1)S(1)} %get-tuple-element.16), channel_id=1, source_target_pairs={{0,2},{2,0},{4,6},{6,4},{8,10},{10,8},{12,14},{14,12},{1,3},{3,1},... | collective-permute-start | bytes 786440 | tf_op jit(solution)/shard_map/ppermute | solution.py:67
  22.7 5.0 %collective-permute-start.1 = (bf16[32,2048]{1,0:T(8,128)(2,1)S(1)}, bf16[32,2048]{1,0:T(8,128)(2,1)S(1)}, u32[]{:S(2)}, u32[]{:S(2)}) collective-permute-start(bf16[32,2048]{1,0:T(8,128)(2,1)S(1)} %slice.51), channel_id=1, source_target_pairs={{0,2},{2,0},{4,6},{6,4},{8,10},{10,8},{12,14},{14,12},{1,3},{3,1},... | collective-permute-start | bytes 393224 | tf_op jit(solution)/shard_map/ppermute | solution.py:67
  24.5 5.7 %collective-permute-start.4 = (bf16[32,2048]{1,0:T(8,128)(2,1)S(1)}, bf16[32,2048]{1,0:T(8,128)(2,1)S(1)}, u32[]{:S(2)}, u32[]{:S(2)}) collective-permute-start(bf16[32,2048]{1,0:T(8,128)(2,1)S(1)} %slice.50), channel_id=1, source_target_pairs={{0,4},{2,6},{4,0},{6,2},{8,12},{10,14},{12,8},{14,10},{1,5},{3,7},... | collective-permute-start | bytes 393224 | tf_op jit(solution)/shard_map/ppermute | solution.py:67
  27.8 5.9 %collective-permute-start.2 = (bf16[16,2048]{1,0:T(8,128)(2,1)S(1)}, bf16[16,2048]{1,0:T(8,128)(2,1)S(1)}, u32[]{:S(2)}, u32[]{:S(2)}) collective-permute-start(bf16[16,2048]{1,0:T(8,128)(2,1)S(1)} %slice.53), channel_id=1, source_target_pairs={{0,8},{2,10},{4,12},{6,14},{8,0},{10,2},{12,4},{14,6},{1,9},{3,11}... | collective-permute-start | bytes 196616 | tf_op jit(solution)/shard_map/ppermute | solution.py:67
  30.4 5.2 %collective-permute-start.5 = (bf16[16,2048]{1,0:T(8,128)(2,1)S(1)}, bf16[16,2048]{1,0:T(8,128)(2,1)S(1)}, u32[]{:S(2)}, u32[]{:S(2)}) collective-permute-start(bf16[16,2048]{1,0:T(8,128)(2,1)S(1)} %slice.52), channel_id=1, source_target_pairs={{0,8},{2,10},{4,12},{6,14},{8,0},{10,2},{12,4},{14,6},{1,9},{3,11}... | collective-permute-start | bytes 196616 | tf_op jit(solution)/shard_map/ppermute | solution.py:67

commit v7 on v5

--- a/solution.py
+++ b/solution.py
@@ -63,16 +63,16 @@
     return context.reshape(row_count, half_width).astype(jnp.bfloat16)
 
 
-def swap(x, n, masks):
-    pairs = [(2 * i + head, 2 * (i ^ masks[head]) + head) for i in range(n) for head in range(2)]
-    return lax.ppermute(x, ("seq", "head"), pairs)
-
-
-TARGETS = ((7, 3, 5, 1, 6, 2, 4, 0), (7, 3, 6, 2, 5, 1, 4, 0))
+def swap(x, n, mask):
+    return lax.ppermute(x, "seq", [(i, i ^ mask) for i in range(n)])
+
+
+TARGETS = (7, 3, 5, 1, 6, 2, 4, 0)
+MIDDLE = 4
 
 
 def keys_kernel(
-    pos_ref, head_ref, len_ref, null_ref, w_ref, code_ref, rows_ref, send_ref, keep_ref, sel_ref, count_ref
+    pos_ref, len_ref, null_ref, w_ref, code_ref, rows_ref, send_ref, keep_ref, sel_ref, count_ref
 ):
     features = null_ref.shape[1]
     rows = sel_ref.shape[0]
@@ -81,9 +81,8 @@
     text = rows_ref[:, :features]
     text = jnp.concatenate([text, jnp.zeros((rows - total, features), text.dtype)], axis=0)
     codes = []
-    for m, m_last in zip(*TARGETS):
-        peer = jnp.bitwise_xor(pos_ref[0], jnp.where(head_ref[0] == 0, m, m_last))
-        code = code_ref[peer][:, features:].astype(jnp.float32)
+    for m in TARGETS:
+        code = code_ref[jnp.bitwise_xor(pos_ref[0], m ^ MIDDLE)][:, features:].astype(jnp.float32)
         codes += [code] * (NULL_LEN // text_dev)
     code = jnp.concatenate(codes, axis=0)
     reqs = len_ref.shape[1]
@@ -97,7 +96,7 @@
     own = rows - NULL_LEN
     count_ref[...] = length[own : own + 8].astype(jnp.int32)
     row = lax.broadcasted_iota(jnp.int32, code.shape, 0) % NULL_LEN
-    col = lax.broadcasted_iota(jnp.int32, code.shape, 1)
+    col = jnp.bitwise_xor(lax.broadcasted_iota(jnp.int32, code.shape, 1), MIDDLE * text_dev)
     pick = col.astype(jnp.float32) == start + row.astype(jnp.float32)
     pick = pick.astype(jnp.float32).astype(jnp.bfloat16)
     text_sel = jnp.dot(pick, text, preferred_element_type=jnp.float32)
@@ -145,21 +144,21 @@
     return jnp.concatenate(blocks, axis=0)
 
 
-def probs_kernel(count_ref, q_ref, kept_ref, got_ref, out_ref, wide_ref):
+def probs_kernel(count_ref, q_ref, kept_ref, got_ref, out_ref, wide_ref, scores_ref):
     heads = q_ref.shape[1] // HDIM
     width = q_ref.shape[1]
     for c in range(0, width, 512):
         cols = slice(c, c + 512)
         wide_ref[:, cols] = spread_heads(kept_ref, got_ref, cols)
-    count = jnp.broadcast_to(jnp.concatenate([count_ref[:1]] * (out_ref.shape[1] // 128), axis=1), (256, out_ref.shape[1]))
-    block = 256
+    scores_ref[...] = lax.dot_general(
+        q_ref[...], wide_ref[...], (((1,), (1,)), ((), ())), preferred_element_type=jnp.float32
+    )
+    block = 128
+    lanes = out_ref.shape[1]
+    count = jnp.concatenate([count_ref[:1]] * (lanes // 128), axis=1)
+    count = jnp.broadcast_to(count, (block, lanes))
     for first in range(0, q_ref.shape[0], block):
-        scores = lax.dot_general(
-            q_ref[first : first + block],
-            wide_ref[...],
-            (((1,), (1,)), ((), ())),
-            preferred_element_type=jnp.float32,
-        )
+        scores = scores_ref[first : first + block]
         scores = scores * SCALE
         key = lax.broadcasted_iota(jnp.int32, scores.shape, 1) // heads
         scores = jnp.where(key < count, scores, NEG)
@@ -208,8 +207,12 @@
     text_dev = text_rows.shape[0]
     code = (block_owner[0] + reqs * uncond_flags[0]).astype(jnp.bfloat16)
     text = text_rows.reshape(text_dev, n, features).transpose(1, 0, 2)
+    text = jnp.concatenate([text[MIDDLE:], text[:MIDDLE]], axis=0)
     packed = jnp.concatenate([text, jnp.full((n, text_dev, 128), code, jnp.bfloat16)], axis=2)
-    held = lax.all_to_all(packed, "seq", split_axis=0, concat_axis=0, tiled=True)
+    group = [place ^ MIDDLE for place in range(n)]
+    held = lax.all_to_all(
+        packed, "seq", split_axis=0, concat_axis=0, axis_index_groups=[group], tiled=True
+    )
     null_cols = lax.dynamic_slice_in_dim(null_rows, pos * features, features, 1)
     weight = kv_weight.reshape(features, 2 * width)
     half = n * NULL_LEN // 2
@@ -228,14 +231,13 @@
             jax.ShapeDtypeStruct((2 * half, features), jnp.bfloat16),
             jax.ShapeDtypeStruct((8, 128), jnp.int32),
         ],
-        in_specs=[smem] * 2 + [vmem] * 5,
+        in_specs=[smem] + [vmem] * 5,
         out_specs=[vmem] * 4,
         compiler_params=params,
         cost_estimate=estimate,
         name="keys",
     )(
         pos.reshape(1),
-        lax.axis_index("head").astype(jnp.int32).reshape(1),
         prompt_lengths.reshape(1, reqs),
         null_cols,
         weight,
@@ -257,10 +259,10 @@
             total = keep + swap(send, n, mask).astype(jnp.float32)
             cut = total.shape[0] // 2
             send, keep = total[:cut].astype(jnp.bfloat16), total[cut:]
-        return keep, swap(send, n, (4, 4))
-
-    k_parts = reduce_parts(send_k, keep_k, ((1, 2), (2, 1)))
-    v_parts = reduce_parts(send_v, keep_v, ((2, 1), (1, 2)))
+        return keep, swap(send, n, 4)
+
+    k_parts = reduce_parts(send_k, keep_k, (1, 2))
+    v_parts = reduce_parts(send_v, keep_v, (2, 1))
 
     lanes = heads * NULL_LEN
     probs = pl.pallas_call(
@@ -268,7 +270,10 @@
         out_shape=jax.ShapeDtypeStruct((rows, lanes), jnp.bfloat16),
         in_specs=[vmem] * 4,
         out_specs=vmem,
-        scratch_shapes=[pltpu.VMEM((lanes, width), jnp.bfloat16)],
+        scratch_shapes=[
+            pltpu.VMEM((lanes, width), jnp.bfloat16),
+            pltpu.VMEM((rows, lanes), jnp.float32),
+        ],
         compiler_params=params,
         cost_estimate=pl.CostEstimate(
             flops=2 * rows * width * lanes, bytes_accessed=2 * rows * width, transcendentals=rows * lanes
@@ -297,7 +302,7 @@
 
     def per_device(queries, text_rows, null_rows, kv_weight, *rest):
         longest = n * text_rows.shape[0] // 4
-        few = n == 8 and mesh.shape["head"] == 2 and longest == NULL_LEN and text_rows.shape[0] == 8
+        few = n == 8 and longest == NULL_LEN and text_rows.shape[0] == 8
         if few:
             return select_plan(n, queries, text_rows, null_rows, kv_weight, *rest)
         return gather_plan(queries, text_rows, null_rows, kv_weight, *rest)

time: 41.1 us -> 37.2 us (0.905)
  waiting for transfers between devices: 17 us -> 12.2 us
  starting transfers between devices: 13.9 us -> 14.7 us
  other arithmetic: 0.14 us -> 0.77 us
  local copies, waits for them, and re-layouts: 3.96 us -> 3.35 us
    ppermute x6, waiting for transfers between devices: 12.7 us -> 10.3 us  [swap(): return lax.ppermute(x, 'seq', [(i, i ^ mask) for i in range(n)])]
    all_to_all x1, waiting for transfers between devices: 4.28 us -> 1.92 us  [select_plan(): lax.all_to_all(packed, 'seq', split_axis=0, concat_axis=0, axis_index_gro...]
    concatenate x1 -> x0, local copies, waits for them, and re-layouts: 1.38 us -> none  [select_plan(): jnp.concatenate([text, jnp.full((n, text_dev, 128), code, jnp.bfloat16)],...]
    slice x0 -> x1, local copies, waits for them, and re-layouts: none -> 0.77 us  [select_plan(): text = jnp.concatenate([text[MIDDLE:], text[:MIDDLE]], axis=0)]
    concatenate x0 -> x1, other arithmetic: none -> 0.63 us  [select_plan(): text = jnp.concatenate([text[MIDDLE:], text[:MIDDLE]], axis=0)]
    all_to_all x1, starting transfers between devices: 7.25 us -> 7.81 us  [select_plan(): lax.all_to_all(packed, 'seq', split_axis=0, concat_axis=0, axis_index_gro...]
  transfers between devices with their start and end apart: 7 -> 7, of which waited for: 6 -> 5; matrix products, arithmetic and copies ran while one was open for 7% -> 7% of each run, Pallas kernels for 4% -> 5%
where the time goes in v7:
time: 37.2 us; the launch traced here: 36.9 us
  starting transfers between devices  14.7 us (40%)
  waiting for transfers between devices  12.2 us (33%)
  Pallas kernels  4.43 us (12%)
  local copies, waits for them, and re-layouts  3.35 us (9%)
  between operations  1.43 us (4%)
  other arithmetic  0.77 us (2%)
    ppermute x6, waiting for transfers between devices, swap(): return lax.ppermute(x, 'seq', [(i, i ^ mask) for i in range(n)])  10.3 us
    all_to_all x1, starting transfers between devices, select_plan(): lax.all_to_all(packed, 'seq', split_axis=0, concat_axis=0, axis_index_gro...  7.81 us
    ppermute x6, starting transfers between devices, swap(): return lax.ppermute(x, 'seq', [(i, i ^ mask) for i in range(n)])  6.85 us
    unnamed x7, local copies, waits for them, and re-layouts  2.5 us
    pallas_call x1, Pallas kernels, select_plan(): pl.pallas_call(context_kernel, out_shape=jax.ShapeDtypeStruct((rows, widt...  2.07 us
    all_to_all x1, waiting for transfers between devices, select_plan(): lax.all_to_all(packed, 'seq', split_axis=0, concat_axis=0, axis_index_gro...  1.92 us
    pallas_call x1, Pallas kernels, select_plan(): pl.pallas_call(probs_kernel, out_shape=jax.ShapeDtypeStruct((rows, lanes)...  1.58 us
    slice x1, local copies, waits for them, and re-layouts, select_plan(): text = jnp.concatenate([text[MIDDLE:], text[:MIDDLE]], axis=0)  0.77 us
  transfers between devices with their start and end apart: 7, of which 5 were waited for; matrix products, arithmetic and copies ran while one was open for 7% of the time, Pallas kernels for 5%

profile of v7, /device:TPU:0, one launch (start us, length us, event | category | flops | bytes accessed | tf_op | source)
XLA Modules:
  0.0 36.9 jit_solution(4627977811032569917)
XLA Ops:
  0.0 0.0 copy-start
  0.0 0.0 copy-start.2
  0.0 0.8 %fusion.3 = (bf16[4,8,256]{2,1,0:T(8,128)(2,1)S(1)}, bf16[4,8,256]{2,1,0:T(8,128)(2,1)S(1)}) fusion(bf16[8,8,256]{2,1,0:T(8,128)(2,1)} %bitcast.14), kind=kLoop, calls=%fused_computation.13 | loop fusion | bytes 65536 | tf_op jit(solution)/shard_map/slice | solution.py:210
  2.1 0.6 %fusion.2 = bf16[8,8,384]{2,1,0:T(8,128)(2,1)} fusion(bf16[4,8,256]{2,1,0:T(8,128)(2,1)S(1)} %get-tuple-element.18, bf16[4,8,256]{2,1,0:T(8,128)(2,1)S(1)} %get-tuple-element.17, bf16[]{:T(256)} %bitcast.5), kind=kLoop, calls=%fused_computation.11 | loop fusion | flops 172032 | bytes 81922 | tf_op jit(solution)/shard_map/concatenate | solution.py:210
  2.7 7.8 %all-to-all-start = ((bf16[8,8,384]{2,1,0:T(8,128)(2,1)}), bf16[8,8,384]{2,1,0:T(8,128)(2,1)S(1)}, u32[]{:S(2)}, u32[]{:S(2)}) async-start(bf16[8,8,384]{2,1,0:T(8,128)(2,1)} %fusion.2), calls=%async_computation | async-start | bytes 98304 | tf_op jit(solution)/shard_map/all_to_all | solution.py:213
  10.5 2.5 %copy.8 = bf16[32,8,2,2048]{3,1,2,0:T(8,128)(2,1)S(1)} copy(bf16[32,8,2,2048]{3,2,1,0:T(2,128)(2,1)} %bitcast.13) | data formatting | bytes 4194304
  13.0 0.0 copy-done
  13.0 1.9 %all-to-all-done.code_ref = bf16[8,8,384]{2,1,0:T(8,128)(2,1)S(1)} async-done(((bf16[8,8,384]{2,1,0:T(8,128)(2,1)}), bf16[8,8,384]{2,1,0:T(8,128)(2,1)S(1)}, u32[]{:S(2)}, u32[]{:S(2)}) %all-to-all-start) | async-done | bytes 49184 | tf_op jit(solution)/shard_map/all_to_all | solution.py:213
  15.0 0.0 copy-done.2
  15.0 0.5 %keys.1 = (bf16[64,2048]{1,0:T(8,128)(2,1)S(1)}, f32[64,2048]{1,0:T(8,128)S(1)}, bf16[128,256]{1,0:T(8,128)(2,1)S(1)}, s32[8,128]{1,0:T(8,128)S(1)}) custom-call(s32[1]{0:T(128)} %bitcast.pos_ref, s32[1,8]{1,0:T(1,128)S(1)} %bitcast.12, bf16[16,256]{1,0:T(8,128)(2,1)S(1)} %constant_dynamic-slice_fusion.null_ref, bf16[256,4096]{1,0:T(8,128)(2,1)S(1)} %bitcast.9, ...), custom_call_target="tpu_custom_call" | custom-call | flops 134217728 | bytes 1048576 | tf_op jit(solution)/shard_map/keys/pallas_call | solution.py:226
  15.4 0.5 %collective-permute-start = (bf16[64,2048]{1,0:T(8,128)(2,1)S(1)}, bf16[64,2048]{1,0:T(8,128)(2,1)S(1)}, u32[]{:S(2)}, u32[]{:S(2)}) collective-permute-start(bf16[64,2048]{1,0:T(8,128)(2,1)S(1)} %get-tuple-element.13), channel_id=1, source_target_pairs={{0,2},{2,0},{4,6},{6,4},{8,10},{10,8},{12,14},{14,12},{1,3},{3,1},... | collective-permute-start | bytes 786440 | tf_op jit(solution)/shard_map/ppermute | solution.py:67
  15.9 0.3 values.1
  16.3 0.0 copy-start.1
  16.3 0.8 %collective-permute-start.3 = (bf16[64,2048]{1,0:T(8,128)(2,1)S(1)}, bf16[64,2048]{1,0:T(8,128)(2,1)S(1)}, u32[]{:S(2)}, u32[]{:S(2)}) collective-permute-start(bf16[64,2048]{1,0:T(8,128)(2,1)S(1)} %get-tuple-element.16), channel_id=1, source_target_pairs={{0,4},{2,6},{4,0},{6,2},{8,12},{10,14},{12,8},{14,10},{1,5},{3,7},... | collective-permute-start | bytes 786440 | tf_op jit(solution)/shard_map/ppermute | solution.py:67
  17.1 5.0 %collective-permute-done = bf16[64,2048]{1,0:T(8,128)(2,1)S(1)} collective-permute-done((bf16[64,2048]{1,0:T(8,128)(2,1)S(1)}, bf16[64,2048]{1,0:T(8,128)(2,1)S(1)}, u32[]{:S(2)}, u32[]{:S(2)}) %collective-permute-start) | collective-permute-done | bytes 262176 | tf_op jit(solution)/shard_map/ppermute | solution.py:67
  22.2 0.6 %collective-permute-start.1 = (bf16[32,2048]{1,0:T(8,128)(2,1)S(1)}, bf16[32,2048]{1,0:T(8,128)(2,1)S(1)}, u32[]{:S(2)}, u32[]{:S(2)}) collective-permute-start(bf16[32,2048]{1,0:T(8,128)(2,1)S(1)} %slice.61), channel_id=1, source_target_pairs={{0,4},{2,6},{4,0},{6,2},{8,12},{10,14},{12,8},{14,10},{1,5},{3,7},... | collective-permute-start | bytes 393224 | tf_op jit(solution)/shard_map/ppermute | solution.py:67
  22.8 0.6 %collective-permute-done.3 = bf16[64,2048]{1,0:T(8,128)(2,1)S(1)} collective-permute-done((bf16[64,2048]{1,0:T(8,128)(2,1)S(1)}, bf16[64,2048]{1,0:T(8,128)(2,1)S(1)}, u32[]{:S(2)}, u32[]{:S(2)}) %collective-permute-start.3) | collective-permute-done | bytes 262176 | tf_op jit(solution)/shard_map/ppermute | solution.py:67
  23.5 1.8 %collective-permute-start.4 = (bf16[32,2048]{1,0:T(8,128)(2,1)S(1)}, bf16[32,2048]{1,0:T(8,128)(2,1)S(1)}, u32[]{:S(2)}, u32[]{:S(2)}) collective-permute-start(bf16[32,2048]{1,0:T(8,128)(2,1)S(1)} %slice.60), channel_id=1, source_target_pairs={{0,2},{2,0},{4,6},{6,4},{8,10},{10,8},{12,14},{14,12},{1,3},{3,1},... | collective-permute-start | bytes 393224 | tf_op jit(solution)/shard_map/ppermute | solution.py:67
  25.4 1.9 %collective-permute-done.1 = bf16[32,2048]{1,0:T(8,128)(2,1)S(1)} collective-permute-done((bf16[32,2048]{1,0:T(8,128)(2,1)S(1)}, bf16[32,2048]{1,0:T(8,128)(2,1)S(1)}, u32[]{:S(2)}, u32[]{:S(2)}) %collective-permute-start.1) | collective-permute-done | bytes 131104 | tf_op jit(solution)/shard_map/ppermute | solution.py:67
  27.3 1.4 %collective-permute-start.2 = (bf16[16,2048]{1,0:T(8,128)(2,1)S(1)}, bf16[16,2048]{1,0:T(8,128)(2,1)S(1)}, u32[]{:S(2)}, u32[]{:S(2)}) collective-permute-start(bf16[16,2048]{1,0:T(8,128)(2,1)S(1)} %slice.63), channel_id=1, source_target_pairs={{0,8},{2,10},{4,12},{6,14},{8,0},{10,2},{12,4},{14,6},{1,9},{3,11}... | collective-permute-start | bytes 196616 | tf_op jit(solution)/shard_map/ppermute | solution.py:67
  28.7 0.0 collective-permute-done.4
  28.7 1.7 %collective-permute-start.5 = (bf16[16,2048]{1,0:T(8,128)(2,1)S(1)}, bf16[16,2048]{1,0:T(8,128)(2,1)S(1)}, u32[]{:S(2)}, u32[]{:S(2)}) collective-permute-start(bf16[16,2048]{1,0:T(8,128)(2,1)S(1)} %slice.62), channel_id=1, source_target_pairs={{0,8},{2,10},{4,12},{6,14},{8,0},{10,2},{12,4},{14,6},{1,9},{3,11}... | collective-permute-start | bytes 196616 | tf_op jit(solution)/shard_map/ppermute | solution.py:67
  30.4 2.8 %collective-permute-done.2.got_ref = bf16[16,2048]{1,0:T(8,128)(2,1)S(1)} collective-permute-done((bf16[16,2048]{1,0:T(8,128)(2,1)S(1)}, bf16[16,2048]{1,0:T(8,128)(2,1)S(1)}, u32[]{:S(2)}, u32[]{:S(2)}) %collective-permute-start.2) | collective-permute-done | bytes 65568 | tf_op jit(solution)/shard_map/ppermute | solution.py:67
  33.2 0.0 copy-done.1
  33.2 1.6 %probs.1.p_ref = bf16[768,256]{1,0:T(8,128)(2,1)S(1)} custom-call(s32[8,128]{1,0:T(8,128)S(1)} %get-tuple-element.11.count_ref, bf16[768,2048]{1,0:T(8,128)(2,1)S(1)} %copy-done.1, f32[16,2048]{1,0:T(8,128)S(1)} %slice.48.kept_ref, bf16[16,2048]{1,0:T(8,128)(2,1)S(1)} %collective-permute-done.2.got_ref), custom_call_target="tpu_custom_call" | custom-call | flops 805306368 | bytes 3145728 | tf_op jit(solution)/shard_map/probs/pallas_call | solution.py:268
  34.8 0.0 collective-permute-done.5.got_ref
  34.8 2.1 %context.1 = bf16[768,2048]{1,0:T(8,128)(2,1)} custom-call(bf16[768,256]{1,0:T(8,128)(2,1)S(1)} %probs.1.p_ref, f32[16,2048]{1,0:T(8,128)S(1)} %slice.52.kept_ref, bf16[16,2048]{1,0:T(8,128)(2,1)S(1)} %collective-permute-done.5.got_ref), custom_call_target="tpu_custom_call" | custom-call | flops 805306368 | bytes 3145728 | tf_op jit(solution)/shard_map/context/pallas_call | solution.py:283
  (11 shorter events, 0.2 us)
Async XLA Ops:
  0.0 13.0 %copy-start = (bf16[16,2048]{1,0:T(8,128)(2,1)S(1)}, bf16[16,2048]{1,0:T(8,128)(2,1)}, u32[]{:S(2)}) copy-start(bf16[16,2048]{1,0:T(8,128)(2,1)} %param.9) | copy-start | bytes 196612
  0.0 15.0 %copy-start.2 = (s32[8]{0:T(128)S(1)}, s32[8]{0:T(128)}, u32[]{:S(2)}) copy-start(s32[8]{0:T(128)} %param.11) | copy-start | bytes 100
  2.7 12.2 %all-to-all-start = ((bf16[8,8,384]{2,1,0:T(8,128)(2,1)}), bf16[8,8,384]{2,1,0:T(8,128)(2,1)S(1)}, u32[]{:S(2)}, u32[]{:S(2)}) async-start(bf16[8,8,384]{2,1,0:T(8,128)(2,1)} %fusion.2), calls=%async_computation | async-start | bytes 98304 | tf_op jit(solution)/shard_map/all_to_all | solution.py:213
  15.4 6.7 %collective-permute-start = (bf16[64,2048]{1,0:T(8,128)(2,1)S(1)}, bf16[64,2048]{1,0:T(8,128)(2,1)S(1)}, u32[]{:S(2)}, u32[]{:S(2)}) collective-permute-start(bf16[64,2048]{1,0:T(8,128)(2,1)S(1)} %get-tuple-element.13), channel_id=1, source_target_pairs={{0,2},{2,0},{4,6},{6,4},{8,10},{10,8},{12,14},{14,12},{1,3},{3,1},... | collective-permute-start | bytes 786440 | tf_op jit(solution)/shard_map/ppermute | solution.py:67
  16.3 17.0 %copy-start.1 = (bf16[768,2048]{1,0:T(8,128)(2,1)S(1)}, bf16[768,2048]{1,0:T(8,128)(2,1)}, u32[]{:S(2)}) copy-start(bf16[768,2048]{1,0:T(8,128)(2,1)} %q_ref.1) | copy-start | bytes 9437188
  16.3 7.2 %collective-permute-start.3 = (bf16[64,2048]{1,0:T(8,128)(2,1)S(1)}, bf16[64,2048]{1,0:T(8,128)(2,1)S(1)}, u32[]{:S(2)}, u32[]{:S(2)}) collective-permute-start(bf16[64,2048]{1,0:T(8,128)(2,1)S(1)} %get-tuple-element.16), channel_id=1, source_target_pairs={{0,4},{2,6},{4,0},{6,2},{8,12},{10,14},{12,8},{14,10},{1,5},{3,7},... | collective-permute-start | bytes 786440 | tf_op jit(solution)/shard_map/ppermute | solution.py:67
  22.2 5.0 %collective-permute-start.1 = (bf16[32,2048]{1,0:T(8,128)(2,1)S(1)}, bf16[32,2048]{1,0:T(8,128)(2,1)S(1)}, u32[]{:S(2)}, u32[]{:S(2)}) collective-permute-start(bf16[32,2048]{1,0:T(8,128)(2,1)S(1)} %slice.61), channel_id=1, source_target_pairs={{0,4},{2,6},{4,0},{6,2},{8,12},{10,14},{12,8},{14,10},{1,5},{3,7},... | collective-permute-start | bytes 393224 | tf_op jit(solution)/shard_map/ppermute | solution.py:67
  23.5 5.1 %collective-permute-start.4 = (bf16[32,2048]{1,0:T(8,128)(2,1)S(1)}, bf16[32,2048]{1,0:T(8,128)(2,1)S(1)}, u32[]{:S(2)}, u32[]{:S(2)}) collective-permute-start(bf16[32,2048]{1,0:T(8,128)(2,1)S(1)} %slice.60), channel_id=1, source_target_pairs={{0,2},{2,0},{4,6},{6,4},{8,10},{10,8},{12,14},{14,12},{1,3},{3,1},... | collective-permute-start | bytes 393224 | tf_op jit(solution)/shard_map/ppermute | solution.py:67
  27.3 5.9 %collective-permute-start.2 = (bf16[16,2048]{1,0:T(8,128)(2,1)S(1)}, bf16[16,2048]{1,0:T(8,128)(2,1)S(1)}, u32[]{:S(2)}, u32[]{:S(2)}) collective-permute-start(bf16[16,2048]{1,0:T(8,128)(2,1)S(1)} %slice.63), channel_id=1, source_target_pairs={{0,8},{2,10},{4,12},{6,14},{8,0},{10,2},{12,4},{14,6},{1,9},{3,11}... | collective-permute-start | bytes 196616 | tf_op jit(solution)/shard_map/ppermute | solution.py:67
  28.7 6.1 %collective-permute-start.5 = (bf16[16,2048]{1,0:T(8,128)(2,1)S(1)}, bf16[16,2048]{1,0:T(8,128)(2,1)S(1)}, u32[]{:S(2)}, u32[]{:S(2)}) collective-permute-start(bf16[16,2048]{1,0:T(8,128)(2,1)S(1)} %slice.62), channel_id=1, source_target_pairs={{0,8},{2,10},{4,12},{6,14},{8,0},{10,2},{12,4},{14,6},{1,9},{3,11}... | collective-permute-start | bytes 196616 | tf_op jit(solution)/shard_map/ppermute | solution.py:67
